TPU v7x, 128 devices: a whole 4x4x4 slice. The times are simulated.
128 devices in a mesh: dp: 16 (over y_hi, x, core), tensor: 8 (over y_lo, z).
Axes of the slice: x: 4, y: 4 (y_hi: 2, y_lo: 2; y = y_hi * 2 + y_lo), z: 4, core: 2. Of those that a mesh axis runs over, the one named last changes fastest.
Arguments:
- tokens: bfloat16 [16, 1024, 2048], P('dp', 'tensor'), may hold values from -6 to 6
- lengths: int32 [16], P('dp'), may hold values from 897 to 1024, as said below
- w_query: bfloat16 [2048, 2048], P('dp', 'tensor'), may hold values from -0.125 to 0.125
- w_key: bfloat16 [2048, 2048], P('dp', 'tensor'), may hold values from -0.125 to 0.125
- w_value: bfloat16 [2048, 2048], P('dp', 'tensor'), may hold values from -0.125 to 0.125
- w_out: bfloat16 [2048, 2048], P('tensor', 'dp'), may hold values from -0.125 to 0.125
- w_gate: bfloat16 [2048, 8192], P('dp', 'tensor'), may hold values from -0.125 to 0.125
- w_up: bfloat16 [2048, 8192], P('dp', 'tensor'), may hold values from -0.125 to 0.125
- w_down: bfloat16 [8192, 2048], P('tensor', 'dp'), may hold values from -0.0625 to 0.0625
- q_gain: float32 [2048], replicated, may hold values from 0.25 to 1.75
- k_gain: float32 [2048], replicated, may hold values from 0.25 to 1.75
- attn_gain: float32 [2048], replicated, may hold values from 0.25 to 1.75
- mlp_gain: float32 [2048], replicated, may hold values from 0.25 to 1.75
- cotangent: bfloat16 [16, 1024, 2048], P('dp', 'tensor'), may hold values from -6 to 6
Outputs:
- activations: bfloat16 [16, 1024, 2048], P('dp', 'tensor')
- input_grad: float32 [16, 1024, 2048], P('dp', 'tensor')
- w_query_grad: float32 [2048, 2048], P('dp', 'tensor')
- w_key_grad: float32 [2048, 2048], P('dp', 'tensor')
- w_value_grad: float32 [2048, 2048], P('dp', 'tensor')
- w_out_grad: float32 [2048, 2048], P('tensor', 'dp')
- w_gate_grad: float32 [2048, 8192], P('dp', 'tensor')
- w_up_grad: float32 [2048, 8192], P('dp', 'tensor')
- w_down_grad: float32 [8192, 2048], P('tensor', 'dp')
- q_gain_grad: float32 [2048], replicated
- k_gain_grad: float32 [2048], replicated
- attn_gain_grad: float32 [2048], replicated
- mlp_gain_grad: float32 [2048], replicated
Inputs may be any that keep to these rules, and one draw needn't show every extreme that they name: `lengths`: one sequence of the batch, drawn from the seed, has length 1024; every other sequence is shorter.
All inputs are finite; a program needn't handle non-finite values.
Results may differ from a plain program's by a relative error of at most 0.024.
Values may be sent and summed in bfloat16 or wider, within the bound.
A program may use at most 192 MiB of HBM per device.

v0:
```python
import jax
import jax.numpy as jnp
from jax import lax
from jax.sharding import PartitionSpec as P

HEAD_DIM = 128


EPS = 1e-06
THETA = 500000.0


def rope_tables(count, size):
    half_size = size // 2
    frequency = THETA ** (-(jnp.arange(half_size, dtype=jnp.float32) * 2.0 / size))
    angles = jnp.arange(count, dtype=jnp.float32)[:, None] * frequency[None, :]
    return (jnp.cos(angles), jnp.sin(angles))


def rotate(values, cosine, sine_table, direction):
    half_size = values.shape[-1] // 2
    first_half = values[..., :half_size]
    second_half = values[..., half_size:]
    cos_b = cosine[:, None, :]
    sin_b = direction * sine_table[:, None, :]
    return jnp.concatenate(
        [first_half * cos_b - second_half * sin_b, second_half * cos_b + first_half * sin_b], -1
    )


def dot_last(left, right):
    return lax.dot_general(
        left, right, (((1,), (1,)), ((), ())), preferred_element_type=jnp.float32
    )


def dot_first(left, right):
    return lax.dot_general(
        left, right, (((0,), (0,)), ((), ())), preferred_element_type=jnp.float32
    )


def rms_scale(values):
    return lax.rsqrt(jnp.mean(values * values, -1, keepdims=True) + EPS)


def norm_back(values, scale_rows, gain, grad_rows):
    weighted = gain * grad_rows
    mean_term = jnp.mean(values * weighted, -1, keepdims=True)
    return scale_rows * weighted - values * scale_rows**3 * mean_term


def masked_scores(rotated_queries, rotated_keys, length):
    unscaled_scores = jnp.einsum(
        "euk,zuk->uez", rotated_queries, rotated_keys, preferred_element_type=jnp.float32
    )
    count = rotated_queries.shape[0]
    row_pos = lax.broadcasted_iota(jnp.int32, (count, count), 0)
    col_pos = lax.broadcasted_iota(jnp.int32, (count, count), 1)
    allowed = (col_pos <= row_pos) & (col_pos < length)
    return jnp.where(allowed[None], unscaled_scores, -1e30)


def attend(operands):
    rotated_queries, rotated_keys, value_lower_precision, length = operands
    score_matrix = masked_scores(rotated_queries, rotated_keys, length)
    row_peak = jnp.max(score_matrix, -1, keepdims=True)
    exp_terms = jnp.exp(score_matrix - row_peak)
    row_total = jnp.sum(exp_terms, -1, keepdims=True)
    attention_probability = exp_terms / row_total
    lse_rows = row_peak[..., 0] + jnp.log(row_total[..., 0])
    mixed_heads = jnp.einsum(
        "gqk,kgf->qgf",
        attention_probability.astype(jnp.bfloat16),
        value_lower_precision,
        preferred_element_type=jnp.float32,
    )
    return (mixed_heads.astype(jnp.bfloat16), lse_rows)


def attend_back(operands):
    rotated_queries, rotated_keys, value_lower_precision, mixed_value_gradient, lse_rows, length = (
        operands
    )
    score_matrix = masked_scores(rotated_queries, rotated_keys, length)
    attention_probability = jnp.exp(score_matrix - lse_rows[..., None])
    probability_gradient = jnp.einsum(
        "euk,zuk->uez",
        mixed_value_gradient,
        value_lower_precision,
        preferred_element_type=jnp.float32,
    )
    delta_rows = jnp.sum(attention_probability * probability_gradient, -1, keepdims=True)
    score_gradient = (attention_probability * (probability_gradient - delta_rows)).astype(
        jnp.bfloat16
    )
    rotated_query_gradient = jnp.einsum(
        "gqk,kgf->qgf", score_gradient, rotated_keys, preferred_element_type=jnp.float32
    )
    rotated_key_gradient = jnp.einsum(
        "jkt,kji->tji", score_gradient, rotated_queries, preferred_element_type=jnp.float32
    )
    d_vlow = jnp.einsum(
        "jkt,kji->tji",
        attention_probability.astype(jnp.bfloat16),
        mixed_value_gradient,
        preferred_element_type=jnp.float32,
    )
    return (rotated_query_gradient, rotated_key_gradient, d_vlow.astype(jnp.bfloat16))


def local(
    tokens,
    lengths,
    w_query,
    w_key,
    w_value,
    w_out,
    w_gate,
    w_up,
    w_down,
    q_gain,
    k_gain,
    attn_gain,
    mlp_gain,
    cotangent,
):
    sequences, part_len, width = tokens.shape
    tp_count = lax.axis_size("tensor")
    tp_index = lax.axis_index("tensor")
    full_len = part_len * tp_count
    columns = w_query.shape[1]
    heads_dev = columns // HEAD_DIM
    gathered = (
        lax.all_gather(w_query, "dp", axis=0, tiled=True),
        lax.all_gather(w_key, "dp", axis=0, tiled=True),
        lax.all_gather(w_value, "dp", axis=0, tiled=True),
        lax.all_gather(w_out, "dp", axis=1, tiled=True),
        lax.all_gather(w_gate, "dp", axis=0, tiled=True),
        lax.all_gather(w_up, "dp", axis=0, tiled=True),
        lax.all_gather(w_down, "dp", axis=1, tiled=True),
    )
    wq_full, wk_full, wv_full, wo_full, wg_full, wu_full, wd_full = gathered
    q_gain_dev = lax.dynamic_slice_in_dim(q_gain, tp_index * columns, columns)
    k_gain_dev = lax.dynamic_slice_in_dim(k_gain, tp_index * columns, columns)
    positions = tp_index * part_len + lax.broadcasted_iota(jnp.int32, (sequences, part_len), 1)
    valid_rows = (positions < lengths[:, None])[..., None]
    whole_rows = lax.all_gather(tokens, "tensor", axis=1, tiled=True).reshape(
        sequences * full_len, width
    )
    q_raw = jnp.dot(whole_rows, wq_full, preferred_element_type=jnp.float32)
    k_raw = jnp.dot(whole_rows, wk_full, preferred_element_type=jnp.float32)
    v_raw = jnp.dot(whole_rows, wv_full, preferred_element_type=jnp.float32)
    q_sums, k_sums = lax.psum((jnp.sum(q_raw * q_raw, -1), jnp.sum(k_raw * k_raw, -1)), "tensor")
    q_scale = lax.rsqrt(q_sums / width + EPS)[:, None]
    k_scale = lax.rsqrt(k_sums / width + EPS)[:, None]
    q_norm = q_raw * q_scale * q_gain_dev
    k_norm = k_raw * k_scale * k_gain_dev
    cosine, sine_table = rope_tables(full_len, HEAD_DIM)
    head_shape = (sequences, full_len, heads_dev, HEAD_DIM)
    score_scale = HEAD_DIM ** (-0.5)
    rotated_queries = (
        rotate(q_norm.reshape(head_shape), cosine, sine_table, 1.0) * score_scale
    ).astype(jnp.bfloat16)
    rotated_keys = rotate(k_norm.reshape(head_shape), cosine, sine_table, 1.0).astype(jnp.bfloat16)
    value_lower_precision = v_raw.astype(jnp.bfloat16).reshape(head_shape)
    mixed_heads, lse_all = lax.map(
        attend, (rotated_queries, rotated_keys, value_lower_precision, lengths)
    )
    mixed_flat = mixed_heads.reshape(sequences * full_len, columns)
    branch_part = jnp.dot(mixed_flat, wo_full, preferred_element_type=jnp.float32).reshape(
        sequences, full_len, width
    )
    branch = lax.psum_scatter(branch_part, "tensor", scatter_dimension=1, tiled=True)
    b_scale = rms_scale(branch)
    residual = tokens.astype(jnp.float32) + branch * b_scale * attn_gain
    res_low = residual.astype(jnp.bfloat16)
    res_whole = lax.all_gather(res_low, "tensor", axis=1, tiled=True).reshape(
        sequences * full_len, width
    )
    gate_value = jnp.dot(res_whole, wg_full, preferred_element_type=jnp.float32)
    up_value = jnp.dot(res_whole, wu_full, preferred_element_type=jnp.float32)
    sigmoid_gate = jax.nn.sigmoid(gate_value)
    silu_gate = gate_value * sigmoid_gate
    inner_act = (silu_gate * up_value).astype(jnp.bfloat16)
    down_part = jnp.dot(inner_act, wd_full, preferred_element_type=jnp.float32).reshape(
        sequences, full_len, width
    )
    down_value = lax.psum_scatter(
        down_part.astype(jnp.bfloat16), "tensor", scatter_dimension=1, tiled=True
    ).astype(jnp.float32)
    d_scale = rms_scale(down_value)
    activations = jnp.where(valid_rows, residual + down_value * d_scale * mlp_gain, 0.0).astype(
        jnp.bfloat16
    )
    back_weights = (
        lax.all_gather(w_query, "dp", axis=0, tiled=True),
        lax.all_gather(w_key, "dp", axis=0, tiled=True),
        lax.all_gather(w_value, "dp", axis=0, tiled=True),
        lax.all_gather(w_out, "dp", axis=1, tiled=True),
        lax.all_gather(w_gate, "dp", axis=0, tiled=True),
        lax.all_gather(w_up, "dp", axis=0, tiled=True),
        lax.all_gather(w_down, "dp", axis=1, tiled=True),
    )
    wq_back, wk_back, wv_back, wo_back, wg_back, wu_back, wd_back = back_weights
    grad_out = jnp.where(valid_rows, cotangent.astype(jnp.float32), 0.0)
    mlp_gain_part = jnp.sum(grad_out * down_value * d_scale, (0, 1))
    d_down = norm_back(down_value, d_scale, mlp_gain, grad_out).astype(jnp.bfloat16)
    d_down_whole = lax.all_gather(d_down, "tensor", axis=1, tiled=True).reshape(
        sequences * full_len, width
    )
    d_inner = dot_last(d_down_whole, wd_back)
    w_down_part = dot_first(inner_act, d_down_whole)
    d_gate = (d_inner * up_value * sigmoid_gate * (1.0 + gate_value * (1.0 - sigmoid_gate))).astype(
        jnp.bfloat16
    )
    d_up = (d_inner * silu_gate).astype(jnp.bfloat16)
    w_gate_part = dot_first(res_whole, d_gate)
    w_up_part = dot_first(res_whole, d_up)
    d_res_part = (dot_last(d_gate, wg_back) + dot_last(d_up, wu_back)).reshape(
        sequences, full_len, width
    )
    d_res = grad_out + lax.psum_scatter(
        d_res_part.astype(jnp.bfloat16), "tensor", scatter_dimension=1, tiled=True
    ).astype(jnp.float32)
    attn_gain_part = jnp.sum(d_res * branch * b_scale, (0, 1))
    d_branch = norm_back(branch, b_scale, attn_gain, d_res).astype(jnp.bfloat16)
    d_branch_whole = lax.all_gather(d_branch, "tensor", axis=1, tiled=True).reshape(
        sequences * full_len, width
    )
    w_out_part = dot_first(mixed_flat, d_branch_whole)
    mixed_value_gradient = (
        dot_last(d_branch_whole, wo_back).astype(jnp.bfloat16).reshape(head_shape)
    )
    rotated_query_gradient, rotated_key_gradient, d_vlow = lax.map(
        attend_back,
        (
            rotated_queries,
            rotated_keys,
            value_lower_precision,
            mixed_value_gradient,
            lse_all,
            lengths,
        ),
    )
    d_qnorm = rotate(rotated_query_gradient * score_scale, cosine, sine_table, -1.0).reshape(
        sequences * full_len, columns
    )
    d_knorm = rotate(rotated_key_gradient, cosine, sine_table, -1.0).reshape(
        sequences * full_len, columns
    )
    q_weighted = d_qnorm * q_gain_dev
    k_weighted = d_knorm * k_gain_dev
    q_inner, k_inner = lax.psum(
        (jnp.sum(q_raw * q_weighted, -1), jnp.sum(k_raw * k_weighted, -1)), "tensor"
    )
    d_qraw = (q_scale * q_weighted - q_raw * q_scale**3 * (q_inner / width)[:, None]).astype(
        jnp.bfloat16
    )
    d_kraw = (k_scale * k_weighted - k_raw * k_scale**3 * (k_inner / width)[:, None]).astype(
        jnp.bfloat16
    )
    d_vflat = d_vlow.reshape(sequences * full_len, columns)
    q_gain_part = jnp.sum(d_qnorm * q_raw * q_scale, 0)
    k_gain_part = jnp.sum(d_knorm * k_raw * k_scale, 0)
    w_query_part = dot_first(whole_rows, d_qraw)
    w_key_part = dot_first(whole_rows, d_kraw)
    w_value_part = dot_first(whole_rows, d_vflat)
    d_input_part = (
        dot_last(d_qraw, wq_back) + dot_last(d_kraw, wk_back) + dot_last(d_vflat, wv_back)
    ).reshape(sequences, full_len, width)
    input_grad = d_res + lax.psum_scatter(
        d_input_part.astype(jnp.bfloat16), "tensor", scatter_dimension=1, tiled=True
    ).astype(jnp.float32)
    grads_owned = (
        lax.psum_scatter(
            w_query_part.astype(jnp.bfloat16), "dp", scatter_dimension=0, tiled=True
        ).astype(jnp.float32),
        lax.psum_scatter(
            w_key_part.astype(jnp.bfloat16), "dp", scatter_dimension=0, tiled=True
        ).astype(jnp.float32),
        lax.psum_scatter(
            w_value_part.astype(jnp.bfloat16), "dp", scatter_dimension=0, tiled=True
        ).astype(jnp.float32),
        lax.psum_scatter(
            w_out_part.astype(jnp.bfloat16), "dp", scatter_dimension=1, tiled=True
        ).astype(jnp.float32),
        lax.psum_scatter(
            w_gate_part.astype(jnp.bfloat16), "dp", scatter_dimension=0, tiled=True
        ).astype(jnp.float32),
        lax.psum_scatter(
            w_up_part.astype(jnp.bfloat16), "dp", scatter_dimension=0, tiled=True
        ).astype(jnp.float32),
        lax.psum_scatter(
            w_down_part.astype(jnp.bfloat16), "dp", scatter_dimension=1, tiled=True
        ).astype(jnp.float32),
    )
    empty_gain = jnp.zeros((width,), jnp.float32)
    q_gain_full = lax.dynamic_update_slice_in_dim(empty_gain, q_gain_part, tp_index * columns, 0)
    k_gain_full = lax.dynamic_update_slice_in_dim(empty_gain, k_gain_part, tp_index * columns, 0)
    gain_totals = lax.psum(
        (q_gain_full, k_gain_full, attn_gain_part, mlp_gain_part), ("dp", "tensor")
    )
    return (
        activations,
        input_grad,
        grads_owned[0],
        grads_owned[1],
        grads_owned[2],
        grads_owned[3],
        grads_owned[4],
        grads_owned[5],
        grads_owned[6],
        gain_totals[0],
        gain_totals[1],
        gain_totals[2],
        gain_totals[3],
    )


def solution(mesh):
    return jax.shard_map(
        local,
        mesh=mesh,
        in_specs=(
            P("dp", "tensor", None),
            P("dp"),
            P("dp", "tensor"),
            P("dp", "tensor"),
            P("dp", "tensor"),
            P("tensor", "dp"),
            P("dp", "tensor"),
            P("dp", "tensor"),
            P("tensor", "dp"),
            P(),
            P(),
            P(),
            P(),
            P("dp", "tensor", None),
        ),
        out_specs=(
            P("dp", "tensor", None),
            P("dp", "tensor", None),
            P("dp", "tensor"),
            P("dp", "tensor"),
            P("dp", "tensor"),
            P("tensor", "dp"),
            P("dp", "tensor"),
            P("dp", "tensor"),
            P("tensor", "dp"),
            P(),
            P(),
            P(),
            P(),
        ),
        check_vma=False,
    )
```

profile of v0, /device:TPU:0, one launch (start us, length us, event | category | flops | bytes accessed | tf_op | source)
XLA Modules:
  0.0 1421.4 jit_solution(17353708088207074598)
XLA Ops:
  16.0 41.9 %all-gather.16.cloned.1.call-done = bf16[2048,256]{1,0:T(8,128)(2,1)} async-done(((bf16[128,256]{1,0:T(8,128)(2,1)}), bf16[2048,256]{1,0:T(8,128)(2,1)}) %all-gather.16.cloned.1.call-update) | async-done | bytes 1048592 | tf_op jit(solution)/shard_map/all_gather | solution.py:135
  57.9 53.3 %all-gather.12.cloned.1.call-done = bf16[1,1024,2048]{2,1,0:T(8,128)(2,1)} async-done(((bf16[1,128,2048]{2,1,0:T(8,128)(2,1)}), bf16[1,1024,2048]{2,1,0:T(8,128)(2,1)}) %all-gather.12.cloned.1.call-update) | async-done | bytes 4194320 | tf_op jit(solution)/shard_map/all_gather | solution.py:148
  115.0 42.3 %all-gather.18.cloned.1.call-done = bf16[2048,256]{1,0:T(8,128)(2,1)} async-done(((bf16[128,256]{1,0:T(8,128)(2,1)}), bf16[2048,256]{1,0:T(8,128)(2,1)}) %all-gather.18.cloned.1.call-update) | async-done | bytes 1048592 | tf_op jit(solution)/shard_map/all_gather | solution.py:136
  162.1 19.3 %all-reduce.2 = (f32[1024]{0:T(1024)S(1)}, f32[1024]{0:T(1024)S(1)}) all-reduce(f32[1024]{0:T(1024)S(1)} %get-tuple-element.137, f32[1024]{0:T(1024)S(1)} %get-tuple-element.139), channel_id=1, replica_groups=mesh['dp'=16,'tensor'=8] {'tensor'}, use_global_device_ids=true, to_apply=%region_1.0 | all-reduce | flops 2048 | bytes 16384 | tf_op jit(solution)/shard_map/psum | solution.py:154
  212.9 36.8 %all-gather.20.cloned.1.call-done = bf16[256,2048]{1,0:T(8,128)(2,1)} async-done(((bf16[256,128]{1,0:T(8,128)(2,1)}), bf16[256,2048]{1,0:T(8,128)(2,1)}) %all-gather.20.cloned.1.call-update) | async-done | bytes 1048592 | tf_op jit(solution)/shard_map/all_gather | solution.py:138
  256.3 91.1 %reduce-scatter.22.cloned.1.call-done = f32[1,128,2048]{2,1,0:T(8,128)} async-done(((f32[1,1024,2048]{2,1,0:T(8,128)}), f32[1,128,2048]{2,1,0:T(8,128)}) %reduce-scatter.22.cloned.1.call-update) | async-done | bytes 1048592 | tf_op jit(solution)/shard_map/reduce_scatter | solution.py:174
  352.6 51.9 %all-gather.24.cloned.1.call-done = bf16[2048,1024]{1,0:T(8,128)(2,1)} async-done(((bf16[128,1024]{1,0:T(8,128)(2,1)}), bf16[2048,1024]{1,0:T(8,128)(2,1)}) %all-gather.24.cloned.1.call-update) | async-done | bytes 4194320 | tf_op jit(solution)/shard_map/all_gather | solution.py:139
  404.5 53.9 %all-gather.22.cloned.1.call-done = bf16[1,1024,2048]{2,1,0:T(8,128)(2,1)} async-done(((bf16[1,128,2048]{2,1,0:T(8,128)(2,1)}), bf16[1,1024,2048]{2,1,0:T(8,128)(2,1)}) %all-gather.22.cloned.1.call-update) | async-done | bytes 4194320 | tf_op jit(solution)/shard_map/all_gather | solution.py:178
  468.4 47.1 %all-gather.26.cloned.1.call-done = bf16[2048,1024]{1,0:T(8,128)(2,1)} async-done(((bf16[128,1024]{1,0:T(8,128)(2,1)}), bf16[2048,1024]{1,0:T(8,128)(2,1)}) %all-gather.26.cloned.1.call-update) | async-done | bytes 4194320 | tf_op jit(solution)/shard_map/all_gather | solution.py:140
  515.5 12.1 multiply_convert_fusion.3
  527.6 47.9 %all-gather.28.cloned.1.call-done = bf16[1024,2048]{1,0:T(8,128)(2,1)} async-done(((bf16[1024,128]{1,0:T(8,128)(2,1)}), bf16[1024,2048]{1,0:T(8,128)(2,1)}) %all-gather.28.cloned.1.call-update) | async-done | bytes 4194320 | tf_op jit(solution)/shard_map/all_gather | solution.py:141
  585.0 52.1 %reduce-scatter.24.cloned.1.call-done = bf16[1,128,2048]{2,1,0:T(8,128)(2,1)} async-done(((bf16[1,1024,2048]{2,1,0:T(8,128)(2,1)}), bf16[1,128,2048]{2,1,0:T(8,128)(2,1)}) %reduce-scatter.24.cloned.1.call-update) | async-done | bytes 524304 | tf_op jit(solution)/shard_map/reduce_scatter | solution.py:189
  642.5 51.2 %all-gather.30.cloned.1.call-done = bf16[1,1024,2048]{2,1,0:T(8,128)(2,1)} async-done(((bf16[1,128,2048]{2,1,0:T(8,128)(2,1)}), bf16[1,1024,2048]{2,1,0:T(8,128)(2,1)}) %all-gather.30.cloned.1.call-update) | async-done | bytes 4194320 | tf_op jit(solution)/shard_map/all_gather | solution.py:209
  693.7 13.0 multiply_convert_fusion.1
  719.2 52.0 %reduce-scatter.26.cloned.1.call-done = bf16[1,128,2048]{2,1,0:T(8,128)(2,1)} async-done(((bf16[1,1024,2048]{2,1,0:T(8,128)(2,1)}), bf16[1,128,2048]{2,1,0:T(8,128)(2,1)}) %reduce-scatter.26.cloned.1.call-update) | async-done | bytes 524304 | tf_op jit(solution)/shard_map/reduce_scatter | solution.py:223
  811.3 16.1 %all-gather.32.cloned.1.call-done = bf16[1,1024,2048]{2,1,0:T(8,128)(2,1)} async-done(((bf16[1,128,2048]{2,1,0:T(8,128)(2,1)}), bf16[1,1024,2048]{2,1,0:T(8,128)(2,1)}) %all-gather.32.cloned.1.call-update) | async-done | bytes 4194320 | tf_op jit(solution)/shard_map/all_gather | solution.py:228
  856.1 17.9 %all-reduce.1 = (f32[1024]{0:T(1024)S(1)}, f32[1024]{0:T(1024)S(1)}) all-reduce(f32[1024]{0:T(1024)S(1)} %get-tuple-element.95, f32[1024]{0:T(1024)S(1)} %get-tuple-element.93), channel_id=1, replica_groups=mesh['dp'=16,'tensor'=8] {'tensor'}, use_global_device_ids=true, to_apply=%region_15.16 | all-reduce | flops 2048 | bytes 16384 | tf_op jit(solution)/shard_map/psum | solution.py:254
  915.8 78.3 %reduce-scatter.30.cloned.1.call-done = bf16[128,1024]{1,0:T(8,128)(2,1)} async-done(((bf16[2048,1024]{1,0:T(8,128)(2,1)}), bf16[128,1024]{1,0:T(8,128)(2,1)}) %reduce-scatter.30.cloned.1.call-update) | async-done | bytes 262160 | tf_op jit(solution)/shard_map/reduce_scatter | solution.py:288
  995.9 81.4 %reduce-scatter.32.cloned.1.call-done = bf16[128,1024]{1,0:T(8,128)(2,1)} async-done(((bf16[2048,1024]{1,0:T(8,128)(2,1)}), bf16[128,1024]{1,0:T(8,128)(2,1)}) %reduce-scatter.32.cloned.1.call-update) | async-done | bytes 262160 | tf_op jit(solution)/shard_map/reduce_scatter | solution.py:291
  1079.5 65.7 %all-reduce = (f32[2048]{0:T(1024)}, f32[2048]{0:T(1024)}, f32[2048]{0:T(1024)}, f32[2048]{0:T(1024)}) all-reduce(f32[2048]{0:T(1024)S(1)} %dynamic_update_slice.19, f32[2048]{0:T(1024)S(1)} %dynamic_update_slice.20, f32[2048]{0:T(1024)S(1)} %get-tuple-element.90, ...), channel_id=1, replica_groups=mesh['dp'=16,'tensor'=8] {'dp','tensor'}, use_global_device_ids=true, to_apply=%region_27.28 | all-reduce | flops 8192 | bytes 65536 | tf_op jit(solution)/shard_map/psum | solution.py:301
  1148.8 68.0 %reduce-scatter.40.cloned.1.call-done = bf16[128,256]{1,0:T(8,128)(2,1)} async-done(((bf16[2048,256]{1,0:T(8,128)(2,1)}), bf16[128,256]{1,0:T(8,128)(2,1)}) %reduce-scatter.40.cloned.1.call-update) | async-done | bytes 65552
  1218.4 69.0 %reduce-scatter.34.cloned.1.call-done = bf16[128,256]{1,0:T(8,128)(2,1)} async-done(((bf16[2048,256]{1,0:T(8,128)(2,1)}), bf16[128,256]{1,0:T(8,128)(2,1)}) %reduce-scatter.34.cloned.1.call-update) | async-done | bytes 65552
  1289.1 68.0 %reduce-scatter.38.cloned.1.call-done = bf16[128,256]{1,0:T(8,128)(2,1)} async-done(((bf16[2048,256]{1,0:T(8,128)(2,1)}), bf16[128,256]{1,0:T(8,128)(2,1)}) %reduce-scatter.38.cloned.1.call-update) | async-done | bytes 65552
  1358.8 53.2 %reduce-scatter.28.cloned.1.call-done = bf16[1,128,2048]{2,1,0:T(8,128)(2,1)} async-done(((bf16[1,1024,2048]{2,1,0:T(8,128)(2,1)}), bf16[1,128,2048]{2,1,0:T(8,128)(2,1)}) %reduce-scatter.28.cloned.1.call-update) | async-done | bytes 524304 | tf_op jit(solution)/shard_map/reduce_scatter | solution.py:272
  (232 shorter events, 222.2 us)
Async XLA Ops:
  7.2 50.7 %all-gather.16.cloned.1.call-start = ((), (), s32[]{:S(2)}) async-start(), calls=%async_computation.13 | async-start | bytes 1114112 | tf_op jit(solution)/shard_map/all_gather | solution.py:135
  7.9 103.3 %all-gather.12.cloned.1.call-start = ((), (), s32[]{:S(2)}) async-start(), calls=%async_computation.11 | async-start | bytes 4718592 | tf_op jit(solution)/shard_map/all_gather | solution.py:148
  8.7 148.6 %all-gather.18.cloned.1.call-start = ((), (), s32[]{:S(2)}) async-start(), calls=%async_computation.14 | async-start | bytes 1114112 | tf_op jit(solution)/shard_map/all_gather | solution.py:136
  9.4 194.0 %all-gather.14.cloned.1.call-start = ((), (), s32[]{:S(2)}) async-start(), calls=%async_computation.12 | async-start | bytes 1114112 | tf_op jit(solution)/shard_map/all_gather | solution.py:137
  10.0 239.7 %all-gather.20.cloned.1.call-start = ((), (), s32[]{:S(2)}) async-start(), calls=%async_computation.15 | async-start | bytes 1114112 | tf_op jit(solution)/shard_map/all_gather | solution.py:138
  10.6 336.8 %reduce-scatter.22.cloned.1.call-start = ((), (), s32[]{:S(2)}) async-start(), calls=%async_computation.16 | async-start | bytes 9437184 | tf_op jit(solution)/shard_map/reduce_scatter | solution.py:174
  15.0 177.0 %copy-start.10 = (f32[1024,64]{1,0:T(8,128)}, f32[1024,64]{1,0:T(8,128)S(1)}, u32[]{:S(2)}) copy-start(f32[1024,64]{1,0:T(8,128)S(1)} %get-tuple-element.132) | copy-start | bytes 786436
  255.5 149.0 %all-gather.24.cloned.1.call-start = ((), (), s32[]{:S(2)}) async-start(), calls=%async_computation.18 | async-start | bytes 4456448 | tf_op jit(solution)/shard_map/all_gather | solution.py:139
  256.2 202.1 %all-gather.22.cloned.1.call-start = ((), (), s32[]{:S(2)}) async-start(), calls=%async_computation.17 | async-start | bytes 4718592 | tf_op jit(solution)/shard_map/all_gather | solution.py:178
  351.0 164.4 %all-gather.26.cloned.1.call-start = ((), (), s32[]{:S(2)}) async-start(), calls=%async_computation.19 | async-start | bytes 4456448 | tf_op jit(solution)/shard_map/all_gather | solution.py:140
  351.8 223.7 %all-gather.28.cloned.1.call-start = ((), (), s32[]{:S(2)}) async-start(), calls=%async_computation.20 | async-start | bytes 4456448 | tf_op jit(solution)/shard_map/all_gather | solution.py:141
  352.4 284.6 %reduce-scatter.24.cloned.1.call-start = ((), (), s32[]{:S(2)}) async-start(), calls=%async_computation.21 | async-start | bytes 4718592 | tf_op jit(solution)/shard_map/reduce_scatter | solution.py:189
  584.9 108.8 %all-gather.30.cloned.1.call-start = ((), (), s32[]{:S(2)}) async-start(), calls=%async_computation.22 | async-start | bytes 4718592 | tf_op jit(solution)/shard_map/all_gather | solution.py:209
  642.0 129.2 %reduce-scatter.26.cloned.1.call-start = ((), (), s32[]{:S(2)}) async-start(), calls=%async_computation.23 | async-start | bytes 4718592 | tf_op jit(solution)/shard_map/reduce_scatter | solution.py:223
  719.2 108.2 %all-gather.32.cloned.1.call-start = ((), (), s32[]{:S(2)}) async-start(), calls=%async_computation.24 | async-start | bytes 4718592 | tf_op jit(solution)/shard_map/all_gather | solution.py:228
  775.7 138.1 %reduce-scatter.42.cloned.1.call-start = ((), (), s32[]{:S(2)}) async-start(), calls=%async_computation.32 | async-start | bytes 4456448
  791.8 202.4 %reduce-scatter.30.cloned.1.call-start = ((), (), s32[]{:S(2)}) async-start(), calls=%async_computation.26 | async-start | bytes 4456448 | tf_op jit(solution)/shard_map/reduce_scatter | solution.py:288
  801.3 276.0 %reduce-scatter.32.cloned.1.call-start = ((), (), s32[]{:S(2)}) async-start(), calls=%async_computation.27 | async-start | bytes 4456448 | tf_op jit(solution)/shard_map/reduce_scatter | solution.py:291
  810.9 336.2 %reduce-scatter.36.cloned.1.call-start = ((), (), s32[]{:S(2)}) async-start(), calls=%async_computation.29 | async-start | bytes 1114112
  882.5 334.2 %reduce-scatter.40.cloned.1.call-start = ((), (), s32[]{:S(2)}) async-start(), calls=%async_computation.31 | async-start | bytes 1114112
  889.6 397.7 %reduce-scatter.34.cloned.1.call-start = ((), (), s32[]{:S(2)}) async-start(), calls=%async_computation.28 | async-start | bytes 1114112
  896.8 460.3 %reduce-scatter.38.cloned.1.call-start = ((), (), s32[]{:S(2)}) async-start(), calls=%async_computation.30 | async-start | bytes 1114112
  906.3 505.7 %reduce-scatter.28.cloned.1.call-start = ((), (), s32[]{:S(2)}) async-start(), calls=%async_computation.25 | async-start | bytes 4718592 | tf_op jit(solution)/shard_map/reduce_scatter | solution.py:272
  913.8 498.3 %copy-start.15 = (bf16[1,128,2048]{2,1,0:T(8,128)(2,1)S(1)}, bf16[1,128,2048]{2,1,0:T(8,128)(2,1)}, u32[]{:S(2)}) copy-start(bf16[1,128,2048]{2,1,0:T(8,128)(2,1)} %reduce-scatter.26.cloned.1.call-done) | copy-start | bytes 1572868
  (45 other events, 1045.9 us)
Sparse Core Ops, SparseCore 0:
  10.5 47.4 all-gather.15
  59.6 51.6 all-gather.11
  113.7 43.5 all-gather.17
  159.6 43.7 all-gather.13
  205.5 44.0 all-gather.19
  255.6 91.7 reduce-scatter.21
  349.8 54.6 all-gather.23
  406.7 51.6 all-gather.21
  460.8 54.5 all-gather.25
  517.6 57.8 all-gather.27
  585.0 51.9 reduce-scatter.23
  642.1 51.4 all-gather.29
  719.3 51.8 reduce-scatter.25
  775.9 51.4 all-gather.31
  831.3 79.0 reduce-scatter.41
  914.9 79.2 reduce-scatter.29
  998.0 79.2 reduce-scatter.31
  1081.5 65.5 reduce-scatter.35
  1150.9 65.8 reduce-scatter.39
  1221.5 65.8 reduce-scatter.33
  1291.2 65.8 reduce-scatter.37
  1359.6 52.3 reduce-scatter.27
where the time goes:
time: 1430 us; the launch traced here: 1420 us
  waiting for transfers between devices  1060 us (74%)
  matrix products  150 us (10%)
  blocking collectives  103 us (7%)
  other arithmetic  44 us (3%)
  local copies, waits for them, and re-layouts  40.9 us (3%)
  between operations  15.9 us (1%)
    unnamed x27, waiting for transfers between devices  212 us
    reduce_scatter x1, waiting for transfers between devices, local(): lax.psum_scatter(branch_part, 'tensor', scatter_dimension=1, tiled=True)  91.1 us
    reduce_scatter x1, waiting for transfers between devices, local(): lax.psum_scatter(w_up_part.astype(jnp.bfloat16), 'dp', scatter_dimension=...  81.4 us
    reduce_scatter x1, waiting for transfers between devices, local(): lax.psum_scatter(w_gate_part.astype(jnp.bfloat16), 'dp', scatter_dimensio...  78.3 us
    psum x1, blocking collectives, local(): lax.psum((q_gain_full, k_gain_full, attn_gain_part, mlp_gain_part), ('dp'...  65.7 us
    all_gather x1, waiting for transfers between devices, local(): lax.all_gather(res_low, 'tensor', axis=1, tiled=True)  53.9 us
    all_gather x1, waiting for transfers between devices, local(): lax.all_gather(tokens, 'tensor', axis=1, tiled=True)  53.3 us
    reduce_scatter x1, waiting for transfers between devices, local(): lax.psum_scatter(d_input_part.astype(jnp.bfloat16), 'tensor', scatter_dim...  53.2 us
  transfers between devices with their start and end apart: 22, of which 21 were waited for; matrix products, arithmetic and copies ran while one was open for 13% of the time, Pallas kernels for 0%

commit v1 on v0

--- a/solution.py
+++ b/solution.py
@@ -1,13 +1,469 @@
+import functools
 import jax
 import jax.numpy as jnp
 from jax import lax
+from jax.experimental import pallas as pl
+from jax.experimental.pallas import tpu as pltpu
 from jax.sharding import PartitionSpec as P
 
 HEAD_DIM = 128
-
-
 EPS = 1e-06
 THETA = 500000.0
+MESH = pl.DeviceIdType.MESH
+BF16 = jnp.bfloat16
+F32 = jnp.float32
+ANY = pl.BlockSpec(memory_space=pl.ANY)
+VM = pl.BlockSpec(memory_space=pltpu.VMEM)
+CUT = 80
+
+
+def place():
+    d = lax.axis_index("dp")
+    t = lax.axis_index("tensor")
+    return d // 8, lax.rem(d // 2, 4), lax.rem(d, 2), t // 4, lax.rem(t, 4)
+
+
+def other(dyh=0, dx=0, dc=0, dyl=0, dz=0):
+    yh, x, c, yl, z = place()
+    return (
+        lax.rem(yh + dyh, 2) * 8 + lax.rem(x + dx, 4) * 2 + lax.rem(c + dc, 2),
+        lax.rem(yl + dyl, 2) * 4 + lax.rem(z + dz, 4),
+    )
+
+
+TENSOR_PEERS = (dict(dz=1), dict(dz=2), dict(dz=3), dict(dyl=1))
+DP_PEERS = (dict(dx=1), dict(dx=2), dict(dx=3), dict(dyh=1), dict(dc=1))
+
+
+def greet(peers):
+    barrier = pltpu.get_barrier_semaphore()
+    for peer in peers:
+        pl.semaphore_signal(barrier, 1, device_id=other(**peer), device_id_type=MESH)
+    pl.semaphore_wait(barrier, len(peers))
+
+
+def remote(src, dst, ssem, rsem, peer):
+    return pltpu.make_async_remote_copy(
+        src_ref=src,
+        dst_ref=dst,
+        send_sem=ssem,
+        recv_sem=rsem,
+        device_id=other(**peer),
+        device_id_type=MESH,
+    )
+
+
+class GatherTensor:
+    COPIES = 10
+
+    def __init__(self, buf, ssem, rsem):
+        yh, x, c, yl, z = place()
+        me = yl * 4 + z
+        pair = (1 - yl) * 4 + z
+        self.own = [
+            remote(buf.at[me], buf.at[me], ssem.at[i], rsem.at[i], dict(dz=i + 1)) for i in range(3)
+        ]
+        self.own_pair = remote(buf.at[me], buf.at[me], ssem.at[3], rsem.at[3], dict(dyl=1))
+        low = pl.ds(0, CUT)
+        high = pl.ds(CUT, 128 - CUT)
+        self.to_pair = []
+        for i in range(3):
+            slot = yl * 4 + lax.rem(z + 3 - i, 4)
+            block = buf.at[slot, low]
+            self.to_pair.append(remote(block, block, ssem.at[4 + i], rsem.at[4 + i], dict(dyl=1)))
+        block = buf.at[pair, high]
+        self.from_pair = [
+            remote(block, block, ssem.at[7 + i], rsem.at[7 + i], dict(dz=i + 1)) for i in range(3)
+        ]
+
+    def start(self):
+        self.own_pair.start()
+        for i in (0, 2, 1):
+            self.own[i].start()
+
+    def forward(self):
+        self.own_pair.wait_recv()
+        for copy in self.from_pair:
+            copy.start()
+        for i in (0, 2, 1):
+            self.own[i].wait_recv()
+            self.to_pair[i].start()
+
+    def finish(self):
+        for copy in self.from_pair + self.to_pair:
+            copy.wait_recv()
+        for copy in [self.own_pair] + self.own + self.to_pair + self.from_pair:
+            copy.wait_send()
+
+
+class ScatterTensor:
+    COPIES = 14
+
+    @staticmethod
+    def scratch(n):
+        return [
+            pltpu.VMEM((4, CUT, n), BF16),
+            pltpu.VMEM((3, 2, 128 - CUT, n), BF16),
+            pltpu.VMEM((3, CUT, n), BF16),
+            pltpu.VMEM((128 - CUT, n), BF16),
+            pltpu.SemaphoreType.DMA((14,)),
+            pltpu.SemaphoreType.DMA((14,)),
+        ]
+
+    def __init__(self, part, from_pair, from_z, total_z, total_pair, ssem, rsem):
+        self.part, self.bufs = part, (from_pair, from_z, total_z, total_pair)
+        yh, x, c, yl, z = place()
+        self.yl, self.z = yl, z
+        low = pl.ds(0, CUT)
+        high = pl.ds(CUT, 128 - CUT)
+        self.first_pair = []
+        for i in range(4):
+            q = lax.rem(z + i, 4)
+            self.first_pair.append(
+                remote(part.at[(1 - yl) * 4 + q, low], from_pair.at[i], ssem.at[i], rsem.at[i], dict(dyl=1))
+            )
+        self.first_z = []
+        for i in range(3):
+            for k in range(2):
+                n = 4 + 2 * i + k
+                row = lax.rem(yl + k, 2) * 4 + lax.rem(z + i + 1, 4)
+                self.first_z.append(
+                    remote(part.at[row, high], from_z.at[i, k], ssem.at[n], rsem.at[n], dict(dz=i + 1))
+                )
+        self.second_z = [
+            remote(
+                part.at[yl * 4 + lax.rem(z + i + 1, 4), low],
+                total_z.at[i],
+                ssem.at[10 + i],
+                rsem.at[10 + i],
+                dict(dz=i + 1),
+            )
+            for i in range(3)
+        ]
+        self.second_pair = remote(
+            part.at[(1 - yl) * 4 + z, high], total_pair, ssem.at[13], rsem.at[13], dict(dyl=1)
+        )
+
+    def start(self):
+        for i in (1, 3, 2, 0):
+            self.first_pair[i].start()
+        for k in (1, 0):
+            for i in (0, 2, 1):
+                self.first_z[2 * i + k].start()
+
+    def middle(self):
+        from_pair, from_z, _, _ = self.bufs
+        yl, z, part = self.yl, self.z, self.part
+        low = pl.ds(0, CUT)
+        high = pl.ds(CUT, 128 - CUT)
+        for i in (1, 3, 2, 0):
+            self.first_pair[i].wait_recv()
+            slot = yl * 4 + lax.rem(z + i, 4)
+            part[slot, low] = (part[slot, low].astype(F32) + from_pair[i].astype(F32)).astype(BF16)
+            if i:
+                self.second_z[i - 1].start()
+        for k in (1, 0):
+            slot = lax.rem(yl + k, 2) * 4 + z
+            for i in range(3):
+                self.first_z[2 * i + k].wait_recv()
+            total = part[slot, high].astype(F32)
+            for i in range(3):
+                total += from_z[i, k].astype(F32)
+            part[slot, high] = total.astype(BF16)
+            if k:
+                self.second_pair.start()
+
+    def finish(self, out):
+        _, _, total_z, total_pair = self.bufs
+        part, me = self.part, self.yl * 4 + self.z
+        for copy in self.second_z:
+            copy.wait_recv()
+        total = part[me, 0:CUT].astype(F32)
+        for i in range(3):
+            total += total_z[i].astype(F32)
+        out[0:CUT] = total.astype(out.dtype)
+        self.second_pair.wait_recv()
+        out[CUT:128] = (part[me, CUT:128].astype(F32) + total_pair[...].astype(F32)).astype(out.dtype)
+        for copy in self.first_pair + self.first_z + self.second_z + [self.second_pair]:
+            copy.wait_send()
+
+
+def block_of(ref, kind, slot):
+    if kind == "slot":
+        return ref.at[slot]
+    size = ref.shape[1] // 16
+    return ref.at[:, pl.ds(pl.multiple_of(slot * size, size), size)]
+
+
+class GatherDp:
+    COPIES = 15
+
+    def __init__(self, shard, out, kind, ssem, rsem, lsem):
+        yh, x, c, yl, z = place()
+        slot = lambda a, b, d: a * 8 + b * 2 + d
+        mine = block_of(out, kind, slot(yh, x, c))
+        self.local = pltpu.make_async_copy(shard, mine, lsem)
+        self.own = [remote(shard, mine, ssem.at[i], rsem.at[i], dict(dx=i + 1)) for i in range(3)]
+        self.own_y = remote(shard, mine, ssem.at[3], rsem.at[3], dict(dyh=1))
+        far = block_of(out, kind, slot(1 - yh, x, c))
+        self.far = [remote(far, far, ssem.at[4 + i], rsem.at[4 + i], dict(dx=i + 1)) for i in range(3)]
+        self.core = [remote(shard, mine, ssem.at[7], rsem.at[7], dict(dc=1))]
+        for k in range(2):
+            for i in range(4):
+                if k == 0 and i == 0:
+                    continue
+                n = 7 + 4 * k + i
+                block = block_of(out, kind, slot(lax.rem(yh + k, 2), lax.rem(x + 4 - i, 4), c))
+                self.core.append(remote(block, block, ssem.at[n], rsem.at[n], dict(dc=1)))
+
+    def start(self):
+        self.own_y.start()
+        for i in (0, 2, 1):
+            self.own[i].start()
+        self.core[0].start()
+        self.local.start()
+
+    def forward(self):
+        self.own_y.wait_recv()
+        for i in (0, 2, 1):
+            self.far[i].start()
+        self.core[4].start()
+
+    def share(self):
+        for i in (0, 2, 1):
+            self.own[i].wait_recv()
+            self.core[1 + i].start()
+        for i in (0, 2, 1):
+            self.far[i].wait_recv()
+            self.core[5 + i].start()
+
+    def finish(self):
+        for copy in self.core:
+            copy.wait_recv()
+        self.local.wait()
+        for copy in self.own + [self.own_y] + self.far + self.core:
+            copy.wait_send()
+
+
+class ScatterDp:
+    COPIES = 8 + 6 + 1
+
+    @staticmethod
+    def scratch(block):
+        return [
+            pltpu.VMEM((8,) + block, BF16),
+            pltpu.VMEM((3, 2) + block, BF16),
+            pltpu.VMEM(block, BF16),
+            pltpu.SemaphoreType.DMA((15,)),
+            pltpu.SemaphoreType.DMA((15,)),
+        ]
+
+    def __init__(self, part, kind, from_core, from_x, from_y, ssem, rsem):
+        yh, x, c, yl, z = place()
+        self.from_core, self.from_x, self.from_y = from_core, from_x, from_y
+        self.block = lambda k, i, d: block_of(
+            part, kind, lax.rem(yh + k, 2) * 8 + lax.rem(x + i, 4) * 2 + d
+        )
+        self.c = c
+        self.core, self.along = [], []
+        for k in range(2):
+            for i in range(4):
+                n = k * 4 + i
+                self.core.append(
+                    remote(self.block(k, i, 1 - c), from_core.at[n], ssem.at[n], rsem.at[n], dict(dc=1))
+                )
+        for k in range(2):
+            for i in range(3):
+                n = 8 + k * 3 + i
+                self.along.append(
+                    remote(self.block(k, i + 1, c), from_x.at[i, k], ssem.at[n], rsem.at[n], dict(dx=i + 1))
+                )
+        self.last = remote(self.block(1, 0, c), from_y, ssem.at[14], rsem.at[14], dict(dyh=1))
+
+    def start(self):
+        for k in (1, 0):
+            for i in (1, 3, 2, 0):
+                self.core[k * 4 + i].start()
+
+    def along_x(self):
+        for k in (1, 0):
+            for i in (1, 3, 2, 0):
+                n = k * 4 + i
+                self.core[n].wait_recv()
+                ref = self.block(k, i, self.c)
+                ref[...] = (ref[...].astype(F32) + self.from_core[n].astype(F32)).astype(BF16)
+                if i:
+                    self.along[k * 3 + i - 1].start()
+
+    def along_y(self):
+        for i in (0, 2, 1):
+            self.along[3 + i].wait_recv()
+        ref = self.block(1, 0, self.c)
+        total = ref[...].astype(F32)
+        for i in range(3):
+            total += self.from_x[i, 1].astype(F32)
+        ref[...] = total.astype(BF16)
+        self.last.start()
+
+    def finish(self, out):
+        for i in (0, 2, 1):
+            self.along[i].wait_recv()
+        total = self.block(0, 0, self.c)[...].astype(F32)
+        for i in range(3):
+            total += self.from_x[i, 0].astype(F32)
+        self.last.wait_recv()
+        out[...] = total + self.from_y[...].astype(F32)
+        for copy in self.core + self.along + [self.last]:
+            copy.wait_send()
+
+
+def params(cid, vmem=60):
+    return pltpu.CompilerParams(
+        collective_id=cid, has_side_effects=True, vmem_limit_bytes=vmem << 20
+    )
+
+
+def gather_tensor(shard, cid):
+    n = shard.shape[1]
+
+    def gather_rows(shard_ref, out_ref, ssem, rsem, lsem):
+        yh, x, c, yl, z = place()
+        local = pltpu.make_async_copy(shard_ref, out_ref.at[yl * 4 + z], lsem)
+        local.start()
+        greet(TENSOR_PEERS)
+        local.wait()
+        gather = GatherTensor(out_ref, ssem, rsem)
+        gather.start()
+        gather.forward()
+        gather.finish()
+
+    out = pl.pallas_call(
+        gather_rows,
+        out_shape=jax.ShapeDtypeStruct((8, 128, n), shard.dtype),
+        in_specs=[ANY],
+        out_specs=ANY,
+        scratch_shapes=[
+            pltpu.SemaphoreType.DMA((10,)),
+            pltpu.SemaphoreType.DMA((10,)),
+            pltpu.SemaphoreType.DMA,
+        ],
+        compiler_params=params(cid, 16),
+        name="gather_rows_%d" % cid,
+    )(shard)
+    return out.reshape(1024, n)
+
+
+def scatter_tensor(part, cid):
+    n = part.shape[1]
+
+    def scatter_rows(part_ref, out_ref, mine, b0, b1, b2, b3, ssem, rsem, lsem):
+        local = pltpu.make_async_copy(part_ref, mine, lsem)
+        local.start()
+        greet(TENSOR_PEERS)
+        local.wait()
+        scatter = ScatterTensor(mine, b0, b1, b2, b3, ssem, rsem)
+        scatter.start()
+        scatter.middle()
+        scatter.finish(out_ref)
+
+    return pl.pallas_call(
+        scatter_rows,
+        out_shape=jax.ShapeDtypeStruct((128, n), F32),
+        in_specs=[ANY],
+        out_specs=VM,
+        scratch_shapes=[pltpu.VMEM((8, 128, n), BF16)]
+        + ScatterTensor.scratch(n)
+        + [pltpu.SemaphoreType.DMA],
+        compiler_params=params(cid, 40),
+        name="scatter_rows_%d" % cid,
+    )(part.reshape(8, 128, n))
+
+
+def gather_dp(shards, kinds, cid):
+    outs = []
+    for shard, kind in zip(shards, kinds):
+        a, b = shard.shape
+        outs.append(
+            jax.ShapeDtypeStruct((16, a, b) if kind == "slot" else (a, 16 * b), shard.dtype)
+        )
+    n = len(shards)
+
+    def gather_weights(*refs):
+        ins, outs, (ssem, rsem, lsem) = refs[:n], refs[n : 2 * n], refs[2 * n :]
+        greet(DP_PEERS)
+        items = [
+            GatherDp(ins[i], outs[i], kinds[i], ssem.at[i], rsem.at[i], lsem.at[i])
+            for i in range(n)
+        ]
+        for item in items:
+            item.start()
+        for item in items:
+            item.forward()
+        for item in items:
+            item.share()
+        for item in items:
+            item.finish()
+
+    full = pl.pallas_call(
+        gather_weights,
+        out_shape=outs,
+        in_specs=[ANY] * n,
+        out_specs=[ANY] * n,
+        scratch_shapes=[
+            pltpu.SemaphoreType.DMA((n, 15)),
+            pltpu.SemaphoreType.DMA((n, 15)),
+            pltpu.SemaphoreType.DMA((n,)),
+        ],
+        compiler_params=params(cid, 16),
+        name="gather_weights_%d" % cid,
+    )(*shards)
+    return [
+        f.reshape(16 * f.shape[1], f.shape[2]) if kind == "slot" else f
+        for f, kind in zip(full, kinds)
+    ]
+
+
+def scatter_dp(parts, kinds, cid):
+    n = len(parts)
+    shapes, ins = [], []
+    for part, kind in zip(parts, kinds):
+        a, b = part.shape
+        shapes.append((a // 16, b) if kind == "slot" else (a, b // 16))
+        ins.append(part.reshape(16, a // 16, b) if kind == "slot" else part)
+    scratch = []
+    for array, shape in zip(ins, shapes):
+        scratch += [pltpu.VMEM(array.shape, BF16)] + ScatterDp.scratch(shape)
+    scratch.append(pltpu.SemaphoreType.DMA((n,)))
+
+    def scatter_grads(*refs):
+        parts, outs, rest = refs[:n], refs[n : 2 * n], refs[2 * n :]
+        lsem = rest[-1]
+        local = [
+            pltpu.make_async_copy(parts[i], rest[6 * i], lsem.at[i]) for i in range(n)
+        ]
+        for copy in local:
+            copy.start()
+        greet(DP_PEERS)
+        items = [ScatterDp(rest[6 * i], kinds[i], *rest[6 * i + 1 : 6 * i + 6]) for i in range(n)]
+        for copy, item in zip(local, items):
+            copy.wait()
+            item.start()
+        for item in items:
+            item.along_x()
+        for item in items:
+            item.along_y()
+        for item, out in zip(items, outs):
+            item.finish(out)
+
+    return pl.pallas_call(
+        scatter_grads,
+        out_shape=[jax.ShapeDtypeStruct(s, F32) for s in shapes],
+        in_specs=[ANY] * n,
+        out_specs=[VM] * n,
+        scratch_shapes=scratch,
+        compiler_params=params(cid, 60),
+        name="scatter_grads_%d" % cid,
+    )(*ins)
 
 
 def rope_tables(count, size):
@@ -131,23 +587,14 @@
     full_len = part_len * tp_count
     columns = w_query.shape[1]
     heads_dev = columns // HEAD_DIM
-    gathered = (
-        lax.all_gather(w_query, "dp", axis=0, tiled=True),
-        lax.all_gather(w_key, "dp", axis=0, tiled=True),
-        lax.all_gather(w_value, "dp", axis=0, tiled=True),
-        lax.all_gather(w_out, "dp", axis=1, tiled=True),
-        lax.all_gather(w_gate, "dp", axis=0, tiled=True),
-        lax.all_gather(w_up, "dp", axis=0, tiled=True),
-        lax.all_gather(w_down, "dp", axis=1, tiled=True),
-    )
+    kinds = ("slot", "slot", "slot", "col", "slot", "slot", "col")
+    gathered = gather_dp((w_query, w_key, w_value, w_out, w_gate, w_up, w_down), kinds, 1)
     wq_full, wk_full, wv_full, wo_full, wg_full, wu_full, wd_full = gathered
     q_gain_dev = lax.dynamic_slice_in_dim(q_gain, tp_index * columns, columns)
     k_gain_dev = lax.dynamic_slice_in_dim(k_gain, tp_index * columns, columns)
     positions = tp_index * part_len + lax.broadcasted_iota(jnp.int32, (sequences, part_len), 1)
     valid_rows = (positions < lengths[:, None])[..., None]
-    whole_rows = lax.all_gather(tokens, "tensor", axis=1, tiled=True).reshape(
-        sequences * full_len, width
-    )
+    whole_rows = gather_tensor(tokens[0], 2)
     q_raw = jnp.dot(whole_rows, wq_full, preferred_element_type=jnp.float32)
     k_raw = jnp.dot(whole_rows, wk_full, preferred_element_type=jnp.float32)
     v_raw = jnp.dot(whole_rows, wv_full, preferred_element_type=jnp.float32)
@@ -171,13 +618,11 @@
     branch_part = jnp.dot(mixed_flat, wo_full, preferred_element_type=jnp.float32).reshape(
         sequences, full_len, width
     )
-    branch = lax.psum_scatter(branch_part, "tensor", scatter_dimension=1, tiled=True)
+    branch = scatter_tensor(branch_part.astype(jnp.bfloat16)[0], 10)[None]
     b_scale = rms_scale(branch)
     residual = tokens.astype(jnp.float32) + branch * b_scale * attn_gain
     res_low = residual.astype(jnp.bfloat16)
-    res_whole = lax.all_gather(res_low, "tensor", axis=1, tiled=True).reshape(
-        sequences * full_len, width
-    )
+    res_whole = gather_tensor(res_low[0], 3)
     gate_value = jnp.dot(res_whole, wg_full, preferred_element_type=jnp.float32)
     up_value = jnp.dot(res_whole, wu_full, preferred_element_type=jnp.float32)
     sigmoid_gate = jax.nn.sigmoid(gate_value)
@@ -186,29 +631,17 @@
     down_part = jnp.dot(inner_act, wd_full, preferred_element_type=jnp.float32).reshape(
         sequences, full_len, width
     )
-    down_value = lax.psum_scatter(
-        down_part.astype(jnp.bfloat16), "tensor", scatter_dimension=1, tiled=True
-    ).astype(jnp.float32)
+    down_value = scatter_tensor(down_part.astype(jnp.bfloat16)[0], 11)[None]
     d_scale = rms_scale(down_value)
     activations = jnp.where(valid_rows, residual + down_value * d_scale * mlp_gain, 0.0).astype(
         jnp.bfloat16
     )
-    back_weights = (
-        lax.all_gather(w_query, "dp", axis=0, tiled=True),
-        lax.all_gather(w_key, "dp", axis=0, tiled=True),
-        lax.all_gather(w_value, "dp", axis=0, tiled=True),
-        lax.all_gather(w_out, "dp", axis=1, tiled=True),
-        lax.all_gather(w_gate, "dp", axis=0, tiled=True),
-        lax.all_gather(w_up, "dp", axis=0, tiled=True),
-        lax.all_gather(w_down, "dp", axis=1, tiled=True),
-    )
+    back_weights = gathered
     wq_back, wk_back, wv_back, wo_back, wg_back, wu_back, wd_back = back_weights
     grad_out = jnp.where(valid_rows, cotangent.astype(jnp.float32), 0.0)
     mlp_gain_part = jnp.sum(grad_out * down_value * d_scale, (0, 1))
     d_down = norm_back(down_value, d_scale, mlp_gain, grad_out).astype(jnp.bfloat16)
-    d_down_whole = lax.all_gather(d_down, "tensor", axis=1, tiled=True).reshape(
-        sequences * full_len, width
-    )
+    d_down_whole = gather_tensor(d_down[0], 4)
     d_inner = dot_last(d_down_whole, wd_back)
     w_down_part = dot_first(inner_act, d_down_whole)
     d_gate = (d_inner * up_value * sigmoid_gate * (1.0 + gate_value * (1.0 - sigmoid_gate))).astype(
@@ -220,14 +653,10 @@
     d_res_part = (dot_last(d_gate, wg_back) + dot_last(d_up, wu_back)).reshape(
         sequences, full_len, width
     )
-    d_res = grad_out + lax.psum_scatter(
-        d_res_part.astype(jnp.bfloat16), "tensor", scatter_dimension=1, tiled=True
-    ).astype(jnp.float32)
+    d_res = grad_out + scatter_tensor(d_res_part.astype(jnp.bfloat16)[0], 12)[None]
     attn_gain_part = jnp.sum(d_res * branch * b_scale, (0, 1))
     d_branch = norm_back(branch, b_scale, attn_gain, d_res).astype(jnp.bfloat16)
-    d_branch_whole = lax.all_gather(d_branch, "tensor", axis=1, tiled=True).reshape(
-        sequences * full_len, width
-    )
+    d_branch_whole = gather_tensor(d_branch[0], 5)
     w_out_part = dot_first(mixed_flat, d_branch_whole)
     mixed_value_gradient = (
         dot_last(d_branch_whole, wo_back).astype(jnp.bfloat16).reshape(head_shape)
@@ -269,32 +698,9 @@
     d_input_part = (
         dot_last(d_qraw, wq_back) + dot_last(d_kraw, wk_back) + dot_last(d_vflat, wv_back)
     ).reshape(sequences, full_len, width)
-    input_grad = d_res + lax.psum_scatter(
-        d_input_part.astype(jnp.bfloat16), "tensor", scatter_dimension=1, tiled=True
-    ).astype(jnp.float32)
-    grads_owned = (
-        lax.psum_scatter(
-            w_query_part.astype(jnp.bfloat16), "dp", scatter_dimension=0, tiled=True
-        ).astype(jnp.float32),
-        lax.psum_scatter(
-            w_key_part.astype(jnp.bfloat16), "dp", scatter_dimension=0, tiled=True
-        ).astype(jnp.float32),
-        lax.psum_scatter(
-            w_value_part.astype(jnp.bfloat16), "dp", scatter_dimension=0, tiled=True
-        ).astype(jnp.float32),
-        lax.psum_scatter(
-            w_out_part.astype(jnp.bfloat16), "dp", scatter_dimension=1, tiled=True
-        ).astype(jnp.float32),
-        lax.psum_scatter(
-            w_gate_part.astype(jnp.bfloat16), "dp", scatter_dimension=0, tiled=True
-        ).astype(jnp.float32),
-        lax.psum_scatter(
-            w_up_part.astype(jnp.bfloat16), "dp", scatter_dimension=0, tiled=True
-        ).astype(jnp.float32),
-        lax.psum_scatter(
-            w_down_part.astype(jnp.bfloat16), "dp", scatter_dimension=1, tiled=True
-        ).astype(jnp.float32),
-    )
+    input_grad = d_res + scatter_tensor(d_input_part.astype(jnp.bfloat16)[0], 13)[None]
+    parts = (w_query_part, w_key_part, w_value_part, w_out_part, w_gate_part, w_up_part, w_down_part)
+    grads_owned = scatter_dp([part.astype(jnp.bfloat16) for part in parts], kinds, 14)
     empty_gain = jnp.zeros((width,), jnp.float32)
     q_gain_full = lax.dynamic_update_slice_in_dim(empty_gain, q_gain_part, tp_index * columns, 0)
     k_gain_full = lax.dynamic_update_slice_in_dim(empty_gain, k_gain_part, tp_index * columns, 0)

time: 1430 us -> 769 us (0.54)
  waiting for transfers between devices: 1060 us -> 0 us
  Pallas kernels: 0 us -> 470 us
  matrix products: 150 us -> 114 us
  other arithmetic: 44 us -> 27.4 us
    pallas_call x0 -> x10, Pallas kernels: none -> 470 us  [the longest x4 139 us: gather_tensor(): pl.pallas_call(gather_rows, out_shape=jax.ShapeDtypeStruct((8, 128, n), s...]
    all_gather x11 -> x0, waiting for transfers between devices: 445 us -> none  [the longest x1 53.9 us: local(): lax.all_gather(res_low, 'tensor', axis=1, tiled=True)]
    reduce_scatter x6 -> x0, waiting for transfers between devices: 408 us -> none  [the longest x1 91.1 us: local(): lax.psum_scatter(branch_part, 'tensor', scatter_dimension=1, tiled=True)]
    unnamed x27 -> x0, waiting for transfers between devices: 212 us -> none
    unnamed x111 -> x183, local copies, waits for them, and re-layouts: 32.9 us -> 36.4 us
  transfers between devices with their start and end apart: 22 -> 0, of which waited for: 21 -> 0; matrix products, arithmetic and copies ran while one was open for 13% -> 0% of each run, Pallas kernels for 0% -> 0%
where the time goes in v1:
time: 769 us; the launch traced here: 763 us
  Pallas kernels  470 us (61%)
  matrix products  114 us (15%)
  blocking collectives  99.5 us (13%)
  local copies, waits for them, and re-layouts  49 us (6%)
  other arithmetic  27.4 us (4%)
    pallas_call x4, Pallas kernels, gather_tensor(): pl.pallas_call(gather_rows, out_shape=jax.ShapeDtypeStruct((8, 128, n), s...  139 us
    pallas_call x4, Pallas kernels, scatter_tensor(): pl.pallas_call(scatter_rows, out_shape=jax.ShapeDtypeStruct((128, n), F32...  131 us
    pallas_call x1, Pallas kernels, scatter_dp(): pl.pallas_call(scatter_grads, out_shape=[jax.ShapeDtypeStruct(s, F32) for...  100 us
    pallas_call x1, Pallas kernels, gather_dp(): pl.pallas_call(gather_weights, out_shape=outs, in_specs=[ANY] * n, out_sp...  99.9 us
    psum x1, blocking collectives, local(): lax.psum((q_gain_full, k_gain_full, attn_gain_part, mlp_gain_part), ('dp'...  63.3 us
    dot_general x7, matrix products, dot_last(): lax.dot_general(left, right, (((1,), (1,)), ((), ())), preferred_element_...  38.9 us
    dot_general x7, matrix products, dot_first(): lax.dot_general(left, right, (((0,), (0,)), ((), ())), preferred_element_...  37 us
    unnamed x183, local copies, waits for them, and re-layouts  36.4 us

profile of v1, /device:TPU:0, one launch (start us, length us, event | category | flops | bytes accessed | tf_op | source)
XLA Modules:
  0.0 763.4 jit_solution(17168721902506174988)
XLA Ops:
  6.9 99.9 %gather_weights_1.1 = (bf16[16,128,256]{2,1,0:T(8,128)(2,1)S(1)}, bf16[16,128,256]{2,1,0:T(8,128)(2,1)S(1)}, bf16[16,128,256]{2,1,0:T(8,128)(2,1)S(1)}, bf16[256...) custom-call(bf16[128,256]{1,0:T(8,128)(2,1)S(1)} %copy-done.22, ...), custom_call_target="tpu_custom_call" | custom-call | tf_op jit(solution)/shard_map/gather_weights_1/pallas_call | solution.py:407
  114.3 40.1 %gather_rows_2.1 = bf16[8,128,2048]{2,1,0:T(8,128)(2,1)S(1)} custom-call(bf16[128,2048]{1,0:T(8,128)(2,1)S(1)} %bitcast.196), custom_call_target="tpu_custom_call" | custom-call | tf_op jit(solution)/shard_map/gather_rows_2/pallas_call | solution.py:340
  158.0 18.1 %all-reduce.2 = (f32[1024]{0:T(1024)S(1)}, f32[1024]{0:T(1024)S(1)}) all-reduce(f32[1024]{0:T(1024)S(1)} %get-tuple-element.139, f32[1024]{0:T(1024)S(1)} %get-tuple-element.141), channel_id=1, replica_groups=mesh['dp'=16,'tensor'=8] {'tensor'}, use_global_device_ids=true, to_apply=%region_1.0 | all-reduce | flops 2048 | bytes 16384 | tf_op jit(solution)/shard_map/psum | solution.py:601
  209.8 34.3 %scatter_rows_10.1 = f32[128,2048]{1,0:T(8,128)S(1)} custom-call(bf16[8,128,2048]{2,1,0:T(8,128)(2,1)S(1)} %bitcast.194), custom_call_target="tpu_custom_call" | custom-call | tf_op jit(solution)/shard_map/scatter_rows_10/pallas_call | solution.py:369
  244.5 32.8 %gather_rows_3.1 = bf16[8,128,2048]{2,1,0:T(8,128)(2,1)S(1)} custom-call(bf16[128,2048]{1,0:T(8,128)(2,1)S(1)} %fusion.35.shard_ref), custom_call_target="tpu_custom_call" | custom-call | tf_op jit(solution)/shard_map/gather_rows_3/pallas_call | solution.py:340
  281.9 6.5 multiply_convert_fusion.3
  288.4 4.7 convolution_convert_fusion.4
  293.2 33.5 %scatter_rows_11.1 = f32[128,2048]{1,0:T(8,128)S(1)} custom-call(bf16[8,128,2048]{2,1,0:T(8,128)(2,1)S(1)} %bitcast.198), custom_call_target="tpu_custom_call" | custom-call | tf_op jit(solution)/shard_map/scatter_rows_11/pallas_call | solution.py:369
  327.7 34.5 %gather_rows_4.1 = bf16[8,128,2048]{2,1,0:T(8,128)(2,1)S(1)} custom-call(bf16[128,2048]{1,0:T(8,128)(2,1)S(1)} %fusion.38.shard_ref), custom_call_target="tpu_custom_call" | custom-call | tf_op jit(solution)/shard_map/gather_rows_4/pallas_call | solution.py:340
  362.3 11.0 %multiply_convert_fusion.1 = (bf16[1024,1024]{1,0:T(8,128)(2,1)}, bf16[1024,1024]{1,0:T(8,128)(2,1)}) fusion(f32[1024,1024]{1,0:T(8,128)S(1)} %copy-done.81, f32[1024,1024]{1,0:T(8,128)} %get-tuple-element.146, bf16[1024,2048]{1,0:T(8,128)(2,1)S(1)} %bitcast.209, bf16[1024,2048]{1,0:T(8,128)(2,1)S(1)} %copy-done.34), kind=kOutput, calls=%fused_computation.12 | convolution fusion | flops 4308598784 | bytes 20971520 | tf_op jit(solution)/shard_map/dot_general | solution.py:488
  373.2 8.6 %fusion.50 = f32[1024,2048]{1,0:T(8,128)} fusion(bf16[1024,1024]{1,0:T(8,128)(2,1)} %get-tuple-element.109, bf16[2048,1024]{1,0:T(8,128)(2,1)S(1)} %bitcast.222), kind=kOutput, calls=%fused_computation.130 | convolution fusion | flops 4294967296 | bytes 14680064 | tf_op jit(solution)/shard_map/dot_general | solution.py:488
  381.9 7.0 add_convert_fusion.1
  388.9 29.0 %scatter_rows_12.1 = f32[128,2048]{1,0:T(8,128)S(1)} custom-call(bf16[8,128,2048]{2,1,0:T(8,128)(2,1)S(1)} %bitcast.197), custom_call_target="tpu_custom_call" | custom-call | tf_op jit(solution)/shard_map/scatter_rows_12/pallas_call | solution.py:369
  420.0 31.2 %gather_rows_5.1 = bf16[8,128,2048]{2,1,0:T(8,128)(2,1)S(1)} custom-call(bf16[128,2048]{1,0:T(8,128)(2,1)S(1)} %get-tuple-element.118.shard_ref), custom_call_target="tpu_custom_call" | custom-call | tf_op jit(solution)/shard_map/gather_rows_5/pallas_call | solution.py:340
  477.1 63.3 %all-reduce = (f32[2048]{0:T(1024)}, f32[2048]{0:T(1024)}, f32[2048]{0:T(1024)}, f32[2048]{0:T(1024)}) all-reduce(f32[2048]{0:T(1024)S(1)} %dynamic_update_slice.19, f32[2048]{0:T(1024)S(1)} %dynamic_update_slice.20, f32[2048]{0:T(1024)S(1)} %get-tuple-element.92, ...), channel_id=1, replica_groups=mesh['dp'=16,'tensor'=8] {'dp','tensor'}, use_global_device_ids=true, to_apply=%region_16.17 | all-reduce | flops 8192 | bytes 65536 | tf_op jit(solution)/shard_map/psum | solution.py:707
  540.5 9.6 %convolution_convert_fusion.1.refs_6_ = bf16[1024,2048]{1,0:T(8,128)(2,1)} fusion(bf16[1024,1024]{1,0:T(8,128)(2,1)} %copy-done.79, bf16[1024,2048]{1,0:T(8,128)(2,1)} %bitcast.210), kind=kOutput, calls=%fused_computation.23 | convolution fusion | flops 4297064448 | bytes 10485760 | tf_op jit(solution)/shard_map/dot_general | solution.py:494
  552.4 5.9 fusion.15
  561.9 9.6 %convolution_convert_fusion.3 = bf16[2048,1024]{1,0:T(8,128)(2,1)} fusion(bf16[1024,2048]{1,0:T(8,128)(2,1)} %bitcast.207, bf16[1024,1024]{1,0:T(8,128)(2,1)} %get-tuple-element.109), kind=kOutput, calls=%fused_computation.25 | convolution fusion | flops 4297064448 | bytes 10485760 | tf_op jit(solution)/shard_map/dot_general | solution.py:494
  571.4 6.3 convolution_convert_fusion.2
  577.7 18.1 %all-reduce.1 = (f32[1024]{0:T(1024)S(1)}, f32[1024]{0:T(1024)S(1)}) all-reduce(f32[1024]{0:T(1024)S(1)} %get-tuple-element.97, f32[1024]{0:T(1024)S(1)} %get-tuple-element.95), channel_id=1, replica_groups=mesh['dp'=16,'tensor'=8] {'tensor'}, use_global_device_ids=true, to_apply=%region_12.13 | all-reduce | flops 2048 | bytes 16384 | tf_op jit(solution)/shard_map/psum | solution.py:683
  610.9 100.2 %scatter_grads_14.1 = (f32[128,256]{1,0:T(8,128)}, f32[128,256]{1,0:T(8,128)}, f32[128,256]{1,0:T(8,128)}, f32[256,128]{1,0:T(8,128)}, f32[128,1024]{1,0:T(8,128...) custom-call(bf16[16,128,256]{2,1,0:T(8,128)(2,1)} %bitcast.227, bf16[16,128,256]{2,1,0:T(8,128)(2,1)} %bitcast.226, ...), custom_call_target="tpu_custom_call" | custom-call | tf_op jit(solution)/shard_map/scatter_grads_14/pallas_call | solution.py:458
  712.5 4.6 fusion.51
  717.1 5.0 add_convert_fusion
  722.3 34.6 %scatter_rows_13.1 = f32[128,2048]{1,0:T(8,128)S(1)} custom-call(bf16[8,128,2048]{2,1,0:T(8,128)(2,1)S(1)} %bitcast.195), custom_call_target="tpu_custom_call" | custom-call | tf_op jit(solution)/shard_map/scatter_rows_13/pallas_call | solution.py:369
  (247 shorter events, 112.2 us)
Async XLA Ops:
  112.8 42.9 %copy-start.13 = (bf16[16,128,256]{2,1,0:T(8,128)(2,1)}, bf16[16,128,256]{2,1,0:T(8,128)(2,1)S(1)}, u32[]{:S(2)}) copy-start(bf16[16,128,256]{2,1,0:T(8,128)(2,1)S(1)} %get-tuple-element.79) | copy-start | bytes 3145732
  112.8 42.9 %copy-start.15 = (bf16[16,128,256]{2,1,0:T(8,128)(2,1)}, bf16[16,128,256]{2,1,0:T(8,128)(2,1)S(1)}, u32[]{:S(2)}) copy-start(bf16[16,128,256]{2,1,0:T(8,128)(2,1)S(1)} %get-tuple-element.80) | copy-start | bytes 3145732
  112.8 88.0 %copy-start.11 = (bf16[16,128,256]{2,1,0:T(8,128)(2,1)}, bf16[16,128,256]{2,1,0:T(8,128)(2,1)S(1)}, u32[]{:S(2)}) copy-start(bf16[16,128,256]{2,1,0:T(8,128)(2,1)S(1)} %get-tuple-element.78) | copy-start | bytes 3145732
  112.8 95.6 %copy-start.17 = (bf16[256,2048]{1,0:T(8,128)(2,1)}, bf16[256,2048]{1,0:T(8,128)(2,1)S(1)}, u32[]{:S(2)}) copy-start(bf16[256,2048]{1,0:T(8,128)(2,1)S(1)} %get-tuple-element.81) | copy-start | bytes 3145732
  209.8 34.5 %copy-start.1 = (bf16[1,128,2048]{2,1,0:T(8,128)(2,1)S(1)}, bf16[1,128,2048]{2,1,0:T(8,128)(2,1)}, u32[]{:S(2)}) copy-start(bf16[1,128,2048]{2,1,0:T(8,128)(2,1)} %param.14) | copy-start | bytes 1572868
  209.8 34.5 %copy-start.71 = (f32[2048]{0:T(1024)S(1)}, f32[2048]{0:T(1024)}, u32[]{:S(2)}) copy-start(f32[2048]{0:T(1024)} %param.25) | copy-start | bytes 24580
  244.1 33.2 %copy-start.30 = (bf16[16,128,1024]{2,1,0:T(8,128)(2,1)S(1)}, bf16[16,128,1024]{2,1,0:T(8,128)(2,1)}, u32[]{:S(2)}) copy-start(bf16[16,128,1024]{2,1,0:T(8,128)(2,1)} %copy-done.29) | copy-start | bytes 12582916
  293.2 33.7 %copy-start.38 = (bf16[1,128,2048]{2,1,0:T(8,128)(2,1)S(1)}, bf16[1,128,2048]{2,1,0:T(8,128)(2,1)}, u32[]{:S(2)}) copy-start(bf16[1,128,2048]{2,1,0:T(8,128)(2,1)} %param.27) | copy-start | bytes 1572868
  293.2 33.7 %copy-start.76 = (f32[2048]{0:T(1024)S(1)}, f32[2048]{0:T(1024)}, u32[]{:S(2)}) copy-start(f32[2048]{0:T(1024)} %param.26) | copy-start | bytes 24580
  326.9 35.3 %copy-start.34 = (bf16[1024,2048]{1,0:T(8,128)(2,1)S(1)}, bf16[1024,2048]{1,0:T(8,128)(2,1)}, u32[]{:S(2)}) copy-start(bf16[1024,2048]{1,0:T(8,128)(2,1)} %copy-done.32) | copy-start | bytes 12582916
  326.9 35.3 %copy-start.81 = (f32[1024,1024]{1,0:T(8,128)S(1)}, f32[1024,1024]{1,0:T(8,128)}, u32[]{:S(2)}) copy-start(f32[1024,1024]{1,0:T(8,128)} %copy-done.80) | copy-start | bytes 12582916
  388.9 29.1 %copy-start.39 = (bf16[1,128,2048]{2,1,0:T(8,128)(2,1)S(1)}, bf16[1,128,2048]{2,1,0:T(8,128)(2,1)}, u32[]{:S(2)}) copy-start(bf16[1,128,2048]{2,1,0:T(8,128)(2,1)} %param.27) | copy-start | bytes 1572868
  388.9 29.5 %copy-start.2 = (bf16[1,128,2048]{2,1,0:T(8,128)(2,1)S(1)}, bf16[1,128,2048]{2,1,0:T(8,128)(2,1)}, u32[]{:S(2)}) copy-start(bf16[1,128,2048]{2,1,0:T(8,128)(2,1)} %param.14) | copy-start | bytes 1572868
  418.4 34.8 %copy-start.18 = (bf16[256,2048]{1,0:T(8,128)(2,1)S(1)}, bf16[256,2048]{1,0:T(8,128)(2,1)}, u32[]{:S(2)}) copy-start(bf16[256,2048]{1,0:T(8,128)(2,1)} %copy-done.17) | copy-start | bytes 3145732
  418.5 36.1 %slice-start = ((s8[8388608]{0:T(1024)(128)(4,1)}), s8[4194304]{0:T(1024)(128)(4,1)S(1)}, s32[]{:S(2)}) async-start(s8[8388608]{0:T(1024)(128)(4,1)} %bitcast.223), calls=%async_computation | async-start | bytes 8388608
  420.0 34.6 %slice-start.1 = ((s8[8388608]{0:T(1024)(128)(4,1)}), s8[4194304]{0:T(1024)(128)(4,1)S(1)}, s32[]{:S(2)}) async-start(s8[8388608]{0:T(1024)(128)(4,1)} %bitcast.223), calls=%async_computation.1 | async-start | bytes 8388608
  610.9 100.2 %copy-start.16 = (bf16[16,128,256]{2,1,0:T(8,128)(2,1)S(1)}, bf16[16,128,256]{2,1,0:T(8,128)(2,1)}, u32[]{:S(2)}) copy-start(bf16[16,128,256]{2,1,0:T(8,128)(2,1)} %copy-done.15) | copy-start | bytes 3145732
  610.9 100.2 %copy-start.56 = (bf16[1024,256]{0,1:T(8,128)(2,1)S(1)}, bf16[1024,256]{0,1:T(8,128)(2,1)}, u32[]{:S(2)}) copy-start(bf16[1024,256]{0,1:T(8,128)(2,1)} %copy-done.55) | copy-start | bytes 1572868
  722.2 34.6 %copy-start.40 = (bf16[1,128,2048]{2,1,0:T(8,128)(2,1)S(1)}, bf16[1,128,2048]{2,1,0:T(8,128)(2,1)}, u32[]{:S(2)}) copy-start(bf16[1,128,2048]{2,1,0:T(8,128)(2,1)} %param.27) | copy-start | bytes 1572868
  722.2 35.9 %copy-start.75 = (f32[128,256]{1,0:T(8,128)S(1)}, f32[128,256]{1,0:T(8,128)}, u32[]{:S(2)}) copy-start(f32[128,256]{1,0:T(8,128)} %get-tuple-element.166) | copy-start | bytes 393220
  722.2 36.6 %copy-start.74 = (f32[128,256]{1,0:T(8,128)S(1)}, f32[128,256]{1,0:T(8,128)}, u32[]{:S(2)}) copy-start(f32[128,256]{1,0:T(8,128)} %get-tuple-element.167) | copy-start | bytes 393220
  722.2 37.2 %copy-start.73 = (f32[128,256]{1,0:T(8,128)S(1)}, f32[128,256]{1,0:T(8,128)}, u32[]{:S(2)}) copy-start(f32[128,256]{1,0:T(8,128)} %get-tuple-element.168) | copy-start | bytes 393220
  722.2 37.8 %copy-start.72 = (f32[256,128]{1,0:T(8,128)S(1)}, f32[256,128]{1,0:T(8,128)}, u32[]{:S(2)}) copy-start(f32[256,128]{1,0:T(8,128)} %get-tuple-element.169) | copy-start | bytes 393220
  722.3 38.5 %copy-start.66 = (f32[128,1024]{1,0:T(8,128)S(1)}, f32[128,1024]{1,0:T(8,128)}, u32[]{:S(2)}) copy-start(f32[128,1024]{1,0:T(8,128)} %get-tuple-element.170) | copy-start | bytes 1572868
  (62 other events, 316.8 us)

commit v2 on v0

v2 whole, which is shorter than its diff:
```python
import jax
import jax.numpy as jnp
import numpy as np
from jax import lax
from jax.experimental import pallas as pl
from jax.experimental.pallas import tpu as pltpu
from jax.sharding import PartitionSpec as P

HEAD_DIM = 128
EPS = 1e-06
THETA = 500000.0
MESH = pl.DeviceIdType.MESH
BF16 = jnp.bfloat16
F32 = jnp.float32
ANY = pl.BlockSpec(memory_space=pl.ANY)
VM = pl.BlockSpec(memory_space=pltpu.VMEM)
DMA = pltpu.SemaphoreType.DMA
CUT = 896
WIDTH = 2048


def place():
    d = lax.axis_index("dp")
    t = lax.axis_index("tensor")
    return d // 8, lax.rem(d // 2, 4), lax.rem(d, 2), t // 4, lax.rem(t, 4)


def other(dyh=0, dx=0, dc=0, dyl=0, dz=0):
    yh, x, c, yl, z = place()
    return (
        lax.rem(yh + dyh, 2) * 8 + lax.rem(x + dx, 4) * 2 + lax.rem(c + dc, 2),
        lax.rem(yl + dyl, 2) * 4 + lax.rem(z + dz, 4),
    )


TENSOR_PEERS = (dict(dz=1), dict(dz=3), dict(dyl=1))
DP_PEERS = (dict(dx=1), dict(dx=2), dict(dx=3), dict(dyh=1), dict(dc=1))
SMEM = pl.BlockSpec(memory_space=pltpu.SMEM)


def greet(peers):
    barrier = pltpu.get_barrier_semaphore()
    for peer in peers:
        pl.semaphore_signal(barrier, 1, device_id=other(**peer), device_id_type=MESH)
    pl.semaphore_wait(barrier, len(peers))


def remote(src, dst, sems, index, peer):
    ssem, rsem = sems
    return pltpu.make_async_remote_copy(
        src_ref=src,
        dst_ref=dst,
        send_sem=ssem.at[index],
        recv_sem=rsem.at[index],
        device_id=other(**peer),
        device_id_type=MESH,
    )


def rows(ref, slot):
    return ref.at[pl.ds(pl.multiple_of(slot * 128, 128), 128)]


def halves(ref):
    half = ref.shape[0] // 2
    return ref.at[pl.ds(0, half)], ref.at[pl.ds(half, half)]


def add_into(out, *terms):
    @pl.loop(0, out.shape[0] // 16)
    def _(i):
        r = pl.ds(pl.multiple_of(i * 16, 16), 16)
        if len(terms) == 2 and out.dtype == BF16:
            out[r, :] = terms[0][r, :] + terms[1][r, :]
        else:
            total = terms[0][r, :].astype(F32)
            for term in terms[1:]:
                total += term[r, :].astype(F32)
            out[r, :] = total.astype(out.dtype)


class RingGather:
    COPIES = 6

    def __init__(self, block, axis, sems, base, source=None):
        up, down = {axis: 1}, {axis: 3}
        src = halves(block(0) if source is None else source)
        own, behind, ahead = halves(block(0)), halves(block(3)), halves(block(1))
        self.copies = [
            remote(src[0], own[0], sems, base, up),
            remote(src[1], own[1], sems, base + 1, down),
            remote(src[1], own[1], sems, base + 2, up),
            remote(src[0], own[0], sems, base + 3, down),
            remote(behind[0], behind[0], sems, base + 4, up),
            remote(ahead[1], ahead[1], sems, base + 5, down),
        ]

    def start(self):
        for copy in self.copies[:4]:
            copy.start()

    def forward(self):
        for i in range(2):
            self.copies[i].wait_recv()
            self.copies[4 + i].start()

    def behind(self):
        self.copies[2].wait_recv()

    def ahead(self):
        self.copies[3].wait_recv()

    def far(self):
        for copy in self.copies[4:]:
            copy.wait_recv()

    def drain(self):
        for copy in self.copies:
            copy.wait_send()


class RingReduce:
    COPIES = 6

    @staticmethod
    def scratch(n, m):
        return [pltpu.VMEM((2, n // 2, m), BF16), pltpu.VMEM((2, n, m), BF16)]

    def __init__(self, block, axis, part, full, sems, base):
        up, down = {axis: 1}, {axis: 3}
        one, two, three = halves(block(1)), halves(block(2)), halves(block(3))
        from_behind, from_ahead = halves(full.at[0]), halves(full.at[1])
        self.adds = ((one[0], part.at[0]), (three[1], part.at[1]))
        self.terms = (block(0), full.at[0], full.at[1])
        self.copies = [
            remote(two[0], part.at[0], sems, base, up),
            remote(two[1], part.at[1], sems, base + 1, down),
            remote(one[1], from_behind[1], sems, base + 2, up),
            remote(three[0], from_ahead[0], sems, base + 3, down),
            remote(one[0], from_behind[0], sems, base + 4, up),
            remote(three[1], from_ahead[1], sems, base + 5, down),
        ]

    def start(self):
        for copy in self.copies[:4]:
            copy.start()

    def forward(self):
        for i in range(2):
            self.copies[i].wait_recv()
            add_into(self.adds[i][0], *self.adds[i])
            self.copies[4 + i].start()

    def arrive(self):
        for copy in self.copies[2:]:
            copy.wait_recv()

    def drain(self):
        for copy in self.copies:
            copy.wait_send()


class GatherTensor:
    COPIES = 17

    def __init__(self, buf, ssem, rsem):
        yh, x, c, yl, z = place()
        self.yl, self.z = yl, z
        sems = (ssem, rsem)
        slot = lambda k, i: rows(buf, lax.rem(yl + k, 2) * 4 + lax.rem(z + i, 4))
        low = lambda ref: ref.at[:, pl.ds(0, CUT)]
        high = lambda ref: ref.at[:, pl.ds(CUT, WIDTH - CUT)]
        self.ring = RingGather(lambda i: slot(0, i), "dz", sems, 0)
        self.pair_ring = RingGather(lambda i: high(slot(1, i)), "dz", sems, 6)
        own = slot(0, 0)
        pair = dict(dyl=1)
        self.high = remote(high(own), high(own), sems, 12, pair)
        self.low = [
            remote(low(slot(0, i)), low(slot(0, i)), sems, 13 + i, pair) for i in range(4)
        ]

    def start(self):
        self.high.start()
        self.ring.start()
        self.low[0].start()

    def run(self, process, spare=None):
        yl, z = self.yl, self.z

        @pl.loop(0, 2)
        def _(k):
            @pl.when(k == 1)
            def _():
                self.ring.forward()
                self.high.wait_recv()
                self.pair_ring.start()
                self.low[0].wait_recv()

            process(lax.rem(yl + k, 2) * 4 + z)

        if spare is not None:
            spare(0)

        @pl.loop(0, 6)
        def _(j):
            @pl.when(j == 0)
            def _():
                self.ring.behind()
                self.low[3].start()
                self.ring.ahead()
                self.low[1].start()

            @pl.when(j == 2)
            def _():
                self.ring.far()
                self.low[2].start()
                self.pair_ring.forward()

            @pl.when(j == 3)
            def _():
                if spare is not None:
                    spare(1)
                self.pair_ring.behind()
                self.low[3].wait_recv()

            @pl.when(j == 4)
            def _():
                self.pair_ring.ahead()
                self.low[1].wait_recv()

            @pl.when(j == 5)
            def _():
                self.pair_ring.far()
                self.low[2].wait_recv()

            i = lax.rem(j, 3)
            step = (3 * i * i - 7 * i + 6) // 2
            process(lax.rem(yl + j // 3, 2) * 4 + lax.rem(z + step, 4))

        self.ring.drain()
        self.pair_ring.drain()
        for copy in [self.high] + self.low:
            copy.wait_send()


class ScatterTensor:
    COPIES = 23

    @staticmethod
    def scratch():
        return (
            [pltpu.VMEM((4, 128, CUT), BF16), pltpu.VMEM((128, WIDTH - CUT), BF16)]
            + RingReduce.scratch(128, CUT)
            + RingReduce.scratch(128, WIDTH - CUT) * 2
        )

    def __init__(self, part, bufs, ssem, rsem):
        yh, x, c, yl, z = place()
        self.yl = yl
        self.from_pair, self.last = bufs[0], bufs[1]
        sems = (ssem, rsem)
        slot = lambda k, i: rows(part, lax.rem(yl + k, 2) * 4 + lax.rem(z + i, 4))
        low = lambda k, i: slot(k, i).at[:, pl.ds(0, CUT)]
        high = lambda k, i: slot(k, i).at[:, pl.ds(CUT, WIDTH - CUT)]
        pair = dict(dyl=1)
        self.low = lambda i: low(0, i)
        self.low_ring = RingReduce(lambda i: low(0, i), "dz", bufs[2], bufs[3], sems, 0)
        self.pair_ring = RingReduce(lambda i: high(1, i), "dz", bufs[4], bufs[5], sems, 6)
        self.own_ring = RingReduce(lambda i: high(0, i), "dz", bufs[6], bufs[7], sems, 12)
        self.first = [remote(low(1, i), bufs[0].at[i], sems, 18 + i, pair) for i in range(4)]
        self.second = remote(high(1, 0), bufs[1], sems, 22, pair)

    def run(self, process):
        @pl.loop(0, 2)
        def _(k):
            process(lax.rem(self.yl + 1 + k, 2))

            @pl.when(k == 0)
            def _():
                for i in (2, 1, 3, 0):
                    self.first[i].start()
                self.pair_ring.start()

            @pl.when(k == 1)
            def _():
                self.own_ring.start()

    def add_first(self, i):
        self.first[i].wait_recv()
        add_into(self.low(i), self.low(i), self.from_pair.at[i])

    def middle(self):
        self.pair_ring.forward()
        for i in (2, 1, 3):
            self.add_first(i)
        self.low_ring.start()
        self.own_ring.forward()

    def later(self):
        self.pair_ring.arrive()
        add_into(self.pair_ring.terms[0], *self.pair_ring.terms)
        self.second.start()
        self.low_ring.forward()
        self.add_first(0)

    def finish(self, out):
        self.own_ring.arrive()
        self.second.wait_recv()
        add_into(out.at[:, pl.ds(CUT, WIDTH - CUT)], *self.own_ring.terms, self.last)
        self.low_ring.arrive()
        add_into(out.at[:, pl.ds(0, CUT)], *self.low_ring.terms)
        for ring in (self.low_ring, self.pair_ring, self.own_ring):
            ring.drain()
        for copy in self.first + [self.second]:
            copy.wait_send()


def block_of(ref, kind, slot):
    if kind == "row":
        size = ref.shape[0] // 16
        return ref.at[pl.ds(pl.multiple_of(slot * size, size), size)]
    size = ref.shape[1] // 16
    return ref.at[:, pl.ds(pl.multiple_of(slot * size, size), size)]


class GatherDp:
    COPIES = 21

    def __init__(self, shard, out, kind, ssem, rsem, lsem, pair=None):
        yh, x, c, yl, z = place()
        sems = (ssem, rsem)
        self.pair = pair
        block = lambda k, i: block_of(
            out, kind, lax.rem(yh + k, 2) * 8 + lax.rem(x + i, 4) * 2 + c
        )
        self.local = [pltpu.make_async_copy(shard, block(0, 0), lsem.at[0])]
        if pair is not None:
            self.local.append(pltpu.make_async_copy(pair, block(1, 0), lsem.at[1]))
        self.ring = RingGather(lambda i: block(0, i), "dx", sems, 0, shard)
        self.far_ring = RingGather(lambda i: block(1, i), "dx", sems, 6, pair)
        if pair is None:
            self.own_y = remote(shard, block(0, 0), sems, 12, dict(dyh=1))
        core = dict(dc=1)
        self.core = [remote(shard, block(0, 0), sems, 13, core)]
        for n in range(1, 8):
            ref = block(n // 4, n % 4)
            source = pair if n == 4 and pair is not None else ref
            self.core.append(remote(source, ref, sems, 13 + n, core))

    def start(self):
        if self.pair is None:
            self.own_y.start()
        self.ring.start()
        self.core[0].start()
        for copy in self.local:
            copy.start()
        if self.pair is not None:
            self.far_ring.start()
            self.core[4].start()

    def forward(self):
        self.ring.forward()

    def forward_y(self):
        self.own_y.wait_recv()
        self.far_ring.start()
        self.core[4].start()

    def share(self):
        self.ring.behind()
        self.core[3].start()
        self.ring.ahead()
        self.core[1].start()
        self.ring.far()
        self.core[2].start()

    def forward_far(self):
        self.far_ring.forward()

    def share_far(self):
        self.far_ring.behind()
        self.core[7].start()
        self.far_ring.ahead()
        self.core[5].start()
        self.far_ring.far()
        self.core[6].start()

    def finish(self):
        for copy in self.core:
            copy.wait_recv()
        for copy in self.local:
            copy.wait()
        self.ring.drain()
        self.far_ring.drain()
        for copy in self.core if self.pair is not None else [self.own_y] + self.core:
            copy.wait_send()


class ScatterDp:
    COPIES = 21

    @staticmethod
    def scratch(block):
        return (
            [pltpu.VMEM((8,) + block, BF16), pltpu.VMEM(block, BF16)]
            + RingReduce.scratch(*block) * 2
            + [DMA((21,)), DMA((21,))]
        )

    def __init__(self, part, kind, from_core, from_y, h0, f0, h1, f1, ssem, rsem):
        yh, x, c, yl, z = place()
        sems = (ssem, rsem)
        self.from_core, self.from_y = from_core, from_y
        block = lambda k, i, d: block_of(
            part, kind, lax.rem(yh + k, 2) * 8 + lax.rem(x + i, 4) * 2 + d
        )
        self.block = lambda k, i: block(k, i, c)
        self.core = [
            remote(block(n // 4, n % 4, 1 - c), from_core.at[n], sems, n, dict(dc=1))
            for n in range(8)
        ]
        self.ring = RingReduce(lambda i: block(0, i, c), "dx", h0, f0, sems, 8)
        self.far_ring = RingReduce(lambda i: block(1, i, c), "dx", h1, f1, sems, 14)
        self.last = remote(block(1, 0, c), from_y, sems, 20, dict(dyh=1))

    def start(self):
        for n in (6, 5, 7, 4, 2, 1, 3, 0):
            self.core[n].start()

    def add_core(self, n):
        self.core[n].wait_recv()
        ref = self.block(n // 4, n % 4)
        add_into(ref, ref, self.from_core.at[n])

    def along_x(self):
        for n in (6, 5, 7):
            self.add_core(n)
        self.far_ring.start()
        for n in (2, 1, 3):
            self.add_core(n)
        self.ring.start()
        for n in (4, 0):
            self.add_core(n)

    def forward(self):
        self.far_ring.forward()
        self.ring.forward()

    def along_y(self):
        self.far_ring.arrive()
        add_into(self.far_ring.terms[0], *self.far_ring.terms)
        self.last.start()

    def finish(self, out):
        self.ring.arrive()
        self.last.wait_recv()
        add_into(out, *self.ring.terms, self.from_y)
        self.ring.drain()
        self.far_ring.drain()
        for copy in self.core + [self.last]:
            copy.wait_send()


def params(cid):
    return pltpu.CompilerParams(
        collective_id=cid, has_side_effects=True, vmem_limit_bytes=63 << 20
    )


def nn(a, b):
    return jnp.dot(a, b, preferred_element_type=F32)


def nt(a, b):
    return lax.dot_general(a, b, (((1,), (1,)), ((), ())), preferred_element_type=F32)


def tn(a, b):
    return lax.dot_general(a, b, (((0,), (0,)), ((), ())), preferred_element_type=F32)


def tiles(count, size):
    def run(body):
        @pl.loop(0, count // size)
        def _(i):
            body(pl.ds(pl.multiple_of(i * size, size), size))

    return run


def rope_tables():
    frequency = THETA ** (-(np.arange(64, dtype=np.float32) * np.float32(2.0) / np.float32(HEAD_DIM)))
    angles = np.arange(1024, dtype=np.float32)[:, None] * frequency.astype(np.float32)[None, :]
    cosine, sine = np.cos(angles), np.sin(angles)
    return (
        np.concatenate([cosine, cosine], 1).astype(np.float32),
        np.concatenate([-sine, sine], 1).astype(np.float32),
    )


class Exchange:
    PEERS = tuple(dict(dz=a, dyl=b) for b in range(2) for a in range(4) if a or b)

    def __init__(self, buf, ssem, rsem):
        yh, x, c, yl, z = place()
        self.buf = buf
        self.mine = buf.at[yl * 4 + z]
        self.copies = [
            remote(self.mine, self.mine, (ssem, rsem), i, peer)
            for i, peer in enumerate(self.PEERS)
        ]

    def start(self):
        for copy in self.copies:
            copy.start()

    def finish(self):
        for copy in self.copies:
            copy.wait_recv()
        for copy in self.copies:
            copy.wait_send()

    def sum(self):
        total = self.buf[0]
        for i in range(1, 8):
            total += self.buf[i]
        return total


def row_sums(values):
    return nt(jnp.ones((8, values.shape[1]), F32), values)


def spread(pair):
    row = lax.broadcasted_iota(jnp.int32, (8, 256), 0)
    column = lax.broadcasted_iota(jnp.int32, (8, 256), 1)
    pick = jnp.where(row == column // 128 * 4, 1.0, 0.0)
    return lax.dot_general(
        pair, pick, (((0,), (0,)), ((), ())), precision=lax.Precision.HIGHEST, preferred_element_type=F32
    )


def both(a, b):
    return jnp.where(lax.broadcasted_iota(jnp.int32, a.shape, 0) < 4, a, b)


ALL_PEERS = Exchange.PEERS + DP_PEERS
SCALE = HEAD_DIM**-0.5


def diagonal_mask(scores, first, length):
    row = lax.broadcasted_iota(jnp.int32, scores.shape, 0)
    column = lax.broadcasted_iota(jnp.int32, scores.shape, 1)
    return jnp.where((column <= row) & (column + first < length), scores, -1e30)


def attention_forward(tokens, lengths, weights, q_gain, k_gain, tables):
    full = [(2048, 256)] * 3 + [(256, 2048), (2048, 1024), (2048, 1024), (1024, 128)]
    kinds = ("row", "row", "row", "col", "row", "row", "col")

    def attention_step(
        tokens, w0, w1, w2, w3, w4, w5, w6, lengths, q_gain_all, k_gain_all, cosine, sine,
        x_out, f0, f1, f2, f3, f4, f5, f6, q_raw_out, k_raw_out, q_rot_out, k_rot_out, v_out,
        mixed_out, lse_out, scale_out, branch,
        x, wq, wk, wv, wo, q_raw, k_raw, q_rot, k_rot, v_low, mixed, lse, scales, part, sums,
        *rest,
    ):
        bufs, (ssem, rsem, gsem, hsem, wsem, vsem, esem, fsem, lsem, msem) = rest[:8], rest[8:]
        yh, xx, c, yl, z = place()
        own_columns = pl.ds(pl.multiple_of((yl * 4 + z) * 256, 256), 256)
        q_gain, k_gain = q_gain_all[:, own_columns], k_gain_all[:, own_columns]
        length = lengths[0]
        first = pltpu.make_async_copy(tokens, rows(x, yl * 4 + z), msem)
        first.start()
        greet(ALL_PEERS)
        gather = GatherTensor(x, gsem, hsem)
        shards = (w0, w1, w2, w3, w4, w5, w6)
        wholes = (wq, wk, wv, wo, f4, f5, f6)
        items = [
            GatherDp(shards[i], wholes[i], kinds[i], wsem.at[i], vsem.at[i], lsem.at[pl.ds(i, 1)])
            for i in range(6)
        ]
        down_pair = remote(w6, f6, (wsem.at[6], vsem.at[6]), 0, dict(dyh=1))
        small, large = items[:4], items[4:]
        for item in small:
            item.start()
        first.wait()
        gather.start()

        def spread_weights(stage):
            for item in small:
                if stage == 0:
                    item.forward()
                    item.forward_y()
                else:
                    item.share()
                    item.forward_far()

        gather.run(lambda slot: None, spread_weights)
        for item in small:
            item.share_far()
        for item in large:
            item.start()
        for item in small:
            item.finish()
        saves = []

        def save(source, target):
            copy = pltpu.make_async_copy(source, target, lsem.at[7 + len(saves)])
            copy.start()
            saves.append(copy)

        save(x, x_out)
        for source, target in ((wq, f0), (wk, f1), (wv, f2), (wo, f3)):
            save(source, target)

        @tiles(1024, 256)
        def _(r):
            xt = x[r, :]
            q = nn(xt, wq[...])
            k = nn(xt, wk[...])
            q_raw[r, :] = q
            k_raw[r, :] = k
            v_low[r, :] = nn(xt, wv[...]).astype(BF16)
            sums[yl * 4 + z, :, r] = both(row_sums(q * q), row_sums(k * k))

        exchange = Exchange(sums, esem, fsem)
        exchange.start()
        save(q_raw, q_raw_out)
        save(k_raw, k_raw_out)
        save(v_low, v_out)
        exchange.finish()
        down_pair.start()
        for item in large:
            item.forward()
            item.forward_y()
        scales[...] = spread(lax.rsqrt(exchange.sum() * (1.0 / 2048) + EPS))
        save(scales, scale_out)

        @tiles(1024, 256)
        def _(r):
            cos, sin = cosine[r, :], sine[r, :]
            for source, gain, s, target, factor in (
                (q_raw, q_gain, 0, q_rot, SCALE),
                (k_raw, k_gain, 128, k_rot, 1.0),
            ):
                scale = scales[r, s : s + 128]
                for h in (0, 128):
                    v = source[r, h : h + 128] * scale * gain[:, h : h + 128]
                    v = v * cos + pltpu.roll(v, 64, 1) * sin
                    target[r, h : h + 128] = (v * factor).astype(BF16)

        save(q_rot, q_rot_out)
        save(k_rot, k_rot_out)

        for h in (0, 128):
            cols = slice(h, h + 128)
            for i in range(4):
                low = i * 256
                block = slice(low, low + 256)
                q = q_rot[block, cols]
                s1 = diagonal_mask(nt(q, k_rot[block, cols]), low, length)
                peak = jnp.max(s1, 1, keepdims=True)
                if i:
                    s0 = nt(q, k_rot[0:low, cols])
                    peak = jnp.maximum(peak, jnp.max(s0, 1, keepdims=True))
                e1 = jnp.exp(s1 - peak)
                total = jnp.sum(e1, 1, keepdims=True)
                out = nn(e1.astype(BF16), v_low[block, cols])
                if i:
                    e0 = jnp.exp(s0 - peak)
                    total += jnp.sum(e0, 1, keepdims=True)
                    out += nn(e0.astype(BF16), v_low[0:low, cols])
                mixed[block, cols] = (out / total).astype(BF16)
                lse[block, cols] = jnp.broadcast_to(peak + jnp.log(total), (256, 128))

        save(mixed, mixed_out)
        save(lse, lse_out)
        scatter = ScatterTensor(part, bufs, ssem, rsem)

        def project(half):
            s = pl.ds(pl.multiple_of(half * 512, 512), 512)
            m = mixed[s, :]

            @tiles(2048, 512)
            def _(n):
                part[s, n] = nn(m, wo[:, n]).astype(BF16)

        scatter.run(project)
        for item in large:
            item.share()
        scatter.middle()
        for item in large:
            item.forward_far()
        scatter.later()
        for item in large:
            item.share_far()
        scatter.finish(branch)
        for item in large:
            item.finish()
        down_pair.wait()
        for copy in saves:
            copy.wait()

    S = jax.ShapeDtypeStruct
    acts = [((1024, 256), F32), ((1024, 256), F32)] + [((1024, 256), BF16)] * 4
    acts += [((1024, 256), F32)] * 2
    outs = [S((1024, 2048), BF16)] + [S(f, BF16) for f in full] + [S(*a) for a in acts]
    outs.append(S((128, 2048), F32))
    D = DMA
    return pl.pallas_call(
        attention_step,
        out_shape=outs,
        in_specs=[ANY] * 8 + [SMEM] + [VM] * 4,
        out_specs=[ANY] * 16 + [VM],
        scratch_shapes=[pltpu.VMEM((1024, 2048), BF16)]
        + [pltpu.VMEM(f, BF16) for f in full[:4]]
        + [pltpu.VMEM(*a) for a in acts]
        + [pltpu.VMEM((1024, 2048), BF16), pltpu.VMEM((8, 8, 1024), F32)]
        + ScatterTensor.scratch()
        + [D((23,)), D((23,)), D((17,)), D((17,)), D((7, 21)), D((7, 21)), D((7,)), D((7,)), D((24,)), D],
        compiler_params=params(1),
        name="attention_step",
    )(tokens, *weights, lengths, q_gain, k_gain, *tables)


def mlp(tokens, lengths, branch, cotangent, attn_gain, mlp_gain, weights, w_down):
    def mlp_step(
        lengths, tokens, branch, cotangent, attn_gain, mlp_gain, wg_in, wu_in, wd_pair, wd_in,
        act, d_res, d_branch, attn_part, mlp_part, wg_out, wu_out, wd_out,
        x, dd, wg, wu, wd, gate_factor, silu, inner, dg, du, part, residual, total,
        *rest,
    ):
        bufs, (ssem, rsem, gsem, hsem, esem, fsem, tsem, usem, wsem, vsem, lsem) = rest[:8], rest[8:]
        yh, xx, c, yl, z = place()
        me = yl * 4 + z
        length = lengths[0]
        loads = [
            pltpu.make_async_copy(source, target, lsem.at[i])
            for i, (source, target) in enumerate(((wg_in, wg), (wu_in, wu)))
        ]
        for copy in loads:
            copy.start()
        greet(TENSOR_PEERS + DP_PEERS[:3:2] + DP_PEERS[4:])
        item = GatherDp(wd_in, wd, "col", wsem, vsem, lsem.at[pl.ds(2, 2)], wd_pair)
        item.start()
        own = rows(x, me)

        @tiles(128, 16)
        def _(r):
            b = branch[r, :]
            scale = lax.rsqrt(jnp.mean(b * b, 1, keepdims=True) + EPS)
            value = tokens[r, :].astype(F32) + b * scale * attn_gain[...]
            residual[r, :] = value
            own[r, :] = value.astype(BF16)

        gather = GatherTensor(x, gsem, hsem)
        gather.start()
        for copy in loads:
            copy.wait()

        def gate_up(slot):
            s = pl.ds(pl.multiple_of(slot * 128, 128), 128)
            xt = x[s, :]

            @tiles(1024, 512)
            def _(n):
                gate = nn(xt, wg[:, n])
                up = nn(xt, wu[:, n])
                sigmoid = jax.nn.sigmoid(gate)
                low = gate * sigmoid
                silu[s, n] = low.astype(BF16)
                gate_factor[s, n] = (up * (sigmoid + low * (1.0 - sigmoid))).astype(BF16)
                inner[s, n] = (low * up).astype(BF16)

        def spread_down(stage):
            if stage == 0:
                item.forward()
                item.forward_far()
            else:
                item.share()
                item.share_far()

        gather.run(gate_up, spread_down)
        item.finish()

        def down(half):
            s = pl.ds(pl.multiple_of(half * 512, 512), 512)
            it = inner[s, :]

            @tiles(2048, 512)
            def _(n):
                part[s, n] = nn(it, wd[:, n]).astype(BF16)

        scatter = ScatterTensor(part, bufs, ssem, rsem)
        scatter.run(down)
        scatter.middle()
        scatter.later()
        scatter.finish(total)
        mlp_part[...] = jnp.zeros_like(mlp_part)
        attn_part[...] = jnp.zeros_like(attn_part)
        own_d = rows(dd, me)

        @tiles(128, 16)
        def _(r):
            v = total[r, :]
            position = lax.broadcasted_iota(jnp.int32, (16, 1), 0) + (me * 128 + r.start)
            ok = position < length
            scale = lax.rsqrt(jnp.mean(v * v, 1, keepdims=True) + EPS)
            normal = v * scale
            act[r, :] = jnp.where(ok, residual[r, :] + normal * mlp_gain[...], 0.0).astype(BF16)
            grad = jnp.where(ok, cotangent[r, :].astype(F32), 0.0)
            d_res[r, :] = grad
            mlp_part[...] += jnp.sum(grad * normal, 0, keepdims=True)
            weighted = mlp_gain[...] * grad
            mean = jnp.mean(v * weighted, 1, keepdims=True)
            own_d[r, :] = (scale * weighted - v * (scale * scale * scale * mean)).astype(BF16)

        gather = GatherTensor(dd, esem, fsem)
        gather.start()

        def d_inner(slot):
            s = pl.ds(pl.multiple_of(slot * 128, 128), 128)
            dt = dd[s, :]

            @tiles(1024, 512)
            def _(n):
                d = nt(dt, wd[n, :])
                dg[s, n] = (d * gate_factor[s, n].astype(F32)).astype(BF16)
                du[s, n] = (d * silu[s, n].astype(F32)).astype(BF16)

        gather.run(d_inner)

        def d_input(half):
            s = pl.ds(pl.multiple_of(half * 512, 512), 512)
            g, u = dg[s, :], du[s, :]

            @tiles(2048, 512)
            def _(n):
                part[s, n] = (nt(g, wg[n, :]) + nt(u, wu[n, :])).astype(BF16)

        scatter = ScatterTensor(part, bufs, tsem, usem)
        scatter.run(d_input)

        @tiles(1024, 512)
        def _(m):
            @tiles(2048, 1024)
            def _(n):
                wd[m, n] = tn(inner[:, m], dd[:, n]).astype(BF16)

        saves = [pltpu.make_async_copy(wd, wd_out, lsem.at[0])]
        saves[0].start()
        scatter.middle()

        @tiles(2048, 512)
        def _(m):
            wg[m, :] = tn(x[:, m], dg[...]).astype(BF16)

        saves.append(pltpu.make_async_copy(wg, wg_out, lsem.at[1]))
        saves[1].start()
        scatter.later()

        @tiles(2048, 512)
        def _(m):
            wu[m, :] = tn(x[:, m], du[...]).astype(BF16)

        saves.append(pltpu.make_async_copy(wu, wu_out, lsem.at[2]))
        saves[2].start()
        scatter.finish(total)

        @tiles(128, 16)
        def _(r):
            grad = d_res[r, :] + total[r, :]
            d_res[r, :] = grad
            b = branch[r, :]
            scale = lax.rsqrt(jnp.mean(b * b, 1, keepdims=True) + EPS)
            attn_part[...] += jnp.sum(grad * b * scale, 0, keepdims=True)
            weighted = attn_gain[...] * grad
            mean = jnp.mean(b * weighted, 1, keepdims=True)
            d_branch[r, :] = (scale * weighted - b * (scale * scale * scale * mean)).astype(BF16)

        for copy in saves:
            copy.wait()

    S = jax.ShapeDtypeStruct
    D = DMA
    W = pltpu.VMEM
    return pl.pallas_call(
        mlp_step,
        out_shape=[
            S((128, 2048), BF16),
            S((128, 2048), F32),
            S((128, 2048), BF16),
            S((1, 2048), F32),
            S((1, 2048), F32),
            S((2048, 1024), BF16),
            S((2048, 1024), BF16),
            S((1024, 2048), BF16),
        ],
        in_specs=[SMEM] + [VM] * 5 + [ANY] * 4,
        out_specs=[VM] * 5 + [ANY] * 3,
        scratch_shapes=[W((1024, 2048), BF16)] * 2
        + [W((2048, 1024), BF16)] * 2
        + [W((1024, 2048), BF16)]
        + [W((1024, 1024), BF16)] * 5
        + [W((1024, 2048), BF16)]
        + [W((128, 2048), F32)] * 2
        + ScatterTensor.scratch()
        + [D((23,))] * 2
        + [D((17,))] * 4
        + [D((23,))] * 2
        + [D((21,))] * 2
        + [D((4,))],
        compiler_params=params(2),
        name="mlp_step",
    )(lengths, tokens, branch, cotangent, attn_gain, mlp_gain, *weights, w_down)


class SumAll:
    def __init__(self, slots, hold, boxes, ssem, rsem):
        self.exchange = Exchange(slots, ssem, rsem)
        self.hold, self.boxes = hold, boxes
        self.copies = []
        for i, peer in enumerate(DP_PEERS):
            k = (1, 1, 1, 2, 0)[i]
            self.copies.append(remote(hold.at[k], boxes.at[i], (ssem, rsem), 7 + i, peer))

    def start(self):
        self.exchange.start()

    def core(self):
        self.exchange.finish()
        self.hold[0] = self.exchange.sum()
        self.copies[4].start()

    def along_x(self):
        self.copies[4].wait()
        self.hold[1] = self.hold[0] + self.boxes[4]
        for copy in self.copies[:3]:
            copy.start()

    def along_y(self):
        for copy in self.copies[:3]:
            copy.wait()
        self.hold[2] = self.hold[1] + self.boxes[0] + self.boxes[1] + self.boxes[2]
        self.copies[3].start()

    def finish(self, out):
        self.copies[3].wait()
        out[...] = self.hold[2] + self.boxes[3]


def attention_backward(lengths, own, d_res, x, weights, saved, q_gain, k_gain, parts, tables, grads):
    kinds = ("row", "row", "row", "col", "row", "row", "col")
    blocks = ((128, 256),) * 3 + ((256, 128), (128, 1024), (128, 1024), (1024, 128))

    def backward_step(
        lengths, own, d_res, q_gain_all, k_gain_all, attn_part, mlp_part, cosine, sine, x_in, w0, w1, w2, w3,
        q_raw_in, k_raw_in, q_rot_in, k_rot_in, v_in, mixed_in, lse_in, scale_in, g4, g5, g6,
        input_grad, o0, o1, o2, o3, o4, o5, o6, gain_sums,
        x, wq, wk, wv, wo, q_raw, k_raw, q_rot, k_rot, v_low, mixed, lse, scales,
        p4, p5, p6, do, dq, dk, dv, dqr, dkr, dvr, part, sums, gain_slots, gain_hold, gain_boxes,
        *rest,
    ):
        bufs, (ssem, rsem), rest = rest[:8], rest[8:10], rest[10:]
        dp_bufs, rest = [rest[8 * i : 8 * i + 8] for i in range(7)], rest[56:]
        gsem, hsem, esem, fsem, isem, jsem, lsem = rest
        yh, xx, c, yl, z = place()
        me = yl * 4 + z
        own_columns = pl.ds(pl.multiple_of(me * 256, 256), 256)
        q_gain, k_gain = q_gain_all[:, own_columns], k_gain_all[:, own_columns]
        length = lengths[0]
        first = pltpu.make_async_copy(own, rows(x, me), lsem.at[0])
        first.start()
        pairs = ((g4, p4), (g5, p5), (g6, p6), (w3, wo), (mixed_in, mixed), (q_rot_in, q_rot))
        pairs += ((k_rot_in, k_rot), (v_in, v_low), (lse_in, lse), (q_raw_in, q_raw))
        pairs += ((k_raw_in, k_raw), (scale_in, scales), (w0, wq), (w1, wk), (w2, wv))
        loads = [pltpu.make_async_copy(s, t, lsem.at[1 + i]) for i, (s, t) in enumerate(pairs)]
        for copy in loads:
            copy.start()
        greet(ALL_PEERS)
        first.wait()
        gather = GatherTensor(x, gsem, hsem)
        gather.start()
        for copy in loads[:3]:
            copy.wait()
        wholes = (wq, wk, wv, wo, p4, p5, p6)
        items = [ScatterDp(wholes[i], kinds[i], *dp_bufs[i]) for i in range(7)]
        small, large = items[:4], items[4:]
        for item in large:
            item.start()
        loads[3].wait()

        def d_mixed(slot):
            s = pl.ds(pl.multiple_of(slot * 128, 128), 128)
            do[s, :] = nt(x[s, :], wo[...]).astype(BF16)

        def along_x(stage):
            if stage == 0:
                for item in large:
                    item.along_x()

        gather.run(d_mixed, along_x)
        for copy in loads[4:]:
            copy.wait()

        @tiles(2048, 512)
        def _(n):
            wo[:, n] = tn(mixed[...], x[:, n]).astype(BF16)

        reload = pltpu.make_async_copy(x_in, x, lsem.at[0])
        reload.start()

        for h in (0, 128):
            cols = slice(h, h + 128)
            for i in range(4):
                low = i * 256
                block = slice(low, low + 256)
                q, d = q_rot[block, cols], do[block, cols]
                top = lse[block, h : h + 1]
                k1, v1 = k_rot[block, cols], v_low[block, cols]
                p1 = jnp.exp(diagonal_mask(nt(q, k1), low, length) - top)
                dp1 = nt(d, v1)
                delta = jnp.sum(p1 * dp1, 1, keepdims=True)
                if i:
                    k0, v0 = k_rot[0:low, cols], v_low[0:low, cols]
                    p0 = jnp.exp(nt(q, k0) - top)
                    dp0 = nt(d, v0)
                    delta += jnp.sum(p0 * dp0, 1, keepdims=True)
                ds1 = (p1 * (dp1 - delta)).astype(BF16)
                dq_block = nn(ds1, k1)
                dk[block, cols] = tn(ds1, q)
                dv[block, cols] = tn(p1.astype(BF16), d)
                if i:
                    ds0 = (p0 * (dp0 - delta)).astype(BF16)
                    dq_block += nn(ds0, k0)
                    dk[0:low, cols] += tn(ds0, q)
                    dv[0:low, cols] += tn(p0.astype(BF16), d)
                dq[block, cols] = dq_block

        q_total, k_total = [], []
        for i in range(4):
            r = slice(i * 256, i * 256 + 256)
            cos, sin = cosine[r, :], sine[r, :]
            for source, raw, gain, s, factor, totals in (
                (dq, q_raw, q_gain, 0, SCALE, q_total),
                (dk, k_raw, k_gain, 128, 1.0, k_total),
            ):
                scale = scales[r, s : s + 128]
                part_sums = []
                for h in (0, 128):
                    v = source[r, h : h + 128] * factor
                    v = v * cos - pltpu.roll(v, 64, 1) * sin
                    w = v * raw[r, h : h + 128]
                    part_sums.append(jnp.sum(w * scale, 0, keepdims=True))
                    source[r, h : h + 128] = v * gain[:, h : h + 128]
                totals.append(jnp.concatenate(part_sums, 1))
            sums[me, :, r] = both(
                row_sums(dq[r, :] * q_raw[r, :]), row_sums(dk[r, :] * k_raw[r, :])
            )
            dvr[r, :] = dv[r, :].astype(BF16)
        exchange = Exchange(sums, esem, fsem)
        exchange.start()
        row = lax.broadcasted_iota(jnp.int32, (8, 1024), 0)
        column = lax.broadcasted_iota(jnp.int32, (8, 1024), 1)
        message = jnp.zeros((8, 1024), F32)
        for k, line in enumerate((attn_part, attn_part, mlp_part, mlp_part)):
            line = line[:, 1024 * (k % 2) : 1024 * (k % 2) + 1024]
            message = jnp.where(row == 4 + k, line, message)
        for first_row, totals in ((0, q_total), (2, k_total)):
            line = jnp.concatenate([totals[0] + totals[1] + totals[2] + totals[3]] * 4, 1)
            message += jnp.where((row == first_row + yl) & (column // 256 == z), line, 0.0)
        gain_slots[me] = message
        total_gain = SumAll(gain_slots, gain_hold, gain_boxes, isem, jsem)
        total_gain.start()
        for item in large:
            item.forward()
        exchange.finish()
        means = spread(exchange.sum() * (1.0 / 2048))
        for i in range(4):
            r = slice(i * 256, i * 256 + 256)
            for source, raw, s, target in ((dq, q_raw, 0, dqr), (dk, k_raw, 128, dkr)):
                scale = scales[r, s : s + 128]
                factor = scale * scale * scale * means[r, s : s + 128]
                for h in (0, 128):
                    target[r, h : h + 128] = (
                        scale * source[r, h : h + 128] - raw[r, h : h + 128] * factor
                    ).astype(BF16)
        total_gain.core()

        def d_input(half):
            s = pl.ds(pl.multiple_of(half * 512, 512), 512)
            a, b, d = dqr[s, :], dkr[s, :], dvr[s, :]

            @tiles(2048, 512)
            def _(n):
                part[s, n] = (nt(a, wq[n, :]) + nt(b, wk[n, :]) + nt(d, wv[n, :])).astype(BF16)

        scatter = ScatterTensor(part, bufs, ssem, rsem)
        scatter.run(d_input)
        reload.wait()

        @tiles(2048, 512)
        def _(m):
            xt = x[:, m].T
            wq[m, :] = nn(xt, dqr[...]).astype(BF16)
            wk[m, :] = nn(xt, dkr[...]).astype(BF16)
            wv[m, :] = nn(xt, dvr[...]).astype(BF16)

        for item in small:
            item.start()
        total_gain.along_x()
        scatter.middle()
        for item in small:
            item.along_x()
        for item in large:
            item.along_y()
        scatter.later()
        total_gain.along_y()
        for item in small:
            item.forward()
        scatter.finish(input_grad)

        @tiles(128, 16)
        def _(r):
            input_grad[r, :] += d_res[r, :]

        for item, out in zip(large, (o4, o5, o6)):
            item.finish(out)
        for item in small:
            item.along_y()
        total_gain.finish(gain_sums)
        for item, out in zip(small, (o0, o1, o2, o3)):
            item.finish(out)

    S = jax.ShapeDtypeStruct
    D = DMA
    W = pltpu.VMEM
    acts = [((1024, 256), F32)] * 2 + [((1024, 256), BF16)] * 4 + [((1024, 256), F32)] * 2
    scratch = [W((1024, 2048), BF16)] + [W((2048, 256), BF16)] * 3 + [W((256, 2048), BF16)]
    scratch += [W(*a) for a in acts]
    scratch += [W((2048, 1024), BF16)] * 2 + [W((1024, 2048), BF16), W((1024, 256), BF16)]
    scratch += [W((1024, 256), F32)] * 3 + [W((1024, 256), BF16)] * 3 + [W((1024, 2048), BF16)]
    scratch += [W((8, 8, 1024), F32)] * 2 + [W((3, 8, 1024), F32), W((5, 8, 1024), F32)]
    scratch += ScatterTensor.scratch() + [D((23,))] * 2
    for b in blocks:
        scratch += ScatterDp.scratch(b)
    scratch += [D((17,)), D((17,)), D((7,)), D((7,)), D((12,)), D((12,)), D((16,))]
    return pl.pallas_call(
        backward_step,
        out_shape=[S((128, 2048), F32)] + [S(b, F32) for b in blocks] + [S((8, 1024), F32)],
        in_specs=[SMEM, ANY] + [VM] * 7 + [ANY] * 16,
        out_specs=[VM] * 9,
        scratch_shapes=scratch,
        compiler_params=params(3),
        name="backward_step",
    )(lengths, own, d_res, q_gain, k_gain, *parts, *tables, x, *weights, *saved, *grads)


def hand_over(*arrays):
    n = len(arrays)

    def hand_over_step(*refs):
        held, (lsem, ssem) = refs[2 * n : 3 * n], refs[3 * n :]
        loads = [pltpu.make_async_copy(refs[i], held[i], lsem.at[i]) for i in range(n)]
        stores = [pltpu.make_async_copy(held[i], refs[n + i], ssem.at[i]) for i in range(n)]
        for copy in loads:
            copy.start()
        for load, store in zip(loads, stores):
            load.wait()
            store.start()
        for copy in stores:
            copy.wait()

    return pl.pallas_call(
        hand_over_step,
        out_shape=[jax.ShapeDtypeStruct(a.shape, a.dtype) for a in arrays],
        in_specs=[ANY] * n,
        out_specs=[ANY] * n,
        scratch_shapes=[pltpu.VMEM(a.shape, a.dtype) for a in arrays] + [DMA((n,))] * 2,
        compiler_params=pltpu.CompilerParams(vmem_limit_bytes=63 << 20),
        name="hand_over_step",
    )(*arrays)


def local(
    tokens, lengths, w_query, w_key, w_value, w_out, w_gate, w_up, w_down,
    q_gain, k_gain, attn_gain, mlp_gain, cotangent,
):
    tables = rope_tables()
    weights = (w_query, w_key, w_value, w_out, w_gate, w_up, w_down)
    x, *res = attention_forward(tokens[0], lengths, weights, q_gain[None], k_gain[None], tables)
    weights, saved, branch = res[:7], res[7:15], res[15]
    act, d_res, d_branch, attn_part, mlp_part, *grads = mlp(
        tokens[0], lengths, branch, cotangent[0], attn_gain[None], mlp_gain[None], weights[4:], w_down
    )
    input_grad, *owned, sums = attention_backward(
        lengths,
        d_branch,
        d_res,
        x,
        weights[:4],
        saved,
        q_gain[None],
        k_gain[None],
        (attn_part, mlp_part),
        tables,
        grads,
    )
    act, input_grad, *owned = hand_over(act, input_grad, *owned)
    sums = sums.reshape(4, 2048)
    return (act[None], input_grad[None], *owned, sums[0], sums[1], sums[2], sums[3])


def solution(mesh):
    return jax.shard_map(
        local,
        mesh=mesh,
        in_specs=(
            P("dp", "tensor", None),
            P("dp"),
            P("dp", "tensor"),
            P("dp", "tensor"),
            P("dp", "tensor"),
            P("tensor", "dp"),
            P("dp", "tensor"),
            P("dp", "tensor"),
            P("tensor", "dp"),
            P(),
            P(),
            P(),
            P(),
            P("dp", "tensor", None),
        ),
        out_specs=(
            P("dp", "tensor", None),
            P("dp", "tensor", None),
            P("dp", "tensor"),
            P("dp", "tensor"),
            P("dp", "tensor"),
            P("tensor", "dp"),
            P("dp", "tensor"),
            P("dp", "tensor"),
            P("tensor", "dp"),
            P(),
            P(),
            P(),
            P(),
        ),
        check_vma=False,
    )
```

time: 1430 us -> 348 us (0.24)
  waiting for transfers between devices: 1060 us -> 0 us
  Pallas kernels: 0 us -> 342 us
  matrix products: 150 us -> 0 us
  blocking collectives: 103 us -> 0 us
  other arithmetic: 44 us -> 0 us
  local copies, waits for them, and re-layouts: 40.9 us -> 2.16 us
  between operations: 15.9 us -> 1.33 us
    all_gather x11 -> x0, waiting for transfers between devices: 445 us -> none  [the longest x1 53.9 us: local(): lax.all_gather(res_low, 'tensor', axis=1, tiled=True)]
    reduce_scatter x6 -> x0, waiting for transfers between devices: 408 us -> none  [the longest x1 91.1 us: local(): lax.psum_scatter(branch_part, 'tensor', scatter_dimension=1, tiled=True)]
    pallas_call x0 -> x4, Pallas kernels: none -> 342 us  [the longest x1 134 us: mlp(): pl.pallas_call(mlp_step, out_shape=[S((128, 2048), BF16), S((128, 2048),...]
    unnamed x27 -> x0, waiting for transfers between devices: 212 us -> none
    dot_general x27 -> x0, matrix products: 150 us -> none  [the longest x7 42 us: dot_first(): lax.dot_general(left, right, (((0,), (0,)), ((), ())), preferred_element_...]
    psum x3 -> x0, blocking collectives: 103 us -> none  [the longest x1 65.7 us: local(): lax.psum((q_gain_full, k_gain_full, attn_gain_part, mlp_gain_part), ('dp'...]
    unnamed x111 -> x1, local copies, waits for them, and re-layouts: 32.9 us -> 0.95 us
    convert_element_type x11 -> x0, other arithmetic: 18.7 us -> none  [the longest x4 5.09 us: local(): grads_owned = (lax.psum_scatter(w_query_part.astype(jnp.bfloat16), 'dp',...]
  transfers between devices with their start and end apart: 22 -> 0, of which waited for: 21 -> 0; matrix products, arithmetic and copies ran while one was open for 13% -> 0% of each run, Pallas kernels for 0% -> 0%
where the time goes in v2:
time: 348 us; the launch traced here: 345 us
  Pallas kernels  342 us (98%)
    pallas_call x1, Pallas kernels, mlp(): pl.pallas_call(mlp_step, out_shape=[S((128, 2048), BF16), S((128, 2048),...  134 us
    pallas_call x1, Pallas kernels, attention_backward(): pl.pallas_call(backward_step, out_shape=[S((128, 2048), F32)] + [S(b, F32...  109 us
    pallas_call x1, Pallas kernels, attention_forward(): pl.pallas_call(attention_step, out_shape=outs, in_specs=[ANY] * 8 + [SMEM...  95.8 us

profile of v2, /device:TPU:0, one launch (start us, length us, event | category | flops | bytes accessed | tf_op | source)
XLA Modules:
  0.0 345.3 jit_solution(877454279453051780)
XLA Ops:
  1.3 95.8 %attention_step.1 = (bf16[1024,2048]{1,0:T(8,128)(2,1)}, bf16[2048,256]{1,0:T(8,128)(2,1)}, bf16[2048,256]{1,0:T(8,128)(2,1)}, bf16[2048,256]{1,0:T(8,128)(2,1)}...) custom-call(bf16[128,2048]{1,0:T(8,128)(2,1)} %bitcast.24, ...), custom_call_target="tpu_custom_call" | custom-call | tf_op jit(solution)/shard_map/attention_step/pallas_call | solution.py:711
  97.1 133.9 %mlp_step.1 = (bf16[128,2048]{1,0:T(8,128)(2,1)}, f32[128,2048]{1,0:T(8,128)}, bf16[128,2048]{1,0:T(8,128)(2,1)}, f32[1,2048]{1,0:T(1,128)}, f32[1,2048]{1,0:T(1...) custom-call(s32[1]{0:T(128)S(6)} %copy.37.lengths, ...), custom_call_target="tpu_custom_call" | custom-call | tf_op jit(solution)/shard_map/mlp_step/pallas_call | solution.py:888
  231.0 108.9 %backward_step.1 = (f32[128,2048]{1,0:T(8,128)}, f32[128,256]{1,0:T(8,128)}, f32[128,256]{1,0:T(8,128)}, f32[128,256]{1,0:T(8,128)}, f32[256,128]{1,0:T(8,128)},...) custom-call(s32[1]{0:T(128)S(6)} %copy.37.lengths, ...), custom_call_target="tpu_custom_call" | custom-call | tf_op jit(solution)/shard_map/backward_step/pallas_call | solution.py:1149
  339.9 3.2 hand_over_step.1
  343.1 0.9 slice_bitcast_fusion
  344.1 0.6 copy_bitcast_fusion
  344.7 0.6 copy_bitcast_fusion.2

commit v3 on v2

v3 whole, which is shorter than its diff:
```python
import jax
import jax.numpy as jnp
import numpy as np
from jax import lax
from jax.experimental import pallas as pl
from jax.experimental.pallas import tpu as pltpu
from jax.sharding import PartitionSpec as P

HEAD_DIM = 128
EPS = 1e-06
THETA = 500000.0
MESH = pl.DeviceIdType.MESH
BF16 = jnp.bfloat16
F32 = jnp.float32
ANY = pl.BlockSpec(memory_space=pl.ANY)
VM = pl.BlockSpec(memory_space=pltpu.VMEM)
DMA = pltpu.SemaphoreType.DMA
CUT = 896
WIDTH = 2048


def place():
    d = lax.axis_index("dp")
    t = lax.axis_index("tensor")
    return d // 8, lax.rem(d // 2, 4), lax.rem(d, 2), t // 4, lax.rem(t, 4)


def other(dyh=0, dx=0, dc=0, dyl=0, dz=0):
    yh, x, c, yl, z = place()
    return (
        lax.rem(yh + dyh, 2) * 8 + lax.rem(x + dx, 4) * 2 + lax.rem(c + dc, 2),
        lax.rem(yl + dyl, 2) * 4 + lax.rem(z + dz, 4),
    )


TENSOR_PEERS = (dict(dz=1), dict(dz=3), dict(dyl=1))
DP_PEERS = (dict(dx=1), dict(dx=2), dict(dx=3), dict(dyh=1), dict(dc=1))
SMEM = pl.BlockSpec(memory_space=pltpu.SMEM)


def greet(peers):
    barrier = pltpu.get_barrier_semaphore()
    for peer in peers:
        pl.semaphore_signal(barrier, 1, device_id=other(**peer), device_id_type=MESH)
    pl.semaphore_wait(barrier, len(peers))


def remote(src, dst, sems, index, peer):
    ssem, rsem = sems
    return pltpu.make_async_remote_copy(
        src_ref=src,
        dst_ref=dst,
        send_sem=ssem.at[index],
        recv_sem=rsem.at[index],
        device_id=other(**peer),
        device_id_type=MESH,
    )


def rows(ref, slot):
    return ref.at[pl.ds(pl.multiple_of(slot * 128, 128), 128)]


def halves(ref):
    half = ref.shape[0] // 2
    return ref.at[pl.ds(0, half)], ref.at[pl.ds(half, half)]


def add_into(out, *terms):
    @pl.loop(0, out.shape[0] // 16)
    def _(i):
        r = pl.ds(pl.multiple_of(i * 16, 16), 16)
        if len(terms) == 2 and out.dtype == BF16:
            out[r, :] = terms[0][r, :] + terms[1][r, :]
        else:
            total = terms[0][r, :].astype(F32)
            for term in terms[1:]:
                total += term[r, :].astype(F32)
            out[r, :] = total.astype(out.dtype)


class RingGather:
    COPIES = 6

    def __init__(self, block, axis, sems, base, source=None):
        up, down = {axis: 1}, {axis: 3}
        src = halves(block(0) if source is None else source)
        own, behind, ahead = halves(block(0)), halves(block(3)), halves(block(1))
        self.copies = [
            remote(src[0], own[0], sems, base, up),
            remote(src[1], own[1], sems, base + 1, down),
            remote(src[1], own[1], sems, base + 2, up),
            remote(src[0], own[0], sems, base + 3, down),
            remote(behind[0], behind[0], sems, base + 4, up),
            remote(ahead[1], ahead[1], sems, base + 5, down),
        ]

    def start(self):
        for copy in self.copies[:4]:
            copy.start()

    def forward(self):
        for i in range(2):
            self.copies[i].wait_recv()
            self.copies[4 + i].start()

    def behind(self):
        self.copies[2].wait_recv()

    def ahead(self):
        self.copies[3].wait_recv()

    def far(self):
        for copy in self.copies[4:]:
            copy.wait_recv()

    def drain(self):
        for copy in self.copies:
            copy.wait_send()


class RingReduce:
    COPIES = 6

    @staticmethod
    def scratch(n, m):
        return [pltpu.VMEM((2, n // 2, m), BF16), pltpu.VMEM((2, n, m), BF16)]

    def __init__(self, block, axis, part, full, sems, base):
        up, down = {axis: 1}, {axis: 3}
        one, two, three = halves(block(1)), halves(block(2)), halves(block(3))
        from_behind, from_ahead = halves(full.at[0]), halves(full.at[1])
        self.adds = ((one[0], part.at[0]), (three[1], part.at[1]))
        self.terms = (block(0), full.at[0], full.at[1])
        self.copies = [
            remote(two[0], part.at[0], sems, base, up),
            remote(two[1], part.at[1], sems, base + 1, down),
            remote(one[1], from_behind[1], sems, base + 2, up),
            remote(three[0], from_ahead[0], sems, base + 3, down),
            remote(one[0], from_behind[0], sems, base + 4, up),
            remote(three[1], from_ahead[1], sems, base + 5, down),
        ]

    def start(self):
        for copy in self.copies[:4]:
            copy.start()

    def forward(self):
        for i in range(2):
            self.copies[i].wait_recv()
            add_into(self.adds[i][0], *self.adds[i])
            self.copies[4 + i].start()

    def arrive(self):
        for copy in self.copies[2:]:
            copy.wait_recv()

    def drain(self):
        for copy in self.copies:
            copy.wait_send()


class GatherTensor:
    COPIES = 21

    def __init__(self, buf, ssem, rsem, cut=CUT):
        yh, x, c, yl, z = place()
        self.yl, self.z = yl, z
        sems = (ssem, rsem)
        slot = lambda k, i: rows(buf, lax.rem(yl + k, 2) * 4 + lax.rem(z + i, 4))
        low = lambda ref: ref.at[:, pl.ds(0, cut)]
        high = lambda ref: ref.at[:, pl.ds(cut, WIDTH - cut)]
        self.ring = RingGather(lambda i: slot(0, i), "dz", sems, 0)
        self.pair_ring = RingGather(lambda i: high(slot(1, i)), "dz", sems, 6)
        own = slot(0, 0)
        pair = dict(dyl=1)
        self.high = remote(high(own), high(own), sems, 12, pair)
        self.low = []
        for n, i in enumerate((0, 3, 1, 2)):
            for half in halves(low(slot(0, i))):
                self.low.append(remote(half, half, sems, 13 + len(self.low), pair))

    def start(self):
        self.high.start()
        self.ring.start()
        self.low[0].start()
        self.low[1].start()

    def run(self, process, spare=None):
        yl, z = self.yl, self.z

        @pl.loop(0, 2)
        def _(k):
            @pl.when(k == 1)
            def _():
                self.ring.forward()
                self.low[2].start()
                self.low[5].start()
                self.high.wait_recv()
                self.pair_ring.start()
                self.ring.behind()
                self.low[3].start()
                self.ring.ahead()
                self.low[4].start()
                self.low[0].wait_recv()
                self.low[1].wait_recv()

            process(lax.rem(yl + k, 2) * 4 + z)

        if spare is not None:
            spare(0)

        @pl.loop(0, 6)
        def _(j):
            @pl.when(j == 2)
            def _():
                self.ring.far()
                self.low[6].start()
                self.low[7].start()
                self.pair_ring.forward()

            @pl.when(j == 3)
            def _():
                if spare is not None:
                    spare(1)
                self.pair_ring.behind()
                self.low[2].wait_recv()
                self.low[3].wait_recv()

            @pl.when(j == 4)
            def _():
                self.pair_ring.ahead()
                self.low[4].wait_recv()
                self.low[5].wait_recv()

            @pl.when(j == 5)
            def _():
                self.pair_ring.far()
                self.low[6].wait_recv()
                self.low[7].wait_recv()

            i = lax.rem(j, 3)
            step = (3 * i * i - 7 * i + 6) // 2
            process(lax.rem(yl + j // 3, 2) * 4 + lax.rem(z + step, 4))

        self.ring.drain()
        self.pair_ring.drain()
        for copy in [self.high] + self.low:
            copy.wait_send()


class ScatterTensor:
    COPIES = 23

    @staticmethod
    def scratch():
        return (
            [pltpu.VMEM((4, 128, CUT), BF16), pltpu.VMEM((128, WIDTH - CUT), BF16)]
            + RingReduce.scratch(128, CUT)
            + RingReduce.scratch(128, WIDTH - CUT) * 2
        )

    def __init__(self, part, bufs, ssem, rsem):
        yh, x, c, yl, z = place()
        self.yl = yl
        self.from_pair, self.last = bufs[0], bufs[1]
        sems = (ssem, rsem)
        slot = lambda k, i: rows(part, lax.rem(yl + k, 2) * 4 + lax.rem(z + i, 4))
        low = lambda k, i: slot(k, i).at[:, pl.ds(0, CUT)]
        high = lambda k, i: slot(k, i).at[:, pl.ds(CUT, WIDTH - CUT)]
        pair = dict(dyl=1)
        self.low = lambda i: low(0, i)
        self.low_ring = RingReduce(lambda i: low(0, i), "dz", bufs[2], bufs[3], sems, 0)
        self.pair_ring = RingReduce(lambda i: high(1, i), "dz", bufs[4], bufs[5], sems, 6)
        self.own_ring = RingReduce(lambda i: high(0, i), "dz", bufs[6], bufs[7], sems, 12)
        self.first = [remote(low(1, i), bufs[0].at[i], sems, 18 + i, pair) for i in range(4)]
        self.second = remote(high(1, 0), bufs[1], sems, 22, pair)

    def run(self, process):
        @pl.loop(0, 4)
        def _(k):
            process(lax.rem(self.yl + 1 + k // 2, 2), lax.rem((k + 1) // 2, 2))

            @pl.when(k == 0)
            def _():
                for i in (2, 1, 3, 0):
                    self.first[i].start()

            @pl.when(k == 1)
            def _():
                self.pair_ring.start()

    def add_first(self, i):
        self.first[i].wait_recv()
        add_into(self.low(i), self.low(i), self.from_pair.at[i])

    def step(self, n):
        low = self.low_ring.copies
        if n == 0:
            self.pair_ring.forward()
            self.own_ring.start()
            self.add_first(2)
            low[0].start()
            low[1].start()
        if n == 1:
            self.add_first(1)
            low[2].start()
            self.own_ring.forward()
        if n == 2:
            self.pair_ring.arrive()
            add_into(self.pair_ring.terms[0], *self.pair_ring.terms)
            self.second.start()
            self.add_first(3)
            low[3].start()
        if n == 3:
            self.low_ring.forward()
            self.add_first(0)

    def finish(self, out):
        self.own_ring.arrive()
        self.second.wait_recv()
        add_into(out.at[:, pl.ds(CUT, WIDTH - CUT)], *self.own_ring.terms, self.last)
        self.low_ring.arrive()
        add_into(out.at[:, pl.ds(0, CUT)], *self.low_ring.terms)
        for ring in (self.low_ring, self.pair_ring, self.own_ring):
            ring.drain()
        for copy in self.first + [self.second]:
            copy.wait_send()


def block_of(ref, kind, slot):
    if kind == "row":
        size = ref.shape[0] // 16
        return ref.at[pl.ds(pl.multiple_of(slot * size, size), size)]
    if kind == "folded":
        return ref.at[
            pl.ds(pl.multiple_of(lax.rem(slot, 8) * 128, 128), 128),
            pl.ds(pl.multiple_of(slot // 8 * 256, 256), 256),
        ]
    size = ref.shape[1] // 16
    return ref.at[:, pl.ds(pl.multiple_of(slot * size, size), size)]


class GatherDp:
    COPIES = 21

    def __init__(self, shard, out, kind, ssem, rsem, lsem):
        yh, x, c, yl, z = place()
        sems = (ssem, rsem)
        block = lambda k, i: block_of(
            out, kind, lax.rem(yh + k, 2) * 8 + lax.rem(x + i, 4) * 2 + c
        )
        self.local = pltpu.make_async_copy(shard, block(0, 0), lsem)
        self.ring = RingGather(lambda i: block(0, i), "dx", sems, 0, shard)
        self.far_ring = RingGather(lambda i: block(1, i), "dx", sems, 6)
        self.own_y = remote(shard, block(0, 0), sems, 12, dict(dyh=1))
        core = dict(dc=1)
        self.core = [remote(shard, block(0, 0), sems, 13, core)]
        for n in range(1, 8):
            ref = block(n // 4, n % 4)
            self.core.append(remote(ref, ref, sems, 13 + n, core))

    def start(self):
        self.ring.start()
        self.core[0].start()
        self.local.start()

    def forward(self):
        self.ring.forward()

    def forward_y(self):
        self.own_y.wait_recv()
        self.far_ring.start()
        self.core[4].start()

    def share(self):
        self.ring.behind()
        self.core[3].start()
        self.ring.ahead()
        self.core[1].start()
        self.ring.far()
        self.core[2].start()

    def forward_far(self):
        self.far_ring.forward()

    def share_far(self):
        self.far_ring.behind()
        self.core[7].start()
        self.far_ring.ahead()
        self.core[5].start()
        self.far_ring.far()
        self.core[6].start()

    def finish(self):
        for copy in self.core:
            copy.wait_recv()
        self.local.wait()
        self.ring.drain()
        self.far_ring.drain()
        for copy in [self.own_y] + self.core:
            copy.wait_send()


class ScatterDp:
    COPIES = 21

    @staticmethod
    def scratch(block):
        return (
            [pltpu.VMEM(block, BF16)]
            + RingReduce.scratch(*block) * 2
            + [DMA((21,)), DMA((21,))]
        )

    def __init__(self, part, kind, from_core, from_y, h0, f0, h1, f1, ssem, rsem):
        yh, x, c, yl, z = place()
        sems = (ssem, rsem)
        self.from_core, self.from_y = from_core, from_y
        block = lambda k, i, d: block_of(
            part, kind, lax.rem(yh + k, 2) * 8 + lax.rem(x + i, 4) * 2 + d
        )
        self.block = lambda k, i: block(k, i, c)
        self.core = [
            remote(block(n // 4, n % 4, 1 - c), from_core(n), sems, n, dict(dc=1))
            for n in range(8)
        ]
        self.ring = RingReduce(lambda i: block(0, i, c), "dx", h0, f0, sems, 8)
        self.far_ring = RingReduce(lambda i: block(1, i, c), "dx", h1, f1, sems, 14)
        self.last = remote(block(1, 0, c), from_y, sems, 20, dict(dyh=1))

    def start(self):
        for n in (6, 5, 7, 4, 2, 1, 3, 0):
            self.core[n].start()

    def add_core(self, n):
        self.core[n].wait_recv()
        ref = self.block(n // 4, n % 4)
        add_into(ref, ref, self.from_core(n))

    def along_x(self):
        for n in (6, 5, 7):
            self.add_core(n)
        self.far_ring.start()
        for n in (2, 1, 3):
            self.add_core(n)
        self.ring.start()
        for n in (4, 0):
            self.add_core(n)

    def forward(self):
        self.far_ring.forward()
        self.ring.forward()

    def along_y(self):
        self.far_ring.arrive()
        add_into(self.far_ring.terms[0], *self.far_ring.terms)
        self.last.start()

    def finish(self, out):
        self.ring.arrive()
        self.last.wait_recv()
        add_into(out, *self.ring.terms, self.from_y)
        self.ring.drain()
        self.far_ring.drain()
        for copy in self.core + [self.last]:
            copy.wait_send()


def params(cid):
    return pltpu.CompilerParams(
        collective_id=cid, has_side_effects=True, vmem_limit_bytes=65400 << 10
    )


def nn(a, b):
    return jnp.dot(a, b, preferred_element_type=F32)


def nt(a, b):
    return lax.dot_general(a, b, (((1,), (1,)), ((), ())), preferred_element_type=F32)


def tn(a, b):
    return lax.dot_general(a, b, (((0,), (0,)), ((), ())), preferred_element_type=F32)


def tiles(count, size):
    def run(body):
        @pl.loop(0, count // size)
        def _(i):
            body(pl.ds(pl.multiple_of(i * size, size), size))

    return run


def rope_table():
    frequency = THETA ** (-(np.arange(64, dtype=np.float32) * np.float32(2.0) / np.float32(HEAD_DIM)))
    angles = np.arange(1024, dtype=np.float32)[:, None] * frequency.astype(np.float32)[None, :]
    cosine, sine = np.cos(angles), np.sin(angles)
    return np.concatenate([cosine, sine], 1).astype(np.float32)


def cos_sin(table):
    turned = pltpu.roll(table, 64, 1)
    first = lax.broadcasted_iota(jnp.int32, table.shape, 1) < 64
    return jnp.where(first, table, turned), jnp.where(first, -turned, table)


class Exchange:
    PEERS = tuple(dict(dz=a, dyl=b) for b in range(2) for a in range(4) if a or b)

    def __init__(self, buf, ssem, rsem):
        yh, x, c, yl, z = place()
        self.buf = buf
        self.mine = buf.at[yl * 4 + z]
        self.copies = [
            remote(self.mine, self.mine, (ssem, rsem), i, peer)
            for i, peer in enumerate(self.PEERS)
        ]

    def start(self):
        for copy in self.copies:
            copy.start()

    def finish(self):
        for copy in self.copies:
            copy.wait_recv()
        for copy in self.copies:
            copy.wait_send()

    def sum(self):
        total = self.buf[0]
        for i in range(1, 8):
            total += self.buf[i]
        return total


def row_sums(values):
    return nt(jnp.ones((8, values.shape[1]), F32), values)


def spread(out, pair):
    row = lax.broadcasted_iota(jnp.int32, (8, 256), 0)
    column = lax.broadcasted_iota(jnp.int32, (8, 256), 1)
    for i in range(4):
        pick = jnp.where(row == column // 128 * 4 + i, 1.0, 0.0)
        out[pl.ds(256 * i, 256), :] = lax.dot_general(
            pair,
            pick,
            (((0,), (0,)), ((), ())),
            precision=lax.Precision.HIGHEST,
            preferred_element_type=F32,
        )


def note_sums(out, r, a, b):
    row = lax.broadcasted_iota(jnp.int32, (8, 256), 0)
    sums = jnp.where(row < 4, row_sums(a), row_sums(b))
    out[...] = jnp.where(lax.rem(row, 4) == r.start // 256, sums, out[...])


ALL_PEERS = Exchange.PEERS + DP_PEERS
SCALE = HEAD_DIM**-0.5


def diagonal_mask(scores, first, length):
    row = lax.broadcasted_iota(jnp.int32, scores.shape, 0)
    column = lax.broadcasted_iota(jnp.int32, scores.shape, 1)
    return jnp.where((column <= row) & (column + first < length), scores, -1e30)


class SumAll:
    def __init__(self, slots, hold, boxes, ssem, rsem):
        self.exchange = Exchange(slots, ssem, rsem)
        self.hold, self.boxes = hold, boxes
        self.copies = []
        for i, peer in enumerate(DP_PEERS):
            k = (1, 1, 1, 2, 0)[i]
            self.copies.append(remote(hold.at[k], boxes.at[i], (ssem, rsem), 7 + i, peer))

    def start(self):
        self.exchange.start()

    def core(self):
        self.exchange.finish()
        self.hold[0] = self.exchange.sum()
        self.copies[4].start()

    def along_x(self):
        self.copies[4].wait()
        self.hold[1] = self.hold[0] + self.boxes[4]
        for copy in self.copies[:3]:
            copy.start()

    def along_y(self):
        for copy in self.copies[:3]:
            copy.wait()
        self.hold[2] = self.hold[1] + self.boxes[0] + self.boxes[1] + self.boxes[2]
        self.copies[3].start()

    def finish(self, out):
        self.copies[3].wait()
        out[...] = self.hold[2] + self.boxes[3]


def whole_layer(tokens, lengths, cotangent, gains, weights, table):
    kinds = ("row", "row", "row", "col", "row", "row", "col")
    blocks = ((128, 256),) * 3 + ((256, 128), (128, 1024), (128, 1024), (1024, 128))

    def layer_step(
        lengths, cotangent, q_gain_all, k_gain_all, attn_gain, mlp_gain, table,
        tokens, i0, i1, i2, i3, i4, i5, i6,
        act, input_grad, o0, o1, o2, o3, o4, o5, o6,
        q_sum, k_sum, attn_sum, mlp_sum, x_kept, heads_kept, raw_kept,
        x, dd, wg, wu, wd, gate_factor, silu, inner, dg, du, part, residual, attn_part, mlp_part, q_line, k_line,
        wq, wk, wv, wo, stats, branch, do, dq, dk, dv, sums, gain_slots, gain_hold, gain_boxes,
        *rest,
    ):
        bufs, rest = rest[:8], rest[8:]
        dp_bufs, rest = [rest[7 * i : 7 * i + 7] for i in range(7)], rest[49:]
        s0, s1, s2, s3, g0, g1, g2, g3, esems, fsems, isems, wsems = [
            rest[2 * i : 2 * i + 2] for i in range(12)
        ]
        lsem, msem, ready = rest[24:]
        yh, xx, c, yl, z = place()
        me = yl * 4 + z
        length = lengths[0]
        total = input_grad
        own_columns = pl.ds(pl.multiple_of(me * 256, 256), 256)
        q_gain, k_gain = q_gain_all[:, own_columns], k_gain_all[:, own_columns]
        q_rot, k_rot, v_low, mixed = (dg.at[:, pl.ds(256 * i, 256)] for i in range(4))
        q_raw, k_raw, dvr = (du.at[:, pl.ds(256 * i, 256)] for i in range(3))
        dqr, dkr = q_raw, k_raw
        raw = du.at[:, pl.ds(0, 512)]
        load_heads = pltpu.make_async_copy(heads_kept, dg, msem.at[0])
        load_raw = pltpu.make_async_copy(raw_kept, raw, msem.at[2])
        reload = pltpu.make_async_copy(x_kept, x, msem.at[1])
        keep_x = pltpu.make_async_copy(dd, x_kept, msem.at[1])
        keep_heads = pltpu.make_async_copy(dg, heads_kept, msem.at[0])
        keep_raw = pltpu.make_async_copy(raw, raw_kept, msem.at[2])
        first = pltpu.make_async_copy(tokens, rows(dd, me), msem.at[3])
        first.start()
        greet(ALL_PEERS)
        shards = (i0, i1, i2, i3, i4, i5, i6)
        targets = (wq, wk, wv, wo, wg, wu, wd)
        spreads = [
            GatherDp(shards[i], targets[i], kinds[i], wsems[0].at[i], wsems[1].at[i], lsem.at[i])
            for i in range(7)
        ]
        small, large, down_weights = spreads[:4], spreads[4:6], spreads[6]
        for spread_item in small:
            spread_item.start()
            spread_item.own_y.start()
        first.wait()
        gather = GatherTensor(dd, *g0, 512)
        gather.start()

        def spread_small(stage):
            for spread_item in small:
                if stage == 0:
                    spread_item.forward()
                    spread_item.forward_y()
                else:
                    spread_item.share()
                    spread_item.forward_far()

        gather.run(lambda slot: None, spread_small)
        for spread_item in small:
            spread_item.share_far()
        for spread_item in large:
            spread_item.start()
            spread_item.own_y.start()
        for spread_item in small:
            spread_item.finish()
        sums[me] = jnp.zeros((8, 256), F32)
        keep_x.start()

        @tiles(1024, 256)
        def _(r):
            q = nn(dd[r, :], wq[...])
            k = nn(dd[r, :], wk[...])
            dq[r, :] = q
            dk[r, :] = k
            du[r, 0:256] = q.astype(BF16)
            du[r, 256:512] = k.astype(BF16)
            v_low[r, :] = nn(dd[r, :], wv[...]).astype(BF16)
            note_sums(sums.at[me], r, q * q, k * k)

        exchange = Exchange(sums, *esems)
        exchange.start()
        keep_raw.start()
        for spread_item in large:
            spread_item.forward()
        exchange.finish()
        for spread_item in large:
            spread_item.forward_y()
        down_weights.own_y.start()
        down_weights.start()
        spread(dv, lax.rsqrt(exchange.sum() * (1.0 / 2048) + EPS))
        narrow = lax.broadcasted_iota(jnp.int32, (1024, 128), 1) < 64
        stats[:, 128:256] = jnp.where(narrow, dv[:, 0:128], dv[:, 128:256])

        @tiles(1024, 256)
        def _(r):
            cos, sin = cos_sin(table[r, :])
            for source, gain, s, target, factor in (
                (dq, q_gain, 0, q_rot, SCALE),
                (dk, k_gain, 128, k_rot, 1.0),
            ):
                scale = dv[r, s : s + 128]
                for h in (0, 128):
                    v = source[r, h : h + 128] * scale * gain[:, h : h + 128]
                    v = v * cos + pltpu.roll(v, 64, 1) * sin
                    target[r, h : h + 128] = (v * factor).astype(BF16)

        @pl.loop(0, 2)
        def _(h):
            cols = pl.ds(pl.multiple_of(h * 128, 128), 128)
            mine = lax.broadcasted_iota(jnp.int32, (256, 128), 1) // 64 == h
            for i in range(4):
                low = i * 256
                block = slice(low, low + 256)
                q = q_rot[block, cols]
                near = diagonal_mask(nt(q, k_rot[block, cols]), low, length)
                peak = jnp.max(near, 1, keepdims=True)
                if i:
                    past = nt(q, k_rot[0:low, cols])
                    peak = jnp.maximum(peak, jnp.max(past, 1, keepdims=True))
                e1 = jnp.exp(near - peak)
                denom = jnp.sum(e1, 1, keepdims=True)
                out = nn(e1.astype(BF16), v_low[block, cols])
                if i:
                    e0 = jnp.exp(past - peak)
                    denom += jnp.sum(e0, 1, keepdims=True)
                    out += nn(e0.astype(BF16), v_low[0:low, cols])
                mixed[block, cols] = (out / denom).astype(BF16)
                lse = peak + jnp.log(denom)
                stats[block, 0:128] = jnp.where(mine, lse, stats[block, 0:128])

        keep_heads.start()

        def project(half, side):
            s = pl.ds(pl.multiple_of(half * 512, 512), 512)

            @pl.loop(0, 2)
            def _(i):
                n = pl.ds(pl.multiple_of(side * 1024 + i * 512, 512), 512)
                part[s, n] = nn(mixed[s, :], wo[:, n]).astype(BF16)

        scatter = ScatterTensor(part, bufs, *s0)
        scatter.run(project)
        scatter.step(0)
        for spread_item in large:
            spread_item.share()
            spread_item.forward_far()
        scatter.step(1)
        scatter.step(2)
        down_weights.forward()
        down_weights.forward_y()
        for spread_item in large:
            spread_item.share_far()
        scatter.step(3)
        scatter.finish(branch)
        own = rows(x, me)
        own_tokens = rows(dd, me)
        for copy in (keep_x, keep_raw, keep_heads):
            copy.wait()

        def tell(i):
            pl.semaphore_signal(ready.at[i], 1, device_id=other(dc=1), device_id_type=MESH)

        @tiles(128, 16)
        def _(r):
            b = branch[r, :]
            scale = lax.rsqrt(jnp.mean(b * b, 1, keepdims=True) + EPS)
            value = own_tokens[r, :].astype(F32) + b * scale * attn_gain[...]
            residual[r, :] = value
            own[r, :] = value.astype(BF16)

        gather = GatherTensor(x, *g1)
        gather.start()
        for spread_item in large:
            spread_item.finish()

        def gate_up(slot):
            s = pl.ds(pl.multiple_of(slot * 128, 128), 128)

            @tiles(1024, 512)
            def _(n):
                gate = nn(x[s, :], wg[:, n])
                up = nn(x[s, :], wu[:, n])
                sigmoid = jax.nn.sigmoid(gate)
                low = gate * sigmoid
                silu[s, n] = low.astype(BF16)
                gate_factor[s, n] = (up * (sigmoid + low * (1.0 - sigmoid))).astype(BF16)
                inner[s, n] = (low * up).astype(BF16)

        def spread_down(stage):
            if stage == 0:
                down_weights.share()
                down_weights.forward_far()
            else:
                down_weights.share_far()

        gather.run(gate_up, spread_down)
        down_weights.finish()

        def down(half, side):
            s = pl.ds(pl.multiple_of(half * 512, 512), 512)

            @pl.loop(0, 2)
            def _(i):
                n = pl.ds(pl.multiple_of(side * 1024 + i * 512, 512), 512)
                part[s, n] = nn(inner[s, :], wd[:, n]).astype(BF16)

        scatter = ScatterTensor(part, bufs, *s1)
        scatter.run(down)
        for n in range(4):
            scatter.step(n)
        scatter.finish(total)
        mlp_part[...] = jnp.zeros_like(mlp_part)
        attn_part[...] = jnp.zeros_like(attn_part)
        own_d = rows(dd, me)

        @tiles(128, 16)
        def _(r):
            v = total[r, :]
            position = lax.broadcasted_iota(jnp.int32, (16, 1), 0) + (me * 128 + r.start)
            ok = position < length
            scale = lax.rsqrt(jnp.mean(v * v, 1, keepdims=True) + EPS)
            normal = v * scale
            part[r, :] = jnp.where(ok, residual[r, :] + normal * mlp_gain[...], 0.0).astype(BF16)
            grad = jnp.where(ok, cotangent[r, :].astype(F32), 0.0)
            residual[r, :] = grad
            mlp_part[...] += jnp.sum(grad * normal, 0, keepdims=True)
            weighted = mlp_gain[...] * grad
            mean = jnp.mean(v * weighted, 1, keepdims=True)
            own_d[r, :] = (scale * weighted - v * (scale * scale * scale * mean)).astype(BF16)

        gather = GatherTensor(dd, *g2)
        gather.start()
        store_act = pltpu.make_async_copy(part.at[pl.ds(0, 128)], act, msem.at[1])
        store_act.start()

        def d_inner(slot):
            s = pl.ds(pl.multiple_of(slot * 128, 128), 128)

            @tiles(1024, 512)
            def _(n):
                d = nt(dd[s, :], wd[n, :])
                dg[s, n] = (d * gate_factor[s, n].astype(F32)).astype(BF16)
                du[s, n] = (d * silu[s, n].astype(F32)).astype(BF16)

        gather.run(d_inner)
        store_act.wait()
        tell(0)

        def d_input(half, side):
            s = pl.ds(pl.multiple_of(half * 512, 512), 512)

            @pl.loop(0, 2)
            def _(i):
                n = pl.ds(pl.multiple_of(side * 1024 + i * 512, 512), 512)
                part[s, n] = (nt(dg[s, :], wg[n, :]) + nt(du[s, :], wu[n, :])).astype(BF16)

        scatter = ScatterTensor(part, bufs, *s2)
        scatter.run(d_input)
        scatter.step(0)

        def down_grad(i):
            m = pl.ds(i * 512, 512)

            @tiles(2048, 512)
            def _(n):
                wd[m, n] = tn(inner[:, m], dd[:, n]).astype(BF16)

        def gate_grad(first):
            @pl.loop(first, first + 2)
            def _(i):
                m = pl.ds(pl.multiple_of(i * 512, 512), 512)

                @tiles(1024, 512)
                def _(n):
                    wg[m, n] = tn(x[:, m], dg[:, n]).astype(BF16)

        down_grad(0)
        down_grad(1)
        scatter.step(1)
        tell(1)

        def by_rows(ref):
            return lambda n: ref.at[pl.ds(n * 128, 128)]

        def by_columns(ref):
            return lambda n: ref.at[:, pl.ds(n * 128, 128)]

        small_slots = [by_rows(gate_factor.at[:, pl.ds(256 * i, 256)]) for i in range(3)]
        small_slots.append(
            lambda n: gate_factor.at[
                pl.ds(n // 2 * 256, 256), pl.ds(768 + n % 2 * 128, 128)
            ]
        )
        slots = small_slots + [by_rows(silu), by_rows(inner), by_columns(gate_factor)]
        wholes = (wq, wk, dd, wo, wg, wu, wd)
        scatter_kinds = kinds[:2] + ("folded",) + kinds[3:]
        items = [ScatterDp(wholes[i], scatter_kinds[i], slots[i], *dp_bufs[i]) for i in range(7)]
        qk, value_item, out_item, gate_item, up_item, down_item = items[:2], *items[2:]
        pl.semaphore_wait(ready.at[0], 1)
        down_item.start()
        scatter.step(2)
        gate_grad(0)
        scatter.step(3)
        gate_grad(2)
        gate_item.start()
        load_heads.start()
        scatter.finish(total)

        @tiles(128, 16)
        def _(r):
            grad = residual[r, :] + total[r, :]
            residual[r, :] = grad
            b = branch[r, :]
            scale = lax.rsqrt(jnp.mean(b * b, 1, keepdims=True) + EPS)
            attn_part[...] += jnp.sum(grad * b * scale, 0, keepdims=True)
            weighted = attn_gain[...] * grad
            mean = jnp.mean(b * weighted, 1, keepdims=True)
            own_d[r, :] = (scale * weighted - b * (scale * scale * scale * mean)).astype(BF16)

        gather = GatherTensor(dd, *g3, 768)
        gather.start()
        down_item.along_x()
        tell(2)

        gate_item.along_x()

        def d_mixed(slot):
            s = pl.ds(pl.multiple_of(slot * 128, 128), 128)
            do[s, :] = nt(dd[s, :], wo[...]).astype(BF16)

        def beside(stage):
            if stage == 0:
                down_item.forward()

                @tiles(2048, 512)
                def _(m):
                    @tiles(1024, 512)
                    def _(n):
                        wu[m, n] = tn(x[:, m], du[:, n]).astype(BF16)

                reload.start()
                load_raw.start()
                pl.semaphore_wait(ready.at[1], 1)
                up_item.start()
            else:
                gate_item.forward()
                down_item.along_y()

        gather.run(d_mixed, beside)
        up_item.along_x()
        load_heads.wait()
        load_raw.wait()

        @tiles(2048, 512)
        def _(n):
            wo[:, n] = tn(mixed[...], dd[:, n]).astype(BF16)

        pl.semaphore_wait(ready.at[2], 1)
        out_item.start()
        gate_item.along_y()

        @pl.loop(0, 2)
        def _(h):
            cols = pl.ds(pl.multiple_of(h * 128, 128), 128)
            for i in range(4):
                low = i * 256
                block = slice(low, low + 256)
                q, d = q_rot[block, cols], do[block, cols]
                top = jnp.where(h == 0, stats[block, 0:1], stats[block, 64:65])
                k1, v1 = k_rot[block, cols], v_low[block, cols]
                p1 = jnp.exp(diagonal_mask(nt(q, k1), low, length) - top)
                dp1 = nt(d, v1)
                delta = jnp.sum(p1 * dp1, 1, keepdims=True)
                if i:
                    k0, v0 = k_rot[0:low, cols], v_low[0:low, cols]
                    p0 = jnp.exp(nt(q, k0) - top)
                    dp0 = nt(d, v0)
                    delta += jnp.sum(p0 * dp0, 1, keepdims=True)
                ds1 = (p1 * (dp1 - delta)).astype(BF16)
                dq_block = nn(ds1, k1)
                dk[block, cols] = tn(ds1, q)
                dv[block, cols] = tn(p1.astype(BF16), d)
                if i:
                    ds0 = (p0 * (dp0 - delta)).astype(BF16)
                    dq_block += nn(ds0, k0)
                    dk[0:low, cols] += tn(ds0, q)
                    dv[0:low, cols] += tn(p0.astype(BF16), d)
                dq[block, cols] = dq_block

        up_item.forward()
        q_line[...] = jnp.zeros_like(q_line)
        k_line[...] = jnp.zeros_like(k_line)
        sums[me] = jnp.zeros((8, 256), F32)

        @tiles(1024, 256)
        def _(r):
            cos, sin = cos_sin(table[r, :])
            for source, rawer, gain, s, factor, line in (
                (dq, q_raw, q_gain, 128, SCALE, q_line),
                (dk, k_raw, k_gain, 192, 1.0, k_line),
            ):
                scale = stats[r, s : s + 1]
                for h in (0, 128):
                    v = source[r, h : h + 128] * factor
                    v = v * cos - pltpu.roll(v, 64, 1) * sin
                    w = v * rawer[r, h : h + 128].astype(F32)
                    line[:, h : h + 128] += jnp.sum(w * scale, 0, keepdims=True)
                    source[r, h : h + 128] = v * gain[:, h : h + 128]
            note_sums(
                sums.at[me],
                r,
                dq[r, :] * q_raw[r, :].astype(F32),
                dk[r, :] * k_raw[r, :].astype(F32),
            )
            dvr[r, :] = dv[r, :].astype(BF16)

        exchange = Exchange(sums, *fsems)
        exchange.start()
        reload.wait()
        row = lax.broadcasted_iota(jnp.int32, (8, 1024), 0)
        column = lax.broadcasted_iota(jnp.int32, (8, 1024), 1)
        message = jnp.zeros((8, 1024), F32)
        for k, line in enumerate((attn_part, attn_part, mlp_part, mlp_part)):
            line = line[:, 1024 * (k % 2) : 1024 * (k % 2) + 1024]
            message = jnp.where(row == 4 + k, line, message)
        for first_row, line in ((0, q_line), (2, k_line)):
            line = jnp.concatenate([line[...]] * 4, 1)
            message += jnp.where((row == first_row + yl) & (column // 256 == z), line, 0.0)
        gain_slots[me] = message
        total_gain = SumAll(gain_slots, gain_hold, gain_boxes, *isems)

        @pl.loop(0, 4)
        def _(i):
            m = pl.ds(pl.multiple_of(i * 512, 512), 512)
            r = pl.ds(pl.multiple_of(lax.rem(i, 2) * 512, 512), 512)
            columns = pl.ds(pl.multiple_of(i // 2 * 256, 256), 256)
            dd[r, columns] = tn(x[:, m], dvr[...]).astype(BF16)

        value_item.start()
        out_item.along_x()
        exchange.finish()
        total_gain.start()
        spread(dv, exchange.sum() * (1.0 / 2048))

        @tiles(1024, 256)
        def _(r):
            for source, rawer, s, target in ((dq, q_raw, 0, dqr), (dk, k_raw, 128, dkr)):
                scale = stats[r, 128 + s // 2 : 129 + s // 2]
                factor = scale * scale * scale * dv[r, s : s + 128]
                for h in (0, 128):
                    target[r, h : h + 128] = (
                        scale * source[r, h : h + 128]
                        - rawer[r, h : h + 128].astype(F32) * factor
                    ).astype(BF16)

        def d_tokens(half, side):
            s = pl.ds(pl.multiple_of(half * 512, 512), 512)

            @pl.loop(0, 2)
            def _(i):
                n = pl.ds(pl.multiple_of(side * 1024 + i * 512, 512), 512)
                terms = nt(dqr[s, :], wq[n, :]) + nt(dkr[s, :], wk[n, :]) + nt(dvr[s, :], wv[n, :])
                part[s, n] = terms.astype(BF16)

        scatter = ScatterTensor(part, bufs, *s3)
        scatter.run(d_tokens)
        up_item.along_y()
        value_item.along_x()
        scatter.step(0)

        @tiles(2048, 512)
        def _(m):
            xt = x[:, m].T
            wq[m, :] = nn(xt, dqr[...]).astype(BF16)
            wk[m, :] = nn(xt, dkr[...]).astype(BF16)

        for item in qk:
            item.start()
        out_item.forward()
        total_gain.core()
        scatter.step(1)
        for item in qk:
            item.along_x()
        value_item.forward()
        total_gain.along_x()
        scatter.step(2)
        out_item.along_y()
        scatter.step(3)
        for item in qk:
            item.forward()
        total_gain.along_y()
        stores = []

        def store(item, source, target):
            item.finish(source)
            stores.append(pltpu.make_async_copy(source, target, lsem.at[len(stores)]))
            stores[-1].start()

        store(down_item, dv.at[:, pl.ds(0, 128)], o6)
        gate_item.finish(o4)
        up_item.finish(o5)
        value_item.along_y()
        store(out_item, dv.at[pl.ds(0, 256), pl.ds(128, 128)], o3)
        scatter.finish(input_grad)

        @tiles(128, 16)
        def _(r):
            input_grad[r, :] += residual[r, :]

        for item in qk:
            item.along_y()
        total_gain.finish(gain_slots.at[0])
        for i, out in enumerate((q_sum, k_sum, attn_sum, mlp_sum)):
            out[:, 0:1024] = gain_slots[0, 2 * i : 2 * i + 1, :]
            out[:, 1024:2048] = gain_slots[0, 2 * i + 1 : 2 * i + 2, :]
        store(value_item, dk.at[pl.ds(256, 128)], o2)
        for i, out in enumerate((o0, o1)):
            store(qk[i], dk.at[pl.ds(128 * i, 128)], out)
        for copy in stores:
            copy.wait()

    S = jax.ShapeDtypeStruct
    W = pltpu.VMEM
    scratch = [W((1024, 2048), BF16)] * 2 + [W((2048, 1024), BF16)] * 2 + [W((1024, 2048), BF16)]
    scratch += [W((1024, 1024), BF16)] * 5 + [W((1024, 2048), BF16)]
    scratch += [W((128, 2048), F32)] + [W((1, 2048), F32)] * 2 + [W((1, 256), F32)] * 2
    scratch += [W((2048, 256), BF16)] * 3 + [W((256, 2048), BF16)]
    scratch += [W((1024, 256), F32), W((128, 2048), F32), W((1024, 256), BF16)]
    scratch += [W((1024, 256), F32)] * 3
    scratch += [W((8, 8, 256), F32), W((8, 8, 1024), F32)] + [W((3, 8, 1024), F32), W((5, 8, 1024), F32)]
    scratch += ScatterTensor.scratch()
    for b in blocks:
        scratch += ScatterDp.scratch(b)
    for n in (23, 23, 23, 23, 21, 21, 21, 21, 7, 7, 12):
        scratch += [DMA((n,))] * 2
    scratch += [DMA((7, 21))] * 2
    scratch += [DMA((8,)), DMA((4,)), pltpu.SemaphoreType.REGULAR((3,))]
    return pl.pallas_call(
        layer_step,
        out_shape=[S((128, 2048), BF16), S((128, 2048), F32)]
        + [S(b, F32) for b in blocks]
        + [S((1, 2048), F32)] * 4
        + [S((1024, 2048), BF16), S((1024, 1024), BF16), S((1024, 512), BF16)],
        in_specs=[SMEM] + [VM] * 6 + [ANY] * 8,
        out_specs=[ANY, VM] + [ANY] * 4 + [VM] * 2 + [ANY] + [VM] * 4 + [ANY] * 3,
        scratch_shapes=scratch,
        compiler_params=params(1),
        name="layer_step",
    )(lengths, cotangent, *gains, table, tokens, *weights)[:13]


def hand_over(*arrays):
    n = len(arrays)

    def hand_over_step(*refs):
        held, (lsem, ssem) = refs[2 * n : 3 * n], refs[3 * n :]
        loads = [pltpu.make_async_copy(refs[i], held[i], lsem.at[i]) for i in range(n)]
        stores = [pltpu.make_async_copy(held[i], refs[n + i], ssem.at[i]) for i in range(n)]
        for copy in loads:
            copy.start()
        for load, store in zip(loads, stores):
            load.wait()
            store.start()
        for copy in stores:
            copy.wait()

    return pl.pallas_call(
        hand_over_step,
        out_shape=[jax.ShapeDtypeStruct(a.shape, a.dtype) for a in arrays],
        in_specs=[ANY] * n,
        out_specs=[ANY] * n,
        scratch_shapes=[pltpu.VMEM(a.shape, a.dtype) for a in arrays] + [DMA((n,))] * 2,
        compiler_params=pltpu.CompilerParams(vmem_limit_bytes=63 << 20),
        name="hand_over_step",
    )(*arrays)


def local(
    tokens, lengths, w_query, w_key, w_value, w_out, w_gate, w_up, w_down,
    q_gain, k_gain, attn_gain, mlp_gain, cotangent,
):
    weights = (w_query, w_key, w_value, w_out, w_gate, w_up, w_down)
    gains = (q_gain[None], k_gain[None], attn_gain[None], mlp_gain[None])
    results = whole_layer(tokens[0], lengths, cotangent[0], gains, weights, rope_table())
    act, input_grad, *grads = hand_over(*results)
    return (act[None], input_grad[None], *grads[:7], *(g.reshape(2048) for g in grads[7:]))


def solution(mesh):
    return jax.shard_map(
        local,
        mesh=mesh,
        in_specs=(
            P("dp", "tensor", None),
            P("dp"),
            P("dp", "tensor"),
            P("dp", "tensor"),
            P("dp", "tensor"),
            P("tensor", "dp"),
            P("dp", "tensor"),
            P("dp", "tensor"),
            P("tensor", "dp"),
            P(),
            P(),
            P(),
            P(),
            P("dp", "tensor", None),
        ),
        out_specs=(
            P("dp", "tensor", None),
            P("dp", "tensor", None),
            P("dp", "tensor"),
            P("dp", "tensor"),
            P("dp", "tensor"),
            P("tensor", "dp"),
            P("dp", "tensor"),
            P("dp", "tensor"),
            P("tensor", "dp"),
            P(),
            P(),
            P(),
            P(),
        ),
        check_vma=False,
    )
```

time: 348 us -> 315 us (0.905)
  Pallas kernels: 342 us -> 313 us
    pallas_call x3 -> x1, Pallas kernels: 339 us -> 310 us  [whole_layer(): pl.pallas_call(layer_step, out_shape=[S((128, 2048), BF16), S((128, 2048)...]
where the time goes in v3:
time: 315 us
  Pallas kernels  313 us (99%)
    pallas_call x1, Pallas kernels, whole_layer(): pl.pallas_call(layer_step, out_shape=[S((128, 2048), BF16), S((128, 2048)...  310 us

profile of v3, /device:TPU:0, one launch (start us, length us, event | category | flops | bytes accessed | tf_op | source)
XLA Modules:
  0.0 314.5 jit_solution(11022922110393719764)
XLA Ops:
  1.3 309.8 %layer_step.1 = (bf16[128,2048]{1,0:T(8,128)(2,1)}, f32[128,2048]{1,0:T(8,128)}, f32[128,256]{1,0:T(8,128)}, f32[128,256]{1,0:T(8,128)}, f32[128,256]{1,0:T(8,12...) custom-call(s32[1]{0:T(128)S(6)} %copy.28.lengths, ...), custom_call_target="tpu_custom_call" | custom-call | tf_op jit(solution)/shard_map/layer_step/pallas_call | solution.py:1148
  311.1 3.3 %hand_over_step.1 = (bf16[128,2048]{1,0:T(8,128)(2,1)}, f32[128,2048]{1,0:T(8,128)}, f32[128,256]{1,0:T(8,128)}, f32[128,256]{1,0:T(8,128)}, f32[128,256]{1,0:T(...) custom-call(bf16[128,2048]{1,0:T(8,128)(2,1)} %get-tuple-element.39., ...), custom_call_target="tpu_custom_call" | custom-call | tf_op jit(solution)/shard_map/hand_over_step/pallas_call | solution.py:1177

commit v4 on v3

--- a/solution.py
+++ b/solution.py
@@ -50,13 +50,17 @@
     return pltpu.make_async_remote_copy(
         src_ref=src,
         dst_ref=dst,
-        send_sem=ssem.at[index],
+        send_sem=ssem,
         recv_sem=rsem.at[index],
         device_id=other(**peer),
         device_id_type=MESH,
     )
 
 
+def all_of(bytes_of, sem):
+    pltpu.make_async_copy(bytes_of, bytes_of, sem).wait()
+
+
 def rows(ref, slot):
     return ref.at[pl.ds(pl.multiple_of(slot * 128, 128), 128)]
 
@@ -67,9 +71,11 @@
 
 
 def add_into(out, *terms):
-    @pl.loop(0, out.shape[0] // 16)
+    step = min(out.shape[0], 16 if out.shape[1] > 1024 else 64 if out.shape[1] > 128 else 128)
+
+    @pl.loop(0, out.shape[0] // step)
     def _(i):
-        r = pl.ds(pl.multiple_of(i * 16, 16), 16)
+        r = pl.ds(pl.multiple_of(i * step, step), step)
         if len(terms) == 2 and out.dtype == BF16:
             out[r, :] = terms[0][r, :] + terms[1][r, :]
         else:
@@ -113,10 +119,6 @@
     def far(self):
         for copy in self.copies[4:]:
             copy.wait_recv()
-
-    def drain(self):
-        for copy in self.copies:
-            copy.wait_send()
 
 
 class RingReduce:
@@ -155,10 +157,6 @@
         for copy in self.copies[2:]:
             copy.wait_recv()
 
-    def drain(self):
-        for copy in self.copies:
-            copy.wait_send()
-
 
 class GatherTensor:
     COPIES = 21
@@ -166,6 +164,7 @@
     def __init__(self, buf, ssem, rsem, cut=CUT):
         yh, x, c, yl, z = place()
         self.yl, self.z = yl, z
+        self.sent, self.ssem = buf.at[pl.ds(0, 896)], ssem
         sems = (ssem, rsem)
         slot = lambda k, i: rows(buf, lax.rem(yl + k, 2) * 4 + lax.rem(z + i, 4))
         low = lambda ref: ref.at[:, pl.ds(0, cut)]
@@ -186,7 +185,7 @@
         self.low[0].start()
         self.low[1].start()
 
-    def run(self, process, spare=None):
+    def run(self, process, spare=None, by_half=None, early=None):
         yl, z = self.yl, self.z
 
         @pl.loop(0, 2)
@@ -196,6 +195,8 @@
                 self.ring.forward()
                 self.low[2].start()
                 self.low[5].start()
+                if early is not None:
+                    early()
                 self.high.wait_recv()
                 self.pair_ring.start()
                 self.ring.behind()
@@ -210,8 +211,16 @@
         if spare is not None:
             spare(0)
 
-        @pl.loop(0, 6)
+        @pl.loop(0, 6 if by_half is None else 7)
         def _(j):
+            if by_half is not None:
+
+                @pl.when(lax.rem(j, 3) == 0)
+                def _():
+                    @pl.when(j > 0)
+                    def _():
+                        by_half(lax.rem(yl + j // 6, 2))
+
             @pl.when(j == 2)
             def _():
                 self.ring.far()
@@ -235,83 +244,117 @@
 
             @pl.when(j == 5)
             def _():
+                if spare is not None:
+                    spare(2)
                 self.pair_ring.far()
                 self.low[6].wait_recv()
                 self.low[7].wait_recv()
 
             i = lax.rem(j, 3)
             step = (3 * i * i - 7 * i + 6) // 2
-            process(lax.rem(yl + j // 3, 2) * 4 + lax.rem(z + step, 4))
-
-        self.ring.drain()
-        self.pair_ring.drain()
-        for copy in [self.high] + self.low:
-            copy.wait_send()
+
+            @pl.when(j < 6)
+            def _():
+                process(lax.rem(yl + j // 3, 2) * 4 + lax.rem(z + step, 4))
+
+        all_of(self.sent, self.ssem)
 
 
 class ScatterTensor:
     COPIES = 23
 
     @staticmethod
-    def scratch():
+    def scratch(least, most):
         return (
-            [pltpu.VMEM((4, 128, CUT), BF16), pltpu.VMEM((128, WIDTH - CUT), BF16)]
-            + RingReduce.scratch(128, CUT)
-            + RingReduce.scratch(128, WIDTH - CUT) * 2
+            [pltpu.VMEM((4, 128, most), BF16), pltpu.VMEM((128, WIDTH - least), BF16)]
+            + RingReduce.scratch(128, most)
+            + RingReduce.scratch(128, WIDTH - least) * 2
         )
 
-    def __init__(self, part, bufs, ssem, rsem):
+    def __init__(self, part, bufs, ssem, rsem, cut=CUT):
         yh, x, c, yl, z = place()
+        self.z = z
+        narrow = lambda ref, n: ref.at[:, :, pl.ds(0, n)]
+        wide = WIDTH - cut
+        bufs = [
+            narrow(bufs[0], cut),
+            bufs[1].at[:, pl.ds(0, wide)],
+            *(narrow(ref, cut) for ref in bufs[2:4]),
+            *(narrow(ref, wide) for ref in bufs[4:]),
+        ]
         self.yl = yl
         self.from_pair, self.last = bufs[0], bufs[1]
+        self.sent, self.ssem = part.at[pl.ds(0, 896)], ssem
         sems = (ssem, rsem)
         slot = lambda k, i: rows(part, lax.rem(yl + k, 2) * 4 + lax.rem(z + i, 4))
-        low = lambda k, i: slot(k, i).at[:, pl.ds(0, CUT)]
-        high = lambda k, i: slot(k, i).at[:, pl.ds(CUT, WIDTH - CUT)]
+        low = lambda k, i: slot(k, i).at[:, pl.ds(0, cut)]
+        high = lambda k, i: slot(k, i).at[:, pl.ds(cut, wide)]
+        self.cut = cut
         pair = dict(dyl=1)
         self.low = lambda i: low(0, i)
         self.low_ring = RingReduce(lambda i: low(0, i), "dz", bufs[2], bufs[3], sems, 0)
         self.pair_ring = RingReduce(lambda i: high(1, i), "dz", bufs[4], bufs[5], sems, 6)
         self.own_ring = RingReduce(lambda i: high(0, i), "dz", bufs[6], bufs[7], sems, 12)
-        self.first = [remote(low(1, i), bufs[0].at[i], sems, 18 + i, pair) for i in range(4)]
+        self.first = lambda i: remote(low(1, i), bufs[0].at[i], sems, 18 + i, pair)
         self.second = remote(high(1, 0), bufs[1], sems, 22, pair)
 
-    def run(self, process):
+    def run(self, process, before=None):
+        yl, z = self.yl, self.z
+
         @pl.loop(0, 4)
         def _(k):
-            process(lax.rem(self.yl + 1 + k // 2, 2), lax.rem((k + 1) // 2, 2))
+            half = lax.rem(yl + 1 + k // 2, 2)
+            if before is not None:
+
+                @pl.when(lax.rem(k, 2) == 0)
+                def _():
+                    before(half)
+
+            process(half * 512 + lax.rem((z + 2) // 2 + k, 2) * 256)
+            beside = 3 - 2 * lax.rem(z, 2)
 
             @pl.when(k == 0)
             def _():
-                for i in (2, 1, 3, 0):
-                    self.first[i].start()
+                self.first(2).start()
+                self.pair_ring.copies[0].start()
+                self.pair_ring.copies[1].start()
+                self.first(beside).start()
 
             @pl.when(k == 1)
             def _():
-                self.pair_ring.start()
+                self.first(4 - beside).start()
+                self.pair_ring.copies[2].start()
+                self.pair_ring.copies[3].start()
+                self.first(0).start()
 
     def add_first(self, i):
-        self.first[i].wait_recv()
+        self.first(i).wait_recv()
         add_into(self.low(i), self.low(i), self.from_pair.at[i])
 
+    def add_low(self, i):
+        self.add_first(i)
+        for k in (1, 3):
+
+            @pl.when(i == k)
+            def _():
+                self.low_ring.copies[2 + k // 3].start()
+
     def step(self, n):
-        low = self.low_ring.copies
+        beside = 3 - 2 * lax.rem(self.z, 2)
         if n == 0:
             self.pair_ring.forward()
             self.own_ring.start()
             self.add_first(2)
-            low[0].start()
-            low[1].start()
+            self.low_ring.copies[0].start()
+            self.low_ring.copies[1].start()
         if n == 1:
-            self.add_first(1)
-            low[2].start()
             self.own_ring.forward()
+            self.add_low(beside)
         if n == 2:
             self.pair_ring.arrive()
             add_into(self.pair_ring.terms[0], *self.pair_ring.terms)
             self.second.start()
-            self.add_first(3)
-            low[3].start()
+            self.add_low(4 - beside)
         if n == 3:
             self.low_ring.forward()
             self.add_first(0)
@@ -319,13 +362,10 @@
     def finish(self, out):
         self.own_ring.arrive()
         self.second.wait_recv()
-        add_into(out.at[:, pl.ds(CUT, WIDTH - CUT)], *self.own_ring.terms, self.last)
+        add_into(out.at[:, pl.ds(self.cut, WIDTH - self.cut)], *self.own_ring.terms, self.last)
         self.low_ring.arrive()
-        add_into(out.at[:, pl.ds(0, CUT)], *self.low_ring.terms)
-        for ring in (self.low_ring, self.pair_ring, self.own_ring):
-            ring.drain()
-        for copy in self.first + [self.second]:
-            copy.wait_send()
+        add_into(out.at[:, pl.ds(0, self.cut)], *self.low_ring.terms)
+        all_of(self.sent, self.ssem)
 
 
 def block_of(ref, kind, slot):
@@ -341,6 +381,14 @@
     return ref.at[:, pl.ds(pl.multiple_of(slot * size, size), size)]
 
 
+def some_of(ref, kind, count):
+    if kind == "row":
+        return ref.at[pl.ds(0, ref.shape[0] // 16 * count)]
+    if kind == "folded":
+        return ref.at[pl.ds(0, 64 * count), pl.ds(0, 512)]
+    return ref.at[:, pl.ds(0, ref.shape[1] // 16 * count)]
+
+
 class GatherDp:
     COPIES = 21
 
@@ -350,6 +398,7 @@
         block = lambda k, i: block_of(
             out, kind, lax.rem(yh + k, 2) * 8 + lax.rem(x + i, 4) * 2 + c
         )
+        self.sent, self.ssem = some_of(out, kind, 15), ssem
         self.local = pltpu.make_async_copy(shard, block(0, 0), lsem)
         self.ring = RingGather(lambda i: block(0, i), "dx", sems, 0, shard)
         self.far_ring = RingGather(lambda i: block(1, i), "dx", sems, 6)
@@ -358,7 +407,8 @@
         self.core = [remote(shard, block(0, 0), sems, 13, core)]
         for n in range(1, 8):
             ref = block(n // 4, n % 4)
-            self.core.append(remote(ref, ref, sems, 13 + n, core))
+            self.core.append(remote(ref, ref, sems, 13, core))
+        self.shared, self.shared_sem = some_of(out, kind, 8), rsem.at[13]
 
     def start(self):
         self.ring.start()
@@ -393,13 +443,9 @@
         self.core[6].start()
 
     def finish(self):
-        for copy in self.core:
-            copy.wait_recv()
+        all_of(self.shared, self.shared_sem)
         self.local.wait()
-        self.ring.drain()
-        self.far_ring.drain()
-        for copy in [self.own_y] + self.core:
-            copy.wait_send()
+        all_of(self.sent, self.ssem)
 
 
 class ScatterDp:
@@ -410,35 +456,37 @@
         return (
             [pltpu.VMEM(block, BF16)]
             + RingReduce.scratch(*block) * 2
-            + [DMA((21,)), DMA((21,))]
+            + [DMA, DMA((14,))]
         )
 
     def __init__(self, part, kind, from_core, from_y, h0, f0, h1, f1, ssem, rsem):
         yh, x, c, yl, z = place()
         sems = (ssem, rsem)
         self.from_core, self.from_y = from_core, from_y
+        self.sent, self.ssem = some_of(part, kind, 15), ssem
         block = lambda k, i, d: block_of(
             part, kind, lax.rem(yh + k, 2) * 8 + lax.rem(x + i, 4) * 2 + d
         )
         self.block = lambda k, i: block(k, i, c)
         self.core = [
-            remote(block(n // 4, n % 4, 1 - c), from_core(n), sems, n, dict(dc=1))
+            remote(block(n // 4, n % 4, 1 - c), from_core(n), sems, 0, dict(dc=1))
             for n in range(8)
         ]
-        self.ring = RingReduce(lambda i: block(0, i, c), "dx", h0, f0, sems, 8)
-        self.far_ring = RingReduce(lambda i: block(1, i, c), "dx", h1, f1, sems, 14)
-        self.last = remote(block(1, 0, c), from_y, sems, 20, dict(dyh=1))
+        self.ring = RingReduce(lambda i: block(0, i, c), "dx", h0, f0, sems, 1)
+        self.far_ring = RingReduce(lambda i: block(1, i, c), "dx", h1, f1, sems, 7)
+        self.last = remote(block(1, 0, c), from_y, sems, 13, dict(dyh=1))
+        self.shared, self.shared_sem = some_of(part, kind, 8), rsem.at[0]
 
     def start(self):
         for n in (6, 5, 7, 4, 2, 1, 3, 0):
             self.core[n].start()
 
     def add_core(self, n):
-        self.core[n].wait_recv()
         ref = self.block(n // 4, n % 4)
         add_into(ref, ref, self.from_core(n))
 
     def along_x(self):
+        all_of(self.shared, self.shared_sem)
         for n in (6, 5, 7):
             self.add_core(n)
         self.far_ring.start()
@@ -461,10 +509,7 @@
         self.ring.arrive()
         self.last.wait_recv()
         add_into(out, *self.ring.terms, self.from_y)
-        self.ring.drain()
-        self.far_ring.drain()
-        for copy in self.core + [self.last]:
-            copy.wait_send()
+        all_of(self.sent, self.ssem)
 
 
 def params(cid):
@@ -512,7 +557,7 @@
 
     def __init__(self, buf, ssem, rsem):
         yh, x, c, yl, z = place()
-        self.buf = buf
+        self.buf, self.ssem = buf, ssem
         self.mine = buf.at[yl * 4 + z]
         self.copies = [
             remote(self.mine, self.mine, (ssem, rsem), i, peer)
@@ -526,8 +571,7 @@
     def finish(self):
         for copy in self.copies:
             copy.wait_recv()
-        for copy in self.copies:
-            copy.wait_send()
+        all_of(self.buf.at[pl.ds(0, 7)], self.ssem)
 
     def sum(self):
         total = self.buf[0]
@@ -572,12 +616,12 @@
 
 class SumAll:
     def __init__(self, slots, hold, boxes, ssem, rsem):
-        self.exchange = Exchange(slots, ssem, rsem)
+        self.exchange = Exchange(slots, ssem.at[5], rsem)
         self.hold, self.boxes = hold, boxes
         self.copies = []
         for i, peer in enumerate(DP_PEERS):
             k = (1, 1, 1, 2, 0)[i]
-            self.copies.append(remote(hold.at[k], boxes.at[i], (ssem, rsem), 7 + i, peer))
+            self.copies.append(remote(hold.at[k], boxes.at[i], (ssem.at[i], rsem), 7 + i, peer))
 
     def start(self):
         self.exchange.start()
@@ -619,10 +663,10 @@
     ):
         bufs, rest = rest[:8], rest[8:]
         dp_bufs, rest = [rest[7 * i : 7 * i + 7] for i in range(7)], rest[49:]
-        s0, s1, s2, s3, g0, g1, g2, g3, esems, fsems, isems, wsems = [
-            rest[2 * i : 2 * i + 2] for i in range(12)
+        scatter_sems, gather_sems, sum_sems, isems, wsems = [
+            rest[2 * i : 2 * i + 2] for i in range(5)
         ]
-        lsem, msem, ready = rest[24:]
+        lsem, msem, ready = rest[10:]
         yh, xx, c, yl, z = place()
         me = yl * 4 + z
         length = lengths[0]
@@ -653,24 +697,28 @@
             spread_item.start()
             spread_item.own_y.start()
         first.wait()
-        gather = GatherTensor(dd, *g0, 512)
+        gather = GatherTensor(dd, *gather_sems, 640)
         gather.start()
+
+        def forward_small():
+            for spread_item in small:
+                spread_item.forward()
+                spread_item.forward_y()
 
         def spread_small(stage):
             for spread_item in small:
                 if stage == 0:
-                    spread_item.forward()
-                    spread_item.forward_y()
-                else:
                     spread_item.share()
                     spread_item.forward_far()
-
-        gather.run(lambda slot: None, spread_small)
-        for spread_item in small:
-            spread_item.share_far()
+                elif stage == 1:
+                    spread_item.share_far()
+            if stage == 2:
+                down_weights.own_y.start()
+
+        gather.run(lambda slot: None, spread_small, early=forward_small)
         for spread_item in large:
             spread_item.start()
-            spread_item.own_y.start()
+        large[0].own_y.start()
         for spread_item in small:
             spread_item.finish()
         sums[me] = jnp.zeros((8, 256), F32)
@@ -687,16 +735,14 @@
             v_low[r, :] = nn(dd[r, :], wv[...]).astype(BF16)
             note_sums(sums.at[me], r, q * q, k * k)
 
-        exchange = Exchange(sums, *esems)
+        exchange = Exchange(sums, *sum_sems)
         exchange.start()
         keep_raw.start()
+        exchange.finish()
+        large[1].own_y.start()
         for spread_item in large:
             spread_item.forward()
-        exchange.finish()
-        for spread_item in large:
-            spread_item.forward_y()
-        down_weights.own_y.start()
-        down_weights.start()
+        large[0].forward_y()
         spread(dv, lax.rsqrt(exchange.sum() * (1.0 / 2048) + EPS))
         narrow = lax.broadcasted_iota(jnp.int32, (1024, 128), 1) < 64
         stats[:, 128:256] = jnp.where(narrow, dv[:, 0:128], dv[:, 128:256])
@@ -714,53 +760,59 @@
                     v = v * cos + pltpu.roll(v, 64, 1) * sin
                     target[r, h : h + 128] = (v * factor).astype(BF16)
 
-        @pl.loop(0, 2)
-        def _(h):
-            cols = pl.ds(pl.multiple_of(h * 128, 128), 128)
-            mine = lax.broadcasted_iota(jnp.int32, (256, 128), 1) // 64 == h
-            for i in range(4):
-                low = i * 256
-                block = slice(low, low + 256)
-                q = q_rot[block, cols]
-                near = diagonal_mask(nt(q, k_rot[block, cols]), low, length)
-                peak = jnp.max(near, 1, keepdims=True)
-                if i:
-                    past = nt(q, k_rot[0:low, cols])
-                    peak = jnp.maximum(peak, jnp.max(past, 1, keepdims=True))
-                e1 = jnp.exp(near - peak)
-                denom = jnp.sum(e1, 1, keepdims=True)
-                out = nn(e1.astype(BF16), v_low[block, cols])
-                if i:
-                    e0 = jnp.exp(past - peak)
-                    denom += jnp.sum(e0, 1, keepdims=True)
-                    out += nn(e0.astype(BF16), v_low[0:low, cols])
-                mixed[block, cols] = (out / denom).astype(BF16)
-                lse = peak + jnp.log(denom)
-                stats[block, 0:128] = jnp.where(mine, lse, stats[block, 0:128])
-
-        keep_heads.start()
-
-        def project(half, side):
-            s = pl.ds(pl.multiple_of(half * 512, 512), 512)
+        def attend(half):
+            for top in range(2):
+
+                @pl.when(half == top)
+                def _():
+                    @pl.loop(0, 2)
+                    def _(h):
+                        cols = pl.ds(pl.multiple_of(h * 128, 128), 128)
+                        mine = lax.broadcasted_iota(jnp.int32, (256, 128), 1) // 64 == h
+                        for i in (2 * top, 2 * top + 1):
+                            low = i * 256
+                            block = slice(low, low + 256)
+                            q = q_rot[block, cols]
+                            near = diagonal_mask(nt(q, k_rot[block, cols]), low, length)
+                            peak = jnp.max(near, 1, keepdims=True)
+                            if i:
+                                past = nt(q, k_rot[0:low, cols])
+                                peak = jnp.maximum(peak, jnp.max(past, 1, keepdims=True))
+                            e1 = jnp.exp(near - peak)
+                            denom = jnp.sum(e1, 1, keepdims=True)
+                            out = nn(e1.astype(BF16), v_low[block, cols])
+                            if i:
+                                e0 = jnp.exp(past - peak)
+                                denom += jnp.sum(e0, 1, keepdims=True)
+                                out += nn(e0.astype(BF16), v_low[0:low, cols])
+                            mixed[block, cols] = (out / denom).astype(BF16)
+                            lse = peak + jnp.log(denom)
+                            stats[block, 0:128] = jnp.where(mine, lse, stats[block, 0:128])
+
+        def project(first_row):
+            s = pl.ds(pl.multiple_of(first_row, 256), 256)
 
             @pl.loop(0, 2)
             def _(i):
-                n = pl.ds(pl.multiple_of(side * 1024 + i * 512, 512), 512)
+                n = pl.ds(pl.multiple_of(i * 1024, 1024), 1024)
                 part[s, n] = nn(mixed[s, :], wo[:, n]).astype(BF16)
 
-        scatter = ScatterTensor(part, bufs, *s0)
-        scatter.run(project)
+        scatter = ScatterTensor(part, bufs, *scatter_sems)
+        scatter.run(project, attend)
+        keep_heads.start()
+        large[1].forward_y()
         scatter.step(0)
         for spread_item in large:
             spread_item.share()
+        scatter.step(1)
+        for spread_item in large:
             spread_item.forward_far()
-        scatter.step(1)
+        down_weights.start()
+        down_weights.forward_y()
         scatter.step(2)
-        down_weights.forward()
-        down_weights.forward_y()
+        scatter.step(3)
         for spread_item in large:
             spread_item.share_far()
-        scatter.step(3)
         scatter.finish(branch)
         own = rows(x, me)
         own_tokens = rows(dd, me)
@@ -778,8 +830,9 @@
             residual[r, :] = value
             own[r, :] = value.astype(BF16)
 
-        gather = GatherTensor(x, *g1)
+        gather = GatherTensor(x, *gather_sems)
         gather.start()
+        down_weights.forward()
         for spread_item in large:
             spread_item.finish()
 
@@ -800,21 +853,20 @@
             if stage == 0:
                 down_weights.share()
                 down_weights.forward_far()
-            else:
+            elif stage == 1:
                 down_weights.share_far()
-
         gather.run(gate_up, spread_down)
         down_weights.finish()
 
-        def down(half, side):
-            s = pl.ds(pl.multiple_of(half * 512, 512), 512)
+        def down(first_row):
+            s = pl.ds(pl.multiple_of(first_row, 256), 256)
 
             @pl.loop(0, 2)
             def _(i):
-                n = pl.ds(pl.multiple_of(side * 1024 + i * 512, 512), 512)
+                n = pl.ds(pl.multiple_of(i * 1024, 1024), 1024)
                 part[s, n] = nn(inner[s, :], wd[:, n]).astype(BF16)
 
-        scatter = ScatterTensor(part, bufs, *s1)
+        scatter = ScatterTensor(part, bufs, *scatter_sems)
         scatter.run(down)
         for n in range(4):
             scatter.step(n)
@@ -838,7 +890,7 @@
             mean = jnp.mean(v * weighted, 1, keepdims=True)
             own_d[r, :] = (scale * weighted - v * (scale * scale * scale * mean)).astype(BF16)
 
-        gather = GatherTensor(dd, *g2)
+        gather = GatherTensor(dd, *gather_sems)
         gather.start()
         store_act = pltpu.make_async_copy(part.at[pl.ds(0, 128)], act, msem.at[1])
         store_act.start()
@@ -856,15 +908,15 @@
         store_act.wait()
         tell(0)
 
-        def d_input(half, side):
-            s = pl.ds(pl.multiple_of(half * 512, 512), 512)
+        def d_input(first_row):
+            s = pl.ds(pl.multiple_of(first_row, 256), 256)
 
             @pl.loop(0, 2)
             def _(i):
-                n = pl.ds(pl.multiple_of(side * 1024 + i * 512, 512), 512)
+                n = pl.ds(pl.multiple_of(i * 1024, 1024), 1024)
                 part[s, n] = (nt(dg[s, :], wg[n, :]) + nt(du[s, :], wu[n, :])).astype(BF16)
 
-        scatter = ScatterTensor(part, bufs, *s2)
+        scatter = ScatterTensor(part, bufs, *scatter_sems)
         scatter.run(d_input)
         scatter.step(0)
 
@@ -902,7 +954,7 @@
             ]
         )
         slots = small_slots + [by_rows(silu), by_rows(inner), by_columns(gate_factor)]
-        wholes = (wq, wk, dd, wo, wg, wu, wd)
+        wholes = (wq, wk, silu, wo, wg, wu, wd)
         scatter_kinds = kinds[:2] + ("folded",) + kinds[3:]
         items = [ScatterDp(wholes[i], scatter_kinds[i], slots[i], *dp_bufs[i]) for i in range(7)]
         qk, value_item, out_item, gate_item, up_item, down_item = items[:2], *items[2:]
@@ -912,6 +964,8 @@
         gate_grad(0)
         scatter.step(3)
         gate_grad(2)
+        down_item.along_x()
+        tell(2)
         gate_item.start()
         load_heads.start()
         scatter.finish(total)
@@ -927,12 +981,57 @@
             mean = jnp.mean(b * weighted, 1, keepdims=True)
             own_d[r, :] = (scale * weighted - b * (scale * scale * scale * mean)).astype(BF16)
 
-        gather = GatherTensor(dd, *g3, 768)
+        gather = GatherTensor(dd, *gather_sems, 768)
         gather.start()
-        down_item.along_x()
-        tell(2)
+
 
         gate_item.along_x()
+
+        @tiles(2048, 512)
+        def _(m):
+            @tiles(1024, 512)
+            def _(n):
+                wu[m, n] = tn(x[:, m], du[:, n]).astype(BF16)
+
+        reload.start()
+        load_raw.start()
+        pl.semaphore_wait(ready.at[1], 1)
+        up_item.start()
+        dk[...] = jnp.zeros_like(dk)
+        dv[...] = jnp.zeros_like(dv)
+
+        def attend_back(half):
+            for top in range(2):
+
+                @pl.when(half == top)
+                def _():
+                    @pl.loop(0, 2)
+                    def _(h):
+                        cols = pl.ds(pl.multiple_of(h * 128, 128), 128)
+                        for i in (2 * top, 2 * top + 1):
+                            low = i * 256
+                            block = slice(low, low + 256)
+                            q, d = q_rot[block, cols], do[block, cols]
+                            peak = jnp.where(h == 0, stats[block, 0:1], stats[block, 64:65])
+                            k1, v1 = k_rot[block, cols], v_low[block, cols]
+                            p1 = jnp.exp(diagonal_mask(nt(q, k1), low, length) - peak)
+                            dp1 = nt(d, v1)
+                            delta = jnp.sum(p1 * dp1, 1, keepdims=True)
+                            if i:
+                                k0, v0 = k_rot[0:low, cols], v_low[0:low, cols]
+                                p0 = jnp.exp(nt(q, k0) - peak)
+                                dp0 = nt(d, v0)
+                                delta += jnp.sum(p0 * dp0, 1, keepdims=True)
+                            ds1 = (p1 * (dp1 - delta)).astype(BF16)
+                            dq_block = nn(ds1, k1)
+                            dk[block, cols] += tn(ds1, q)
+                            dv[block, cols] += tn(p1.astype(BF16), d)
+                            if i:
+                                ds0 = (p0 * (dp0 - delta)).astype(BF16)
+                                dq_block += nn(ds0, k0)
+                                dk[0:low, cols] += tn(ds0, q)
+                                dv[0:low, cols] += tn(p0.astype(BF16), d)
+                            dq[block, cols] = dq_block
 
         def d_mixed(slot):
             s = pl.ds(pl.multiple_of(slot * 128, 128), 128)
@@ -941,63 +1040,16 @@
         def beside(stage):
             if stage == 0:
                 down_item.forward()
-
-                @tiles(2048, 512)
-                def _(m):
-                    @tiles(1024, 512)
-                    def _(n):
-                        wu[m, n] = tn(x[:, m], du[:, n]).astype(BF16)
-
-                reload.start()
-                load_raw.start()
-                pl.semaphore_wait(ready.at[1], 1)
-                up_item.start()
+                load_heads.wait()
+            elif stage == 1:
+                gate_item.forward()
+                up_item.along_x()
             else:
-                gate_item.forward()
                 down_item.along_y()
 
-        gather.run(d_mixed, beside)
-        up_item.along_x()
-        load_heads.wait()
+        gather.run(d_mixed, beside, attend_back)
         load_raw.wait()
 
-        @tiles(2048, 512)
-        def _(n):
-            wo[:, n] = tn(mixed[...], dd[:, n]).astype(BF16)
-
-        pl.semaphore_wait(ready.at[2], 1)
-        out_item.start()
-        gate_item.along_y()
-
-        @pl.loop(0, 2)
-        def _(h):
-            cols = pl.ds(pl.multiple_of(h * 128, 128), 128)
-            for i in range(4):
-                low = i * 256
-                block = slice(low, low + 256)
-                q, d = q_rot[block, cols], do[block, cols]
-                top = jnp.where(h == 0, stats[block, 0:1], stats[block, 64:65])
-                k1, v1 = k_rot[block, cols], v_low[block, cols]
-                p1 = jnp.exp(diagonal_mask(nt(q, k1), low, length) - top)
-                dp1 = nt(d, v1)
-                delta = jnp.sum(p1 * dp1, 1, keepdims=True)
-                if i:
-                    k0, v0 = k_rot[0:low, cols], v_low[0:low, cols]
-                    p0 = jnp.exp(nt(q, k0) - top)
-                    dp0 = nt(d, v0)
-                    delta += jnp.sum(p0 * dp0, 1, keepdims=True)
-                ds1 = (p1 * (dp1 - delta)).astype(BF16)
-                dq_block = nn(ds1, k1)
-                dk[block, cols] = tn(ds1, q)
-                dv[block, cols] = tn(p1.astype(BF16), d)
-                if i:
-                    ds0 = (p0 * (dp0 - delta)).astype(BF16)
-                    dq_block += nn(ds0, k0)
-                    dk[0:low, cols] += tn(ds0, q)
-                    dv[0:low, cols] += tn(p0.astype(BF16), d)
-                dq[block, cols] = dq_block
-
-        up_item.forward()
         q_line[...] = jnp.zeros_like(q_line)
         k_line[...] = jnp.zeros_like(k_line)
         sums[me] = jnp.zeros((8, 256), F32)
@@ -1024,7 +1076,7 @@
             )
             dvr[r, :] = dv[r, :].astype(BF16)
 
-        exchange = Exchange(sums, *fsems)
+        exchange = Exchange(sums, *sum_sems)
         exchange.start()
         reload.wait()
         row = lax.broadcasted_iota(jnp.int32, (8, 1024), 0)
@@ -1044,12 +1096,13 @@
             m = pl.ds(pl.multiple_of(i * 512, 512), 512)
             r = pl.ds(pl.multiple_of(lax.rem(i, 2) * 512, 512), 512)
             columns = pl.ds(pl.multiple_of(i // 2 * 256, 256), 256)
-            dd[r, columns] = tn(x[:, m], dvr[...]).astype(BF16)
-
+            silu[r, columns] = tn(x[:, m], dvr[...]).astype(BF16)
+
+        pl.semaphore_wait(ready.at[2], 1)
         value_item.start()
-        out_item.along_x()
         exchange.finish()
         total_gain.start()
+        gate_item.along_y()
         spread(dv, exchange.sum() * (1.0 / 2048))
 
         @tiles(1024, 256)
@@ -1063,20 +1116,22 @@
                         - rawer[r, h : h + 128].astype(F32) * factor
                     ).astype(BF16)
 
-        def d_tokens(half, side):
-            s = pl.ds(pl.multiple_of(half * 512, 512), 512)
+        def d_tokens(first_row):
+            s = pl.ds(pl.multiple_of(first_row, 256), 256)
 
             @pl.loop(0, 2)
             def _(i):
-                n = pl.ds(pl.multiple_of(side * 1024 + i * 512, 512), 512)
+                n = pl.ds(pl.multiple_of(i * 1024, 1024), 1024)
                 terms = nt(dqr[s, :], wq[n, :]) + nt(dkr[s, :], wk[n, :]) + nt(dvr[s, :], wv[n, :])
                 part[s, n] = terms.astype(BF16)
 
-        scatter = ScatterTensor(part, bufs, *s3)
+        scatter = ScatterTensor(part, bufs, *scatter_sems, 512)
         scatter.run(d_tokens)
-        up_item.along_y()
+        up_item.forward()
+        total_gain.core()
+        scatter.step(0)
         value_item.along_x()
-        scatter.step(0)
+        total_gain.along_x()
 
         @tiles(2048, 512)
         def _(m):
@@ -1086,19 +1141,28 @@
 
         for item in qk:
             item.start()
-        out_item.forward()
-        total_gain.core()
-        scatter.step(1)
+
+        @tiles(2048, 512)
+        def _(n):
+            wo[:, n] = tn(mixed[...], dd[:, n]).astype(BF16)
+
+        out_item.start()
         for item in qk:
             item.along_x()
+        scatter.step(1)
+        out_item.along_x()
+        up_item.along_y()
+        total_gain.along_y()
         value_item.forward()
-        total_gain.along_x()
         scatter.step(2)
-        out_item.along_y()
-        scatter.step(3)
         for item in qk:
             item.forward()
-        total_gain.along_y()
+        out_item.forward()
+        scatter.step(3)
+        value_item.along_y()
+        for item in qk:
+            item.along_y()
+        out_item.along_y()
         stores = []
 
         def store(item, source, target):
@@ -1108,17 +1172,13 @@
 
         store(down_item, dv.at[:, pl.ds(0, 128)], o6)
         gate_item.finish(o4)
-        up_item.finish(o5)
-        value_item.along_y()
-        store(out_item, dv.at[pl.ds(0, 256), pl.ds(128, 128)], o3)
         scatter.finish(input_grad)
 
         @tiles(128, 16)
         def _(r):
             input_grad[r, :] += residual[r, :]
 
-        for item in qk:
-            item.along_y()
+        up_item.finish(o5)
         total_gain.finish(gain_slots.at[0])
         for i, out in enumerate((q_sum, k_sum, attn_sum, mlp_sum)):
             out[:, 0:1024] = gain_slots[0, 2 * i : 2 * i + 1, :]
@@ -1126,6 +1186,7 @@
         store(value_item, dk.at[pl.ds(256, 128)], o2)
         for i, out in enumerate((o0, o1)):
             store(qk[i], dk.at[pl.ds(128 * i, 128)], out)
+        store(out_item, dv.at[pl.ds(0, 256), pl.ds(128, 128)], o3)
         for copy in stores:
             copy.wait()
 
@@ -1138,12 +1199,11 @@
     scratch += [W((1024, 256), F32), W((128, 2048), F32), W((1024, 256), BF16)]
     scratch += [W((1024, 256), F32)] * 3
     scratch += [W((8, 8, 256), F32), W((8, 8, 1024), F32)] + [W((3, 8, 1024), F32), W((5, 8, 1024), F32)]
-    scratch += ScatterTensor.scratch()
+    scratch += ScatterTensor.scratch(512, CUT)
     for b in blocks:
         scratch += ScatterDp.scratch(b)
-    for n in (23, 23, 23, 23, 21, 21, 21, 21, 7, 7, 12):
-        scratch += [DMA((n,))] * 2
-    scratch += [DMA((7, 21))] * 2
+    scratch += [DMA, DMA((23,)), DMA, DMA((21,)), DMA, DMA((7,)), DMA((6,)), DMA((12,))]
+    scratch += [DMA((7,)), DMA((7, 14))]
     scratch += [DMA((8,)), DMA((4,)), pltpu.SemaphoreType.REGULAR((3,))]
     return pl.pallas_call(
         layer_step,

time: 315 us -> 296 us (0.940)
  Pallas kernels: 313 us -> 294 us
    pallas_call x1, Pallas kernels: 310 us -> 291 us  [whole_layer(): pl.pallas_call(layer_step, out_shape=[S((128, 2048), BF16), S((128, 2048)...]
where the time goes in v4:
time: 296 us
  Pallas kernels  294 us (99%)
    pallas_call x1, Pallas kernels, whole_layer(): pl.pallas_call(layer_step, out_shape=[S((128, 2048), BF16), S((128, 2048)...  291 us

profile of v4, /device:TPU:0, one launch (start us, length us, event | category | flops | bytes accessed | tf_op | source)
XLA Modules:
  0.0 295.7 jit_solution(8190766679667918303)
XLA Ops:
  1.3 291.0 %layer_step.1 = (bf16[128,2048]{1,0:T(8,128)(2,1)}, f32[128,2048]{1,0:T(8,128)}, f32[128,256]{1,0:T(8,128)}, f32[128,256]{1,0:T(8,128)}, f32[128,256]{1,0:T(8,12...) custom-call(s32[1]{0:T(128)S(6)} %copy.28.lengths, ...), custom_call_target="tpu_custom_call" | custom-call | tf_op jit(solution)/shard_map/layer_step/pallas_call | solution.py:1208
  292.3 3.3 %hand_over_step.1 = (bf16[128,2048]{1,0:T(8,128)(2,1)}, f32[128,2048]{1,0:T(8,128)}, f32[128,256]{1,0:T(8,128)}, f32[128,256]{1,0:T(8,128)}, f32[128,256]{1,0:T(...) custom-call(bf16[128,2048]{1,0:T(8,128)(2,1)} %get-tuple-element.39., ...), custom_call_target="tpu_custom_call" | custom-call | tf_op jit(solution)/shard_map/hand_over_step/pallas_call | solution.py:1237

commit v5 on v4

--- a/solution.py
+++ b/solution.py
@@ -185,7 +185,7 @@
         self.low[0].start()
         self.low[1].start()
 
-    def run(self, process, spare=None, by_half=None, early=None):
+    def run(self, process, spare=None, by_block=None, early=None, first=3):
         yl, z = self.yl, self.z
 
         @pl.loop(0, 2)
@@ -211,15 +211,28 @@
         if spare is not None:
             spare(0)
 
-        @pl.loop(0, 6 if by_half is None else 7)
+        @pl.loop(0, 6 if by_block is None else 7)
         def _(j):
-            if by_half is not None:
-
-                @pl.when(lax.rem(j, 3) == 0)
+            if spare is not None:
+                for stage, at in ((1, 3), (2, 5)):
+
+                    @pl.when(j == at)
+                    def _():
+                        spare(stage)
+
+            if by_block is not None:
+                last = j // 6
+                rest = 2 - 2 * yl + last * (1 - z // 2) + (1 - last) * (z // 2)
+
+                @pl.when((j >= 5) | (j == first))
                 def _():
-                    @pl.when(j > 0)
-                    def _():
-                        by_half(lax.rem(yl + j // 6, 2))
+                    @pl.loop(0, 3)
+                    def _(t):
+                        third = t // 2
+
+                        @pl.when(((t < 2) & (j == first)) | ((t == 2) & (j >= 5)))
+                        def _():
+                            by_block((1 - third) * (2 * yl + t) + third * rest)
 
             @pl.when(j == 2)
             def _():
@@ -230,8 +243,6 @@
 
             @pl.when(j == 3)
             def _():
-                if spare is not None:
-                    spare(1)
                 self.pair_ring.behind()
                 self.low[2].wait_recv()
                 self.low[3].wait_recv()
@@ -244,8 +255,6 @@
 
             @pl.when(j == 5)
             def _():
-                if spare is not None:
-                    spare(2)
                 self.pair_ring.far()
                 self.low[6].wait_recv()
                 self.low[7].wait_recv()
@@ -298,18 +307,12 @@
         self.first = lambda i: remote(low(1, i), bufs[0].at[i], sems, 18 + i, pair)
         self.second = remote(high(1, 0), bufs[1], sems, 22, pair)
 
-    def run(self, process, before=None):
+    def run(self, process):
         yl, z = self.yl, self.z
 
         @pl.loop(0, 4)
         def _(k):
             half = lax.rem(yl + 1 + k // 2, 2)
-            if before is not None:
-
-                @pl.when(lax.rem(k, 2) == 0)
-                def _():
-                    before(half)
-
             process(half * 512 + lax.rem((z + 2) // 2 + k, 2) * 256)
             beside = 3 - 2 * lax.rem(z, 2)
 
@@ -658,7 +661,7 @@
         act, input_grad, o0, o1, o2, o3, o4, o5, o6,
         q_sum, k_sum, attn_sum, mlp_sum, x_kept, heads_kept, raw_kept,
         x, dd, wg, wu, wd, gate_factor, silu, inner, dg, du, part, residual, attn_part, mlp_part, q_line, k_line,
-        wq, wk, wv, wo, stats, branch, do, dq, dk, dv, sums, gain_slots, gain_hold, gain_boxes,
+        wq, wk, wv, wo, stats, branch, total, gate_out, up_out, do, dq, dk, dv, sums, gain_slots, gain_hold, gain_boxes,
         *rest,
     ):
         bufs, rest = rest[:8], rest[8:]
@@ -670,7 +673,6 @@
         yh, xx, c, yl, z = place()
         me = yl * 4 + z
         length = lengths[0]
-        total = input_grad
         own_columns = pl.ds(pl.multiple_of(me * 256, 256), 256)
         q_gain, k_gain = q_gain_all[:, own_columns], k_gain_all[:, own_columns]
         q_rot, k_rot, v_low, mixed = (dg.at[:, pl.ds(256 * i, 256)] for i in range(4))
@@ -697,8 +699,10 @@
             spread_item.start()
             spread_item.own_y.start()
         first.wait()
-        gather = GatherTensor(dd, *gather_sems, 640)
+        gather = GatherTensor(dd, *gather_sems, 384)
         gather.start()
+
+        sums[me] = jnp.zeros((8, 256), F32)
 
         def forward_small():
             for spread_item in small:
@@ -712,20 +716,17 @@
                     spread_item.forward_far()
                 elif stage == 1:
                     spread_item.share_far()
+                else:
+                    spread_item.finish()
+            if stage == 1:
+                down_weights.own_y.start()
             if stage == 2:
-                down_weights.own_y.start()
-
-        gather.run(lambda slot: None, spread_small, early=forward_small)
-        for spread_item in large:
-            spread_item.start()
-        large[0].own_y.start()
-        for spread_item in small:
-            spread_item.finish()
-        sums[me] = jnp.zeros((8, 256), F32)
-        keep_x.start()
-
-        @tiles(1024, 256)
-        def _(r):
+                for spread_item in large:
+                    spread_item.start()
+                large[0].own_y.start()
+
+        def heads(i):
+            r = pl.ds(pl.multiple_of(i * 256, 256), 256)
             q = nn(dd[r, :], wq[...])
             k = nn(dd[r, :], wk[...])
             dq[r, :] = q
@@ -735,6 +736,8 @@
             v_low[r, :] = nn(dd[r, :], wv[...]).astype(BF16)
             note_sums(sums.at[me], r, q * q, k * k)
 
+        gather.run(lambda slot: None, spread_small, heads, forward_small, 5)
+        keep_x.start()
         exchange = Exchange(sums, *sum_sems)
         exchange.start()
         keep_raw.start()
@@ -760,36 +763,36 @@
                     v = v * cos + pltpu.roll(v, 64, 1) * sin
                     target[r, h : h + 128] = (v * factor).astype(BF16)
 
-        def attend(half):
-            for top in range(2):
-
-                @pl.when(half == top)
+        def attend(wanted):
+            for i in range(4):
+
+                @pl.when(wanted == i)
                 def _():
                     @pl.loop(0, 2)
                     def _(h):
                         cols = pl.ds(pl.multiple_of(h * 128, 128), 128)
                         mine = lax.broadcasted_iota(jnp.int32, (256, 128), 1) // 64 == h
-                        for i in (2 * top, 2 * top + 1):
-                            low = i * 256
-                            block = slice(low, low + 256)
-                            q = q_rot[block, cols]
-                            near = diagonal_mask(nt(q, k_rot[block, cols]), low, length)
-                            peak = jnp.max(near, 1, keepdims=True)
-                            if i:
-                                past = nt(q, k_rot[0:low, cols])
-                                peak = jnp.maximum(peak, jnp.max(past, 1, keepdims=True))
-                            e1 = jnp.exp(near - peak)
-                            denom = jnp.sum(e1, 1, keepdims=True)
-                            out = nn(e1.astype(BF16), v_low[block, cols])
-                            if i:
-                                e0 = jnp.exp(past - peak)
-                                denom += jnp.sum(e0, 1, keepdims=True)
-                                out += nn(e0.astype(BF16), v_low[0:low, cols])
-                            mixed[block, cols] = (out / denom).astype(BF16)
-                            lse = peak + jnp.log(denom)
-                            stats[block, 0:128] = jnp.where(mine, lse, stats[block, 0:128])
+                        low = i * 256
+                        block = slice(low, low + 256)
+                        q = q_rot[block, cols]
+                        near = diagonal_mask(nt(q, k_rot[block, cols]), low, length)
+                        peak = jnp.max(near, 1, keepdims=True)
+                        if i:
+                            past = nt(q, k_rot[0:low, cols])
+                            peak = jnp.maximum(peak, jnp.max(past, 1, keepdims=True))
+                        e1 = jnp.exp(near - peak)
+                        denom = jnp.sum(e1, 1, keepdims=True)
+                        out = nn(e1.astype(BF16), v_low[block, cols])
+                        if i:
+                            e0 = jnp.exp(past - peak)
+                            denom += jnp.sum(e0, 1, keepdims=True)
+                            out += nn(e0.astype(BF16), v_low[0:low, cols])
+                        mixed[block, cols] = (out / denom).astype(BF16)
+                        lse = peak + jnp.log(denom)
+                        stats[block, 0:128] = jnp.where(mine, lse, stats[block, 0:128])
 
         def project(first_row):
+            attend(first_row // 256)
             s = pl.ds(pl.multiple_of(first_row, 256), 256)
 
             @pl.loop(0, 2)
@@ -798,7 +801,7 @@
                 part[s, n] = nn(mixed[s, :], wo[:, n]).astype(BF16)
 
         scatter = ScatterTensor(part, bufs, *scatter_sems)
-        scatter.run(project, attend)
+        scatter.run(project)
         keep_heads.start()
         large[1].forward_y()
         scatter.step(0)
@@ -964,10 +967,10 @@
         gate_grad(0)
         scatter.step(3)
         gate_grad(2)
+        gate_item.start()
+        load_heads.start()
         down_item.along_x()
         tell(2)
-        gate_item.start()
-        load_heads.start()
         scatter.finish(total)
 
         @tiles(128, 16)
@@ -985,8 +988,6 @@
         gather.start()
 
 
-        gate_item.along_x()
-
         @tiles(2048, 512)
         def _(m):
             @tiles(1024, 512)
@@ -995,43 +996,43 @@
 
         reload.start()
         load_raw.start()
+        gate_item.along_x()
         pl.semaphore_wait(ready.at[1], 1)
         up_item.start()
         dk[...] = jnp.zeros_like(dk)
         dv[...] = jnp.zeros_like(dv)
 
-        def attend_back(half):
-            for top in range(2):
-
-                @pl.when(half == top)
+        def attend_back(wanted):
+            for i in range(4):
+
+                @pl.when(wanted == i)
                 def _():
                     @pl.loop(0, 2)
                     def _(h):
                         cols = pl.ds(pl.multiple_of(h * 128, 128), 128)
-                        for i in (2 * top, 2 * top + 1):
-                            low = i * 256
-                            block = slice(low, low + 256)
-                            q, d = q_rot[block, cols], do[block, cols]
-                            peak = jnp.where(h == 0, stats[block, 0:1], stats[block, 64:65])
-                            k1, v1 = k_rot[block, cols], v_low[block, cols]
-                            p1 = jnp.exp(diagonal_mask(nt(q, k1), low, length) - peak)
-                            dp1 = nt(d, v1)
-                            delta = jnp.sum(p1 * dp1, 1, keepdims=True)
-                            if i:
-                                k0, v0 = k_rot[0:low, cols], v_low[0:low, cols]
-                                p0 = jnp.exp(nt(q, k0) - peak)
-                                dp0 = nt(d, v0)
-                                delta += jnp.sum(p0 * dp0, 1, keepdims=True)
-                            ds1 = (p1 * (dp1 - delta)).astype(BF16)
-                            dq_block = nn(ds1, k1)
-                            dk[block, cols] += tn(ds1, q)
-                            dv[block, cols] += tn(p1.astype(BF16), d)
-                            if i:
-                                ds0 = (p0 * (dp0 - delta)).astype(BF16)
-                                dq_block += nn(ds0, k0)
-                                dk[0:low, cols] += tn(ds0, q)
-                                dv[0:low, cols] += tn(p0.astype(BF16), d)
-                            dq[block, cols] = dq_block
+                        low = i * 256
+                        block = slice(low, low + 256)
+                        q, d = q_rot[block, cols], do[block, cols]
+                        peak = jnp.where(h == 0, stats[block, 0:1], stats[block, 64:65])
+                        k1, v1 = k_rot[block, cols], v_low[block, cols]
+                        p1 = jnp.exp(diagonal_mask(nt(q, k1), low, length) - peak)
+                        dp1 = nt(d, v1)
+                        delta = jnp.sum(p1 * dp1, 1, keepdims=True)
+                        if i:
+                            k0, v0 = k_rot[0:low, cols], v_low[0:low, cols]
+                            p0 = jnp.exp(nt(q, k0) - peak)
+                            dp0 = nt(d, v0)
+                            delta += jnp.sum(p0 * dp0, 1, keepdims=True)
+                        ds1 = (p1 * (dp1 - delta)).astype(BF16)
+                        dq_block = nn(ds1, k1)
+                        dk[block, cols] += tn(ds1, q)
+                        dv[block, cols] += tn(p1.astype(BF16), d)
+                        if i:
+                            ds0 = (p0 * (dp0 - delta)).astype(BF16)
+                            dq_block += nn(ds0, k0)
+                            dk[0:low, cols] += tn(ds0, q)
+                            dv[0:low, cols] += tn(p0.astype(BF16), d)
+                        dq[block, cols] = dq_block
 
         def d_mixed(slot):
             s = pl.ds(pl.multiple_of(slot * 128, 128), 128)
@@ -1125,13 +1126,12 @@
                 terms = nt(dqr[s, :], wq[n, :]) + nt(dkr[s, :], wk[n, :]) + nt(dvr[s, :], wv[n, :])
                 part[s, n] = terms.astype(BF16)
 
-        scatter = ScatterTensor(part, bufs, *scatter_sems, 512)
+        scatter = ScatterTensor(part, bufs, *scatter_sems, 640)
         scatter.run(d_tokens)
         up_item.forward()
         total_gain.core()
         scatter.step(0)
         value_item.along_x()
-        total_gain.along_x()
 
         @tiles(2048, 512)
         def _(m):
@@ -1147,22 +1147,20 @@
             wo[:, n] = tn(mixed[...], dd[:, n]).astype(BF16)
 
         out_item.start()
+        total_gain.along_x()
+        scatter.step(2)
+        value_item.forward()
         for item in qk:
             item.along_x()
         scatter.step(1)
         out_item.along_x()
         up_item.along_y()
         total_gain.along_y()
-        value_item.forward()
-        scatter.step(2)
+        scatter.step(3)
         for item in qk:
             item.forward()
         out_item.forward()
-        scatter.step(3)
         value_item.along_y()
-        for item in qk:
-            item.along_y()
-        out_item.along_y()
         stores = []
 
         def store(item, source, target):
@@ -1171,14 +1169,19 @@
             stores[-1].start()
 
         store(down_item, dv.at[:, pl.ds(0, 128)], o6)
-        gate_item.finish(o4)
-        scatter.finish(input_grad)
+        store(gate_item, gate_out, o4)
+        for item in qk:
+            item.along_y()
+        out_item.along_y()
+        scatter.finish(total)
 
         @tiles(128, 16)
         def _(r):
-            input_grad[r, :] += residual[r, :]
-
-        up_item.finish(o5)
+            total[r, :] += residual[r, :]
+
+        stores.append(pltpu.make_async_copy(total, input_grad, lsem.at[len(stores)]))
+        stores[-1].start()
+        store(up_item, up_out, o5)
         total_gain.finish(gain_slots.at[0])
         for i, out in enumerate((q_sum, k_sum, attn_sum, mlp_sum)):
             out[:, 0:1024] = gain_slots[0, 2 * i : 2 * i + 1, :]
@@ -1196,10 +1199,11 @@
     scratch += [W((1024, 1024), BF16)] * 5 + [W((1024, 2048), BF16)]
     scratch += [W((128, 2048), F32)] + [W((1, 2048), F32)] * 2 + [W((1, 256), F32)] * 2
     scratch += [W((2048, 256), BF16)] * 3 + [W((256, 2048), BF16)]
-    scratch += [W((1024, 256), F32), W((128, 2048), F32), W((1024, 256), BF16)]
+    scratch += [W((1024, 256), F32)] + [W((128, 2048), F32)] * 2
+    scratch += [W((128, 1024), F32)] * 2 + [W((1024, 256), BF16)]
     scratch += [W((1024, 256), F32)] * 3
     scratch += [W((8, 8, 256), F32), W((8, 8, 1024), F32)] + [W((3, 8, 1024), F32), W((5, 8, 1024), F32)]
-    scratch += ScatterTensor.scratch(512, CUT)
+    scratch += ScatterTensor.scratch(640, CUT)
     for b in blocks:
         scratch += ScatterDp.scratch(b)
     scratch += [DMA, DMA((23,)), DMA, DMA((21,)), DMA, DMA((7,)), DMA((6,)), DMA((12,))]
@@ -1212,7 +1216,7 @@
         + [S((1, 2048), F32)] * 4
         + [S((1024, 2048), BF16), S((1024, 1024), BF16), S((1024, 512), BF16)],
         in_specs=[SMEM] + [VM] * 6 + [ANY] * 8,
-        out_specs=[ANY, VM] + [ANY] * 4 + [VM] * 2 + [ANY] + [VM] * 4 + [ANY] * 3,
+        out_specs=[ANY] * 9 + [VM] * 4 + [ANY] * 3,
         scratch_shapes=scratch,
         compiler_params=params(1),
         name="layer_step",

time: 296 us -> 288 us (0.973)
  Pallas kernels: 294 us -> 286 us
    pallas_call x1, Pallas kernels: 291 us -> 283 us  [whole_layer(): pl.pallas_call(layer_step, out_shape=[S((128, 2048), BF16), S((128, 2048)...]
where the time goes in v5:
time: 288 us
  Pallas kernels  286 us (99%)
    pallas_call x1, Pallas kernels, whole_layer(): pl.pallas_call(layer_step, out_shape=[S((128, 2048), BF16), S((128, 2048)...  283 us

profile of v5, /device:TPU:0, one launch (start us, length us, event | category | flops | bytes accessed | tf_op | source)
XLA Modules:
  0.0 288.0 jit_solution(16894042543706949397)
XLA Ops:
  1.3 283.2 %layer_step.1 = (bf16[128,2048]{1,0:T(8,128)(2,1)}, f32[128,2048]{1,0:T(8,128)}, f32[128,256]{1,0:T(8,128)}, f32[128,256]{1,0:T(8,128)}, f32[128,256]{1,0:T(8,12...) custom-call(s32[1]{0:T(128)S(6)} %copy.28.lengths, ...), custom_call_target="tpu_custom_call" | custom-call | tf_op jit(solution)/shard_map/layer_step/pallas_call | solution.py:1212
  284.5 3.3 %hand_over_step.1 = (bf16[128,2048]{1,0:T(8,128)(2,1)}, f32[128,2048]{1,0:T(8,128)}, f32[128,256]{1,0:T(8,128)}, f32[128,256]{1,0:T(8,128)}, f32[128,256]{1,0:T(...) custom-call(bf16[128,2048]{1,0:T(8,128)(2,1)} %get-tuple-element.39., ...), custom_call_target="tpu_custom_call" | custom-call | tf_op jit(solution)/shard_map/hand_over_step/pallas_call | solution.py:1241

commit v6 on v5

--- a/solution.py
+++ b/solution.py
@@ -134,13 +134,14 @@
         from_behind, from_ahead = halves(full.at[0]), halves(full.at[1])
         self.adds = ((one[0], part.at[0]), (three[1], part.at[1]))
         self.terms = (block(0), full.at[0], full.at[1])
+        self.full, self.full_sem = full, sems[1].at[base + 2]
         self.copies = [
             remote(two[0], part.at[0], sems, base, up),
             remote(two[1], part.at[1], sems, base + 1, down),
             remote(one[1], from_behind[1], sems, base + 2, up),
-            remote(three[0], from_ahead[0], sems, base + 3, down),
-            remote(one[0], from_behind[0], sems, base + 4, up),
-            remote(three[1], from_ahead[1], sems, base + 5, down),
+            remote(three[0], from_ahead[0], sems, base + 2, down),
+            remote(one[0], from_behind[0], sems, base + 2, up),
+            remote(three[1], from_ahead[1], sems, base + 2, down),
         ]
 
     def start(self):
@@ -154,8 +155,7 @@
             self.copies[4 + i].start()
 
     def arrive(self):
-        for copy in self.copies[2:]:
-            copy.wait_recv()
+        all_of(self.full, self.full_sem)
 
 
 class GatherTensor:
@@ -302,10 +302,10 @@
         pair = dict(dyl=1)
         self.low = lambda i: low(0, i)
         self.low_ring = RingReduce(lambda i: low(0, i), "dz", bufs[2], bufs[3], sems, 0)
-        self.pair_ring = RingReduce(lambda i: high(1, i), "dz", bufs[4], bufs[5], sems, 6)
-        self.own_ring = RingReduce(lambda i: high(0, i), "dz", bufs[6], bufs[7], sems, 12)
-        self.first = lambda i: remote(low(1, i), bufs[0].at[i], sems, 18 + i, pair)
-        self.second = remote(high(1, 0), bufs[1], sems, 22, pair)
+        self.pair_ring = RingReduce(lambda i: high(1, i), "dz", bufs[4], bufs[5], sems, 3)
+        self.own_ring = RingReduce(lambda i: high(0, i), "dz", bufs[6], bufs[7], sems, 6)
+        self.first = lambda i: remote(low(1, i), bufs[0].at[i], sems, 9 + i, pair)
+        self.second = remote(high(1, 0), bufs[1], sems, 13, pair)
 
     def run(self, process):
         yl, z = self.yl, self.z
@@ -459,7 +459,7 @@
         return (
             [pltpu.VMEM(block, BF16)]
             + RingReduce.scratch(*block) * 2
-            + [DMA, DMA((14,))]
+            + [DMA, DMA((8,))]
         )
 
     def __init__(self, part, kind, from_core, from_y, h0, f0, h1, f1, ssem, rsem):
@@ -476,8 +476,8 @@
             for n in range(8)
         ]
         self.ring = RingReduce(lambda i: block(0, i, c), "dx", h0, f0, sems, 1)
-        self.far_ring = RingReduce(lambda i: block(1, i, c), "dx", h1, f1, sems, 7)
-        self.last = remote(block(1, 0, c), from_y, sems, 13, dict(dyh=1))
+        self.far_ring = RingReduce(lambda i: block(1, i, c), "dx", h1, f1, sems, 4)
+        self.last = remote(block(1, 0, c), from_y, sems, 7, dict(dyh=1))
         self.shared, self.shared_sem = some_of(part, kind, 8), rsem.at[0]
 
     def start(self):
@@ -656,12 +656,11 @@
     blocks = ((128, 256),) * 3 + ((256, 128), (128, 1024), (128, 1024), (1024, 128))
 
     def layer_step(
-        lengths, cotangent, q_gain_all, k_gain_all, attn_gain, mlp_gain, table,
-        tokens, i0, i1, i2, i3, i4, i5, i6,
+        lengths, q_gain_all, k_gain_all, attn_gain, mlp_gain, tokens, cotangent_in, table_in, i0, i1, i2, i3, i4, i5, i6,
         act, input_grad, o0, o1, o2, o3, o4, o5, o6,
         q_sum, k_sum, attn_sum, mlp_sum, x_kept, heads_kept, raw_kept,
         x, dd, wg, wu, wd, gate_factor, silu, inner, dg, du, part, residual, attn_part, mlp_part, q_line, k_line,
-        wq, wk, wv, wo, stats, branch, total, gate_out, up_out, do, dq, dk, dv, sums, gain_slots, gain_hold, gain_boxes,
+        wq, wk, wv, wo, stats, branch, cotangent, table, gain_lines, total, gate_out, up_out, do, dq, dk, dv, sums, gain_slots, gain_hold, gain_boxes,
         *rest,
     ):
         bufs, rest = rest[:8], rest[8:]
@@ -687,6 +686,10 @@
         keep_raw = pltpu.make_async_copy(raw, raw_kept, msem.at[2])
         first = pltpu.make_async_copy(tokens, rows(dd, me), msem.at[3])
         first.start()
+        load_table = pltpu.make_async_copy(table_in, table, msem.at[4])
+        load_cotangent = pltpu.make_async_copy(cotangent_in, cotangent, msem.at[5])
+        load_table.start()
+        load_cotangent.start()
         greet(ALL_PEERS)
         shards = (i0, i1, i2, i3, i4, i5, i6)
         targets = (wq, wk, wv, wo, wg, wu, wd)
@@ -741,6 +744,8 @@
         exchange = Exchange(sums, *sum_sems)
         exchange.start()
         keep_raw.start()
+        load_table.wait()
+        load_cotangent.wait()
         exchange.finish()
         large[1].own_y.start()
         for spread_item in large:
@@ -825,7 +830,7 @@
         def tell(i):
             pl.semaphore_signal(ready.at[i], 1, device_id=other(dc=1), device_id_type=MESH)
 
-        @tiles(128, 16)
+        @tiles(128, 32)
         def _(r):
             b = branch[r, :]
             scale = lax.rsqrt(jnp.mean(b * b, 1, keepdims=True) + EPS)
@@ -878,10 +883,10 @@
         attn_part[...] = jnp.zeros_like(attn_part)
         own_d = rows(dd, me)
 
-        @tiles(128, 16)
+        @tiles(128, 32)
         def _(r):
             v = total[r, :]
-            position = lax.broadcasted_iota(jnp.int32, (16, 1), 0) + (me * 128 + r.start)
+            position = lax.broadcasted_iota(jnp.int32, (32, 1), 0) + (me * 128 + r.start)
             ok = position < length
             scale = lax.rsqrt(jnp.mean(v * v, 1, keepdims=True) + EPS)
             normal = v * scale
@@ -973,7 +978,7 @@
         tell(2)
         scatter.finish(total)
 
-        @tiles(128, 16)
+        @tiles(128, 32)
         def _(r):
             grad = residual[r, :] + total[r, :]
             residual[r, :] = grad
@@ -1129,9 +1134,6 @@
         scatter = ScatterTensor(part, bufs, *scatter_sems, 640)
         scatter.run(d_tokens)
         up_item.forward()
-        total_gain.core()
-        scatter.step(0)
-        value_item.along_x()
 
         @tiles(2048, 512)
         def _(m):
@@ -1141,26 +1143,29 @@
 
         for item in qk:
             item.start()
+        scatter.step(0)
+        value_item.along_x()
+        total_gain.core()
 
         @tiles(2048, 512)
         def _(n):
             wo[:, n] = tn(mixed[...], dd[:, n]).astype(BF16)
 
         out_item.start()
-        total_gain.along_x()
         scatter.step(2)
         value_item.forward()
         for item in qk:
             item.along_x()
         scatter.step(1)
+        total_gain.along_x()
         out_item.along_x()
         up_item.along_y()
-        total_gain.along_y()
         scatter.step(3)
         for item in qk:
             item.forward()
         out_item.forward()
         value_item.along_y()
+        total_gain.along_y()
         stores = []
 
         def store(item, source, target):
@@ -1175,7 +1180,7 @@
         out_item.along_y()
         scatter.finish(total)
 
-        @tiles(128, 16)
+        @tiles(128, 32)
         def _(r):
             total[r, :] += residual[r, :]
 
@@ -1184,8 +1189,10 @@
         store(up_item, up_out, o5)
         total_gain.finish(gain_slots.at[0])
         for i, out in enumerate((q_sum, k_sum, attn_sum, mlp_sum)):
-            out[:, 0:1024] = gain_slots[0, 2 * i : 2 * i + 1, :]
-            out[:, 1024:2048] = gain_slots[0, 2 * i + 1 : 2 * i + 2, :]
+            gain_lines[i, :, 0:1024] = gain_slots[0, 2 * i : 2 * i + 1, :]
+            gain_lines[i, :, 1024:2048] = gain_slots[0, 2 * i + 1 : 2 * i + 2, :]
+            stores.append(pltpu.make_async_copy(gain_lines.at[i], out, lsem.at[len(stores)]))
+            stores[-1].start()
         store(value_item, dk.at[pl.ds(256, 128)], o2)
         for i, out in enumerate((o0, o1)):
             store(qk[i], dk.at[pl.ds(128 * i, 128)], out)
@@ -1199,28 +1206,29 @@
     scratch += [W((1024, 1024), BF16)] * 5 + [W((1024, 2048), BF16)]
     scratch += [W((128, 2048), F32)] + [W((1, 2048), F32)] * 2 + [W((1, 256), F32)] * 2
     scratch += [W((2048, 256), BF16)] * 3 + [W((256, 2048), BF16)]
-    scratch += [W((1024, 256), F32)] + [W((128, 2048), F32)] * 2
+    scratch += [W((1024, 256), F32), W((128, 2048), F32), W((128, 2048), BF16)]
+    scratch += [W((1024, 128), F32), W((4, 1, 2048), F32), W((128, 2048), F32)]
     scratch += [W((128, 1024), F32)] * 2 + [W((1024, 256), BF16)]
     scratch += [W((1024, 256), F32)] * 3
     scratch += [W((8, 8, 256), F32), W((8, 8, 1024), F32)] + [W((3, 8, 1024), F32), W((5, 8, 1024), F32)]
     scratch += ScatterTensor.scratch(640, CUT)
     for b in blocks:
         scratch += ScatterDp.scratch(b)
-    scratch += [DMA, DMA((23,)), DMA, DMA((21,)), DMA, DMA((7,)), DMA((6,)), DMA((12,))]
+    scratch += [DMA, DMA((14,)), DMA, DMA((21,)), DMA, DMA((7,)), DMA((6,)), DMA((12,))]
     scratch += [DMA((7,)), DMA((7, 14))]
-    scratch += [DMA((8,)), DMA((4,)), pltpu.SemaphoreType.REGULAR((3,))]
+    scratch += [DMA((12,)), DMA((6,)), pltpu.SemaphoreType.REGULAR((3,))]
     return pl.pallas_call(
         layer_step,
         out_shape=[S((128, 2048), BF16), S((128, 2048), F32)]
         + [S(b, F32) for b in blocks]
         + [S((1, 2048), F32)] * 4
         + [S((1024, 2048), BF16), S((1024, 1024), BF16), S((1024, 512), BF16)],
-        in_specs=[SMEM] + [VM] * 6 + [ANY] * 8,
-        out_specs=[ANY] * 9 + [VM] * 4 + [ANY] * 3,
+        in_specs=[SMEM] + [VM] * 4 + [ANY] * 10,
+        out_specs=[ANY] * 16,
         scratch_shapes=scratch,
         compiler_params=params(1),
         name="layer_step",
-    )(lengths, cotangent, *gains, table, tokens, *weights)[:13]
+    )(lengths, *gains, tokens, cotangent, table, *weights)[:13]
 
 
 def hand_over(*arrays):

time: 288 us -> 284 us (0.986)
  Pallas kernels: 286 us -> 282 us
    pallas_call x1, Pallas kernels: 283 us -> 279 us  [whole_layer(): pl.pallas_call(layer_step, out_shape=[S((128, 2048), BF16), S((128, 2048)...]
where the time goes in v6:
time: 284 us; the launch traced here: 283 us
  Pallas kernels  282 us (99%)
    pallas_call x1, Pallas kernels, whole_layer(): pl.pallas_call(layer_step, out_shape=[S((128, 2048), BF16), S((128, 2048)...  279 us

profile of v6, /device:TPU:0, one launch (start us, length us, event | category | flops | bytes accessed | tf_op | source)
XLA Modules:
  0.0 283.4 jit_solution(17521368470495149967)
XLA Ops:
  1.3 278.6 %layer_step.1 = (bf16[128,2048]{1,0:T(8,128)(2,1)}, f32[128,2048]{1,0:T(8,128)}, f32[128,256]{1,0:T(8,128)}, f32[128,256]{1,0:T(8,128)}, f32[128,256]{1,0:T(8,12...) custom-call(s32[1]{0:T(128)S(6)} %copy.28.lengths, ...), custom_call_target="tpu_custom_call" | custom-call | tf_op jit(solution)/shard_map/layer_step/pallas_call | solution.py:1220
  279.9 3.3 %hand_over_step.1 = (bf16[128,2048]{1,0:T(8,128)(2,1)}, f32[128,2048]{1,0:T(8,128)}, f32[128,256]{1,0:T(8,128)}, f32[128,256]{1,0:T(8,128)}, f32[128,256]{1,0:T(...) custom-call(bf16[128,2048]{1,0:T(8,128)(2,1)} %get-tuple-element.39., ...), custom_call_target="tpu_custom_call" | custom-call | tf_op jit(solution)/shard_map/hand_over_step/pallas_call | solution.py:1249

commit v7 on v6

--- a/solution.py
+++ b/solution.py
@@ -71,7 +71,7 @@
 
 
 def add_into(out, *terms):
-    step = min(out.shape[0], 16 if out.shape[1] > 1024 else 64 if out.shape[1] > 128 else 128)
+    step = min(out.shape[0], 32 if out.shape[1] > 1024 else 64 if out.shape[1] > 128 else 128)
 
     @pl.loop(0, out.shape[0] // step)
     def _(i):
@@ -876,7 +876,19 @@
 
         scatter = ScatterTensor(part, bufs, *scatter_sems)
         scatter.run(down)
-        for n in range(4):
+        scatter.step(0)
+
+        @pl.loop(0, 2)
+        def _(h):
+            near = pl.ds(pl.multiple_of(h * 1024, 1024), 512)
+            far = pl.ds(pl.multiple_of(h * 1024 + 512, 512), 512)
+            wd[0:512, near] = wd[0:512, near].T
+            wd[512:1024, far] = wd[512:1024, far].T
+            corner = wd[0:512, far].T
+            wd[0:512, far] = wd[512:1024, near].T
+            wd[512:1024, near] = corner
+
+        for n in range(1, 4):
             scatter.step(n)
         scatter.finish(total)
         mlp_part[...] = jnp.zeros_like(mlp_part)
@@ -906,9 +918,11 @@
         def d_inner(slot):
             s = pl.ds(pl.multiple_of(slot * 128, 128), 128)
 
-            @tiles(1024, 512)
-            def _(n):
-                d = nt(dd[s, :], wd[n, :])
+            @pl.loop(0, 2)
+            def _(i):
+                n = pl.ds(pl.multiple_of(i * 512, 512), 512)
+                beyond = pl.ds(pl.multiple_of(1024 + i * 512, 512), 512)
+                d = nn(dd[s, 0:1024], wd[:, n]) + nn(dd[s, 1024:2048], wd[:, beyond])
                 dg[s, n] = (d * gate_factor[s, n].astype(F32)).astype(BF16)
                 du[s, n] = (d * silu[s, n].astype(F32)).astype(BF16)
 
@@ -1111,19 +1125,16 @@
         gate_item.along_y()
         spread(dv, exchange.sum() * (1.0 / 2048))
 
-        @tiles(1024, 256)
-        def _(r):
-            for source, rawer, s, target in ((dq, q_raw, 0, dqr), (dk, k_raw, 128, dkr)):
-                scale = stats[r, 128 + s // 2 : 129 + s // 2]
-                factor = scale * scale * scale * dv[r, s : s + 128]
-                for h in (0, 128):
-                    target[r, h : h + 128] = (
-                        scale * source[r, h : h + 128]
-                        - rawer[r, h : h + 128].astype(F32) * factor
-                    ).astype(BF16)
-
         def d_tokens(first_row):
             s = pl.ds(pl.multiple_of(first_row, 256), 256)
+            for source, rawer, k, target in ((dq, q_raw, 0, dqr), (dk, k_raw, 128, dkr)):
+                scale = stats[s, 128 + k // 2 : 129 + k // 2]
+                factor = scale * scale * scale * dv[s, k : k + 128]
+                for h in (0, 128):
+                    target[s, h : h + 128] = (
+                        scale * source[s, h : h + 128]
+                        - rawer[s, h : h + 128].astype(F32) * factor
+                    ).astype(BF16)
 
             @pl.loop(0, 2)
             def _(i):

time: 284 us -> 282 us (level)
  no operation moved by 1% of the time
where the time goes in v7:
time: 282 us
  Pallas kernels  280 us (99%)
    pallas_call x1, Pallas kernels, whole_layer(): pl.pallas_call(layer_step, out_shape=[S((128, 2048), BF16), S((128, 2048)...  277 us

profile of v7, /device:TPU:0, one launch (start us, length us, event | category | flops | bytes accessed | tf_op | source)
XLA Modules:
  0.0 281.8 jit_solution(2190688170206439885)
XLA Ops:
  1.3 277.1 %layer_step.1 = (bf16[128,2048]{1,0:T(8,128)(2,1)}, f32[128,2048]{1,0:T(8,128)}, f32[128,256]{1,0:T(8,128)}, f32[128,256]{1,0:T(8,128)}, f32[128,256]{1,0:T(8,12...) custom-call(s32[1]{0:T(128)S(6)} %copy.28.lengths, ...), custom_call_target="tpu_custom_call" | custom-call | tf_op jit(solution)/shard_map/layer_step/pallas_call | solution.py:1231
  278.4 3.3 %hand_over_step.1 = (bf16[128,2048]{1,0:T(8,128)(2,1)}, f32[128,2048]{1,0:T(8,128)}, f32[128,256]{1,0:T(8,128)}, f32[128,256]{1,0:T(8,128)}, f32[128,256]{1,0:T(...) custom-call(bf16[128,2048]{1,0:T(8,128)(2,1)} %get-tuple-element.39., ...), custom_call_target="tpu_custom_call" | custom-call | tf_op jit(solution)/shard_map/hand_over_step/pallas_call | solution.py:1260

commit v8 on v7

--- a/solution.py
+++ b/solution.py
@@ -98,8 +98,9 @@
             remote(src[1], own[1], sems, base + 2, up),
             remote(src[0], own[0], sems, base + 3, down),
             remote(behind[0], behind[0], sems, base + 4, up),
-            remote(ahead[1], ahead[1], sems, base + 5, down),
+            remote(ahead[1], ahead[1], sems, base + 4, down),
         ]
+        self.furthest, self.far_sem = block(2), sems[1].at[base + 4]
 
     def start(self):
         for copy in self.copies[:4]:
@@ -117,8 +118,7 @@
         self.copies[3].wait_recv()
 
     def far(self):
-        for copy in self.copies[4:]:
-            copy.wait_recv()
+        all_of(self.furthest, self.far_sem)
 
 
 class RingReduce:
@@ -404,14 +404,14 @@
         self.sent, self.ssem = some_of(out, kind, 15), ssem
         self.local = pltpu.make_async_copy(shard, block(0, 0), lsem)
         self.ring = RingGather(lambda i: block(0, i), "dx", sems, 0, shard)
-        self.far_ring = RingGather(lambda i: block(1, i), "dx", sems, 6)
-        self.own_y = remote(shard, block(0, 0), sems, 12, dict(dyh=1))
+        self.far_ring = RingGather(lambda i: block(1, i), "dx", sems, 5)
+        self.own_y = remote(shard, block(0, 0), sems, 10, dict(dyh=1))
         core = dict(dc=1)
-        self.core = [remote(shard, block(0, 0), sems, 13, core)]
+        self.core = [remote(shard, block(0, 0), sems, 11, core)]
         for n in range(1, 8):
             ref = block(n // 4, n % 4)
-            self.core.append(remote(ref, ref, sems, 13, core))
-        self.shared, self.shared_sem = some_of(out, kind, 8), rsem.at[13]
+            self.core.append(remote(ref, ref, sems, 11, core))
+        self.shared, self.shared_sem = some_of(out, kind, 8), rsem.at[11]
 
     def start(self):
         self.ring.start()
@@ -945,7 +945,7 @@
         def down_grad(i):
             m = pl.ds(i * 512, 512)
 
-            @tiles(2048, 512)
+            @tiles(2048, 1024)
             def _(n):
                 wd[m, n] = tn(inner[:, m], dd[:, n]).astype(BF16)
 
@@ -953,10 +953,7 @@
             @pl.loop(first, first + 2)
             def _(i):
                 m = pl.ds(pl.multiple_of(i * 512, 512), 512)
-
-                @tiles(1024, 512)
-                def _(n):
-                    wg[m, n] = tn(x[:, m], dg[:, n]).astype(BF16)
+                wg[m, :] = tn(x[:, m], dg[...]).astype(BF16)
 
         down_grad(0)
         down_grad(1)
@@ -1009,9 +1006,7 @@
 
         @tiles(2048, 512)
         def _(m):
-            @tiles(1024, 512)
-            def _(n):
-                wu[m, n] = tn(x[:, m], du[:, n]).astype(BF16)
+            wu[m, :] = tn(x[:, m], du[...]).astype(BF16)
 
         reload.start()
         load_raw.start()
@@ -1226,7 +1221,7 @@
     for b in blocks:
         scratch += ScatterDp.scratch(b)
     scratch += [DMA, DMA((14,)), DMA, DMA((21,)), DMA, DMA((7,)), DMA((6,)), DMA((12,))]
-    scratch += [DMA((7,)), DMA((7, 14))]
+    scratch += [DMA((7,)), DMA((7, 12))]
     scratch += [DMA((12,)), DMA((6,)), pltpu.SemaphoreType.REGULAR((3,))]
     return pl.pallas_call(
         layer_step,

time: 282 us -> 282 us (level)
  no operation moved by 1% of the time
where the time goes in v8:
time: 282 us
  Pallas kernels  280 us (99%)
    pallas_call x1, Pallas kernels, whole_layer(): pl.pallas_call(layer_step, out_shape=[S((128, 2048), BF16), S((128, 2048)...  277 us

profile of v8, /device:TPU:0, one launch (start us, length us, event | category | flops | bytes accessed | tf_op | source)
XLA Modules:
  0.0 281.7 jit_solution(7845637122128083634)
XLA Ops:
  1.3 277.0 %layer_step.1 = (bf16[128,2048]{1,0:T(8,128)(2,1)}, f32[128,2048]{1,0:T(8,128)}, f32[128,256]{1,0:T(8,128)}, f32[128,256]{1,0:T(8,128)}, f32[128,256]{1,0:T(8,12...) custom-call(s32[1]{0:T(128)S(6)} %copy.28.lengths, ...), custom_call_target="tpu_custom_call" | custom-call | tf_op jit(solution)/shard_map/layer_step/pallas_call | solution.py:1226
  278.3 3.3 %hand_over_step.1 = (bf16[128,2048]{1,0:T(8,128)(2,1)}, f32[128,2048]{1,0:T(8,128)}, f32[128,256]{1,0:T(8,128)}, f32[128,256]{1,0:T(8,128)}, f32[128,256]{1,0:T(...) custom-call(bf16[128,2048]{1,0:T(8,128)(2,1)} %get-tuple-element.39., ...), custom_call_target="tpu_custom_call" | custom-call | tf_op jit(solution)/shard_map/hand_over_step/pallas_call | solution.py:1255
